TPU v7x, 32 devices: a whole 2x2x4 slice. The times are simulated.
32 devices in a mesh: fsdp: 8 (over y, x, core), ctx: 4 (over z).
Axes of the slice: x: 2, y: 2, z: 4, core: 2. Of those that a mesh axis runs over, the one named last changes fastest.
Arguments:
- tokens: bfloat16 [16384, 1536], P(('fsdp', 'ctx')), may hold values from -6 to 6
- stretch_pairs: int32 [8, 4], P('fsdp'), may hold values from 0 to 3, each once within a row
- cotangent: bfloat16 [16384, 1536], P(('fsdp', 'ctx')), may hold values from -6 to 6
- w_qkv: bfloat16 [2048, 1536], P(('fsdp', 'ctx')), may hold values from -0.15625 to 0.15625
- b_qkv: bfloat16 [2048], P(('fsdp', 'ctx')), may hold values from -3 to 3
- w_out: bfloat16 [1536, 1536], P(('fsdp', 'ctx')), may hold values from -0.625 to 0.625
- norm_attn: bfloat16 [1536], P(('fsdp', 'ctx')), may hold values from 0.099609375 to 1.8984375
- norm_mlp: bfloat16 [1536], P(('fsdp', 'ctx')), may hold values from 0.099609375 to 1.8984375
- w_gate: bfloat16 [8960, 1536], P(('fsdp', 'ctx')), may hold values from -0.15625 to 0.15625
- w_up: bfloat16 [8960, 1536], P(('fsdp', 'ctx')), may hold values from -0.15625 to 0.15625
- w_down: bfloat16 [8960, 1536], P(('fsdp', 'ctx')), may hold values from -0.125 to 0.125
Outputs:
- layer_out: bfloat16 [16384, 1536], P(('fsdp', 'ctx'))
- grad_tokens: float32 [16384, 1536], P(('fsdp', 'ctx'))
- grad_qkv: float32 [2048, 1536], P(('fsdp', 'ctx'))
- grad_query_bias: float32 [1536], P(('fsdp', 'ctx'))
- grad_kv_bias: float32 [512], P(('fsdp', 'ctx'))
- grad_out: float32 [1536, 1536], P(('fsdp', 'ctx'))
- grad_norm_attn: float32 [1536], P(('fsdp', 'ctx'))
- grad_norm_mlp: float32 [1536], P(('fsdp', 'ctx'))
- grad_gate: float32 [8960, 1536], P(('fsdp', 'ctx'))
- grad_up: float32 [8960, 1536], P(('fsdp', 'ctx'))
- grad_down: float32 [8960, 1536], P(('fsdp', 'ctx'))
Inputs may be any that keep to these rules, and one draw needn't show every extreme that they name: `stretch_pairs`: each row is a permutation: the 4 ranks of a sequence hold different block pairs, pair p being blocks p and 7 - p.
All inputs are finite; a program needn't handle non-finite values.
Results may differ from a plain program's by a relative error of at most 0.015.
Values may be sent and summed in bfloat16 or wider, within the bound.
No kernel may reach another device: no remote copies, remote signals or barrier semaphores. Data moves between devices by JAX's collectives and lax.ppermute only.
A program may use at most 320 MiB of HBM per device.

v0:
```python
import jax
import jax.numpy as jnp
from jax import lax
from jax.sharding import PartitionSpec as P

HEADS = 12
KV_HEADS = 2
HEAD = 128


rope_base = 1000000.0
norm_eps = 1e-06


def rope_tables(positions):
    exponent = jnp.arange(0, HEAD, 2).astype(jnp.float32) / HEAD
    inverse = rope_base ** (-exponent)
    angles = positions.astype(jnp.float32)[:, None] * inverse[None, :]
    angles = jnp.concatenate([angles, angles], axis=1)
    return (jnp.cos(angles), jnp.sin(angles))


def rotate(values, cosine, sine_table):
    half_dim = HEAD // 2
    turned = jnp.concatenate([-values[..., half_dim:], values[..., :half_dim]], axis=-1)
    return values * cosine[:, None, :] + turned * sine_table[:, None, :]


def unrotate(grads_in, cosine, sine_table):
    half_dim = HEAD // 2
    scaled = grads_in * sine_table[:, None, :]
    turned = jnp.concatenate([scaled[..., half_dim:], -scaled[..., :half_dim]], axis=-1)
    return grads_in * cosine[:, None, :] + turned


def rms_scale(values):
    return lax.rsqrt(jnp.mean(values * values, axis=-1, keepdims=True) + norm_eps)


def norm_back(d_normed, values, inv_scale, gain):
    scaled = d_normed * gain
    grad_gain = jnp.sum(d_normed * values * inv_scale, axis=0)
    inner = jnp.mean(scaled * values, axis=-1, keepdims=True)
    return (inv_scale * scaled - values * inv_scale * inv_scale * inv_scale * inner, grad_gain)


def project_rows(left, weight_rows):
    return jnp.einsum("rd,fd->rf", left, weight_rows, preferred_element_type=jnp.float32)


def score_block(query_block, key_block, query_pos, key_pos):
    scores = jnp.einsum(
        "lgjd,mgd->gjlm", query_block, key_block, preferred_element_type=jnp.float32
    )
    scores = scores * HEAD ** (-0.5)
    allowed = key_pos[None, :] <= query_pos[:, None]
    return (jnp.where(allowed[None, None], scores, -1e30), allowed)


def attend_forward(item_args):
    query_block, key_block, value_block, query_pos, key_pos = item_args
    scores, allowed = score_block(query_block, key_block, query_pos, key_pos)
    top_score = jnp.max(scores, axis=-1, keepdims=True)
    expon = jnp.exp(scores - top_score)
    totals = jnp.sum(expon, axis=-1, keepdims=True)
    probs_low = (expon / totals).astype(jnp.bfloat16)
    log_total = (top_score + jnp.log(totals))[..., 0]
    attended = jnp.einsum(
        "gjlm,mgd->lgjd", probs_low, value_block, preferred_element_type=jnp.float32
    )
    return (attended.reshape(attended.shape[0], HEADS * HEAD).astype(jnp.bfloat16), log_total)


def attend_backward(item_args):
    query_block, key_block, value_block, d_block, log_total, query_pos, key_pos = item_args
    scores, allowed = score_block(query_block, key_block, query_pos, key_pos)
    probs = jnp.where(allowed[None, None], jnp.exp(scores - log_total[..., None]), 0.0)
    probs_low = probs.astype(jnp.bfloat16)
    d_probs = jnp.einsum("lgjd,mgd->gjlm", d_block, value_block, preferred_element_type=jnp.float32)
    row_dot = jnp.sum(probs * d_probs, axis=-1, keepdims=True)
    d_scores = (probs * (d_probs - row_dot)).astype(jnp.bfloat16)
    scale = HEAD ** (-0.5)
    d_query = (
        jnp.einsum("gjlm,mgd->lgjd", d_scores, key_block, preferred_element_type=jnp.float32)
        * scale
    )
    d_key = (
        jnp.einsum("gjlm,lgjd->mgd", d_scores, query_block, preferred_element_type=jnp.float32)
        * scale
    )
    d_value = jnp.einsum("gjlm,lgjd->mgd", probs_low, d_block, preferred_element_type=jnp.float32)
    rows_here = d_query.shape[0]
    keys_here = d_key.shape[0]
    return (
        d_query.reshape(rows_here, HEADS * HEAD),
        d_key.reshape(keys_here, KV_HEADS * HEAD),
        d_value.reshape(keys_here, KV_HEADS * HEAD),
    )


def unit_backward(gate_pre, up_pre, cot_rows, gate_rows, up_rows, down_rows):
    sigmoid_gate = jax.nn.sigmoid(gate_pre)
    silu_gate = gate_pre * sigmoid_gate
    hidden = (silu_gate * up_pre).astype(jnp.bfloat16)
    d_hidden = project_rows(cot_rows, down_rows)
    d_up = (d_hidden * silu_gate).astype(jnp.bfloat16)
    d_gate = (d_hidden * up_pre * sigmoid_gate * (1.0 + gate_pre * (1.0 - sigmoid_gate))).astype(
        jnp.bfloat16
    )
    d_normed = jnp.dot(d_gate, gate_rows, preferred_element_type=jnp.float32) + jnp.dot(
        d_up, up_rows, preferred_element_type=jnp.float32
    )
    return (hidden, d_gate, d_up, d_normed)


def unit_terms(d_gate, d_up, hidden, normed_rows, cot_rows):
    return jnp.concatenate(
        [
            jnp.einsum("rf,rd->fd", d_gate, normed_rows, preferred_element_type=jnp.float32),
            jnp.einsum("rf,rd->fd", d_up, normed_rows, preferred_element_type=jnp.float32),
            jnp.einsum("rf,rd->fd", hidden, cot_rows, preferred_element_type=jnp.float32),
        ],
        axis=1,
    )


def on_device(
    tokens, stretch_pairs, cotangent, w_qkv, b_qkv, w_out, norm_attn, norm_mlp, w_gate, w_up, w_down
):
    ctx_count = lax.axis_size("ctx")
    ctx_rank = lax.axis_index("ctx")
    seq_count = stretch_pairs.shape[0]
    row_count = tokens.shape[0]
    local_len = row_count // seq_count
    half_len = local_len // 2
    seq_len = local_len * ctx_count
    query_width = HEADS * HEAD
    kv_width = KV_HEADS * HEAD
    group_size = HEADS // KV_HEADS
    width = tokens.shape[1]
    offsets = jnp.arange(local_len)

    def place(pair_col):
        return jnp.where(
            offsets < half_len,
            pair_col * half_len + offsets,
            (2 * ctx_count - 1 - pair_col) * half_len + offsets - half_len,
        )

    key_pos = place(stretch_pairs[:, :, None]).reshape(seq_count, seq_len)
    own_pair = jnp.sum(
        jnp.where(jnp.arange(ctx_count)[None, :] == ctx_rank, stretch_pairs, 0), axis=1
    )
    query_pos = place(own_pair[:, None])
    cosine, sine_table = rope_tables(query_pos.reshape(row_count))
    qkv_all, bias_all, out_all, gain_one, gain_two = (
        lax.all_gather(w_qkv, ("fsdp", "ctx"), axis=0, tiled=True),
        lax.all_gather(b_qkv, ("fsdp", "ctx"), axis=0, tiled=True),
        lax.all_gather(w_out, ("fsdp", "ctx"), axis=0, tiled=True),
        lax.all_gather(norm_attn, ("fsdp", "ctx"), axis=0, tiled=True),
        lax.all_gather(norm_mlp, ("fsdp", "ctx"), axis=0, tiled=True),
    )
    gain_one = gain_one.astype(jnp.float32)
    gain_two = gain_two.astype(jnp.float32)
    inputs = tokens.astype(jnp.float32)
    inv_one = rms_scale(inputs)
    normed_one = (inputs * inv_one * gain_one).astype(jnp.bfloat16)
    projected = project_rows(normed_one, qkv_all) + bias_all.astype(jnp.float32)
    queries = rotate(
        projected[:, :query_width].reshape(row_count, HEADS, HEAD), cosine, sine_table
    ).astype(jnp.bfloat16)
    keys_low = rotate(
        projected[:, query_width : query_width + kv_width].reshape(row_count, KV_HEADS, HEAD),
        cosine,
        sine_table,
    ).astype(jnp.bfloat16)
    values_low = projected[:, query_width + kv_width :].astype(jnp.bfloat16)
    keys_all, values_all = (
        lax.all_gather(keys_low.reshape(seq_count, local_len, kv_width), "ctx", axis=1, tiled=True),
        lax.all_gather(
            values_low.reshape(seq_count, local_len, kv_width), "ctx", axis=1, tiled=True
        ),
    )
    query_groups = queries.reshape(seq_count, local_len, KV_HEADS, group_size, HEAD)
    key_heads = keys_all.reshape(seq_count, seq_len, KV_HEADS, HEAD)
    value_heads = values_all.reshape(seq_count, seq_len, KV_HEADS, HEAD)
    attended, log_totals = lax.map(
        attend_forward, (query_groups, key_heads, value_heads, query_pos, key_pos)
    )
    attended = attended.reshape(row_count, query_width)
    middle = inputs + jnp.dot(attended, out_all, preferred_element_type=jnp.float32)
    inv_two = rms_scale(middle)
    normed_two = (middle * inv_two * gain_two).astype(jnp.bfloat16)
    normed_rows, cot_rows = (
        lax.all_gather(normed_two, "ctx", axis=0, tiled=True),
        lax.all_gather(cotangent, "ctx", axis=0, tiled=True),
    )
    gate_part, up_part, down_part = (
        lax.all_gather(w_gate, "fsdp", axis=0, tiled=True),
        lax.all_gather(w_up, "fsdp", axis=0, tiled=True),
        lax.all_gather(w_down, "fsdp", axis=0, tiled=True),
    )
    gate_pre = project_rows(normed_rows, gate_part)
    up_pre = project_rows(normed_rows, up_part)
    hidden, d_gate, d_up, d_normed_part = unit_backward(
        gate_pre, up_pre, cot_rows, gate_part, up_part, down_part
    )
    branch_part = jnp.dot(hidden, down_part, preferred_element_type=jnp.float32)
    branch_two, d_normed_two = (
        lax.psum_scatter(branch_part, "ctx", scatter_dimension=0, tiled=True),
        lax.psum_scatter(d_normed_part, "ctx", scatter_dimension=0, tiled=True),
    )
    mlp_shares = lax.psum_scatter(
        unit_terms(d_gate, d_up, hidden, normed_rows, cot_rows).astype(jnp.bfloat16),
        "fsdp",
        scatter_dimension=0,
        tiled=True,
    ).astype(jnp.float32)
    layer_out = (middle + branch_two).astype(jnp.bfloat16)
    grad_gate = mlp_shares[:, :width]
    grad_up = mlp_shares[:, width : 2 * width]
    grad_down = mlp_shares[:, 2 * width :]
    d_mid_norm, grad_gain_two = norm_back(d_normed_two, middle, inv_two, gain_two)
    d_middle = cotangent.astype(jnp.float32) + d_mid_norm
    d_branch = d_middle.astype(jnp.bfloat16)
    grad_out_local = jnp.einsum("rq,rd->qd", attended, d_branch, preferred_element_type=jnp.float32)
    d_attended = project_rows(d_branch, out_all).astype(jnp.bfloat16)
    d_groups = d_attended.reshape(seq_count, local_len, KV_HEADS, group_size, HEAD)
    d_queries, d_keys_part, d_values_part = lax.map(
        attend_backward,
        (query_groups, key_heads, value_heads, d_groups, log_totals, query_pos, key_pos),
    )
    d_keys, d_values = (
        lax.psum_scatter(
            d_keys_part.astype(jnp.bfloat16), "ctx", scatter_dimension=1, tiled=True
        ).astype(jnp.float32),
        lax.psum_scatter(
            d_values_part.astype(jnp.bfloat16), "ctx", scatter_dimension=1, tiled=True
        ).astype(jnp.float32),
    )
    d_query_pre = unrotate(d_queries.reshape(row_count, HEADS, HEAD), cosine, sine_table)
    d_key_pre = unrotate(d_keys.reshape(row_count, KV_HEADS, HEAD), cosine, sine_table)
    d_projected = jnp.concatenate(
        [
            d_query_pre.reshape(row_count, query_width),
            d_key_pre.reshape(row_count, kv_width),
            d_values.reshape(row_count, kv_width),
        ],
        axis=1,
    ).astype(jnp.bfloat16)
    bias_local = jnp.sum(d_projected, axis=0, dtype=jnp.float32)
    query_bias_local = bias_local[:query_width]
    kv_bias_local = bias_local[query_width:]
    qkv_local = jnp.einsum("rf,rd->fd", d_projected, normed_one, preferred_element_type=jnp.float32)
    d_normed_one = jnp.dot(d_projected, qkv_all, preferred_element_type=jnp.float32)
    d_in_norm, grad_gain_one = norm_back(d_normed_one, inputs, inv_one, gain_one)
    grad_tokens = d_middle + d_in_norm
    grad_qkv, grad_query_bias, grad_kv_bias, grad_out, grad_norm_attn, grad_norm_mlp = (
        lax.psum_scatter(qkv_local, ("fsdp", "ctx"), scatter_dimension=0, tiled=True),
        lax.psum_scatter(query_bias_local, ("fsdp", "ctx"), scatter_dimension=0, tiled=True),
        lax.psum_scatter(kv_bias_local, ("fsdp", "ctx"), scatter_dimension=0, tiled=True),
        lax.psum_scatter(grad_out_local, ("fsdp", "ctx"), scatter_dimension=0, tiled=True),
        lax.psum_scatter(grad_gain_one, ("fsdp", "ctx"), scatter_dimension=0, tiled=True),
        lax.psum_scatter(grad_gain_two, ("fsdp", "ctx"), scatter_dimension=0, tiled=True),
    )
    return (
        layer_out,
        grad_tokens,
        grad_qkv,
        grad_query_bias,
        grad_kv_bias,
        grad_out,
        grad_norm_attn,
        grad_norm_mlp,
        grad_gate,
        grad_up,
        grad_down,
    )


def solution(mesh):
    return jax.shard_map(
        on_device,
        mesh=mesh,
        in_specs=(
            P(("fsdp", "ctx"), None),
            P("fsdp", None),
            P(("fsdp", "ctx"), None),
            P(("fsdp", "ctx"), None),
            P(("fsdp", "ctx")),
            P(("fsdp", "ctx"), None),
            P(("fsdp", "ctx")),
            P(("fsdp", "ctx")),
            P(("fsdp", "ctx"), None),
            P(("fsdp", "ctx"), None),
            P(("fsdp", "ctx"), None),
        ),
        out_specs=(
            P(("fsdp", "ctx"), None),
            P(("fsdp", "ctx"), None),
            P(("fsdp", "ctx"), None),
            P(("fsdp", "ctx")),
            P(("fsdp", "ctx")),
            P(("fsdp", "ctx"), None),
            P(("fsdp", "ctx")),
            P(("fsdp", "ctx")),
            P(("fsdp", "ctx"), None),
            P(("fsdp", "ctx"), None),
            P(("fsdp", "ctx"), None),
        ),
        check_vma=False,
    )
```

profile of v0, /device:TPU:0, one launch (start us, length us, event | category | flops | bytes accessed | tf_op | source)
XLA Modules:
  0.0 1712.1 jit_solution(18049167855663635974)
XLA Ops:
  13.1 42.3 %all-reduce.9 = (bf16[2048]{0:T(1024)(128)(2,1)S(1)}, bf16[1536]{0:T(1024)(128)(2,1)S(1)}, bf16[1536]{0:T(1024)(128)(2,1)S(1)}) all-reduce(bf16[2048]{0:T(1024)(128)(2,1)S(1)} %dynamic-update-slice.1, bf16[1536]{0:T(1024)(128)(2,1)S(1)} %dynamic-update-slice, ...), channel_id=1, replica_groups=mesh['fsdp'=8,'ctx'=4] {'fsdp','ctx'}, use_global_device_ids=true, to_apply=%add.1 | all-reduce | flops 5120 | bytes 20480
  58.6 24.6 %all-gather.12.cloned.1.call-done = bf16[2048,1536]{1,0:T(8,128)(2,1)} async-done(((bf16[64,1536]{1,0:T(8,128)(2,1)}), bf16[2048,1536]{1,0:T(8,128)(2,1)}) %all-gather.12.cloned.1.call-update) | async-done | bytes 6291472 | tf_op jit(solution)/shard_map/all_gather | solution.py:157
  128.3 20.3 %fusion.9 = (f32[2,6,512]{2,1,0:T(8,128)S(1)}, f32[2,2048,512,6]{2,1,3,0:T(8,128)}) fusion(pred[512,2048]{0,1:T(8,128)(4,1)S(1)} %broadcast_compare_fusion, bf16[2048,2,128,1]{0,2,3,1:T(8,128)(2,1)} %copy.80, bf16[512,2,6,128]{0,3,2,1:T(8,128)(2,1)S(1)} %fusion.23), kind=kOutput, calls=%fused_computation.15 | convolution fusion | flops 3258968064 | bytes 54026240 | tf_op jit(solution)/shard_map/while/body/eval_jaxpr/lgjd,mgd->gjlm/dot_general | solution.py:52
  154.2 21.2 %fusion.3 = f32[2,6,512]{2,1,0:T(8,128)S(1)} fusion(f32[2,6,512]{2,1,0:T(8,128)S(1)} %get-tuple-element.100, f32[2,2048,512,6]{2,1,3,0:T(8,128)} %get-tuple-element.101, pred[512,2048]{0,1:T(8,128)(4,1)S(1)} %broadcast_compare_fusion), kind=kLoop, calls=%fused_computation.9 | loop fusion | flops 50325504 | bytes 51429376 | tf_op jit(solution)/shard_map/while/body/eval_jaxpr/reduce_sum | solution.py:65
  175.5 23.7 %fusion.34 = bf16[2,128,6,512]{3,1,2,0:T(8,128)(2,1)} fusion(f32[2,6,512]{2,1,0:T(8,128)S(1)} %fusion.3, f32[2,6,512]{2,1,0:T(8,128)S(1)} %get-tuple-element.100, f32[2,2048,512,6]{2,1,3,0:T(8,128)} %get-tuple-element.101, pred[512,2048]{0,1:T(8,128)(4,1)S(1)} %broadcast_compare_fusion, bf16[2048,2,128,1]{2,1,0,3:T(2,128)(2,1)} %bitcast.157), kind=kOutput, calls=%fused_computation.66 | convolution fusion | flops 3284926464 | bytes 54050816 | tf_op jit(solution)/shard_map/while/body/eval_jaxpr/gjlm,mgd->lgjd/dot_general | solution.py:68
  228.5 37.9 %all-gather.20.cloned.1.call-done = bf16[2240,1536]{1,0:T(8,128)(2,1)} async-done(((bf16[280,1536]{1,0:T(8,128)(2,1)}), bf16[2240,1536]{1,0:T(8,128)(2,1)}) %all-gather.20.cloned.1.call-update) | async-done | bytes 6881296 | tf_op jit(solution)/shard_map/all_gather | solution.py:200
  266.3 117.4 %all-gather.16.cloned.1.call-done = bf16[2048,1536]{1,0:T(8,128)(2,1)} async-done(((bf16[512,1536]{1,0:T(8,128)(2,1)}), bf16[2048,1536]{1,0:T(8,128)(2,1)}) %all-gather.16.cloned.1.call-update) | async-done | bytes 6291472 | tf_op jit(solution)/shard_map/all_gather | solution.py:195
  383.7 20.6 %fusion.60 = f32[2048,2240]{0,1:T(8,128)} fusion(bf16[2048,1536]{1,0:T(8,128)(2,1)} %all-gather.16.cloned.1.call-done, bf16[2240,1536]{1,0:T(8,128)(2,1)} %all-gather.20.cloned.1.call-done), kind=kOutput, calls=%fused_computation.118 | convolution fusion | flops 14092861440 | bytes 31522816 | tf_op jit(solution)/shard_map/rd,fd->rf/dot_general | solution.py:48
  404.3 27.6 %all-gather.18.cloned.1.call-done = bf16[2240,1536]{1,0:T(8,128)(2,1)} async-done(((bf16[280,1536]{1,0:T(8,128)(2,1)}), bf16[2240,1536]{1,0:T(8,128)(2,1)}) %all-gather.18.cloned.1.call-update) | async-done | bytes 6881296 | tf_op jit(solution)/shard_map/all_gather | solution.py:199
  431.9 20.4 %fusion.59 = f32[2048,2240]{0,1:T(8,128)} fusion(bf16[2048,1536]{1,0:T(8,128)(2,1)} %all-gather.16.cloned.1.call-done, bf16[2240,1536]{1,0:T(8,128)(2,1)} %all-gather.18.cloned.1.call-done), kind=kOutput, calls=%fused_computation.117 | convolution fusion | flops 14092861440 | bytes 31522816 | tf_op jit(solution)/shard_map/rd,fd->rf/dot_general | solution.py:48
  452.3 96.5 %all-gather.24.cloned.1.call-done = bf16[2048,1536]{1,0:T(8,128)(2,1)} async-done(((bf16[512,1536]{1,0:T(8,128)(2,1)}), bf16[2048,1536]{1,0:T(8,128)(2,1)}) %all-gather.24.cloned.1.call-update) | async-done | bytes 6291472 | tf_op jit(solution)/shard_map/all_gather | solution.py:196
  548.9 48.2 %all-gather.22.cloned.1.call-done = bf16[2240,1536]{1,0:T(8,128)(2,1)} async-done(((bf16[280,1536]{1,0:T(8,128)(2,1)}), bf16[2240,1536]{1,0:T(8,128)(2,1)}) %all-gather.22.cloned.1.call-update) | async-done | bytes 6881296 | tf_op jit(solution)/shard_map/all_gather | solution.py:201
  597.0 33.6 %multiply_convert_fusion = (bf16[2048,2240]{0,1:T(8,128)(2,1)}, bf16[2048,2240]{0,1:T(8,128)(2,1)}, bf16[2048,2240]{0,1:T(8,128)(2,1)}) fusion(f32[2048,2240]{0,1:T(8,128)} %fusion.59, f32[2048,2240]{0,1:T(8,128)} %fusion.60, bf16[2048,1536]{1,0:T(8,128)(2,1)} %all-gather.24.cloned.1.call-done, bf16[2240,1536]{1,0:T(8,128)(2,1)} %all-gather.22.cloned.1.call-done), kind=kOutput, calls=%fused_computation.16 | convolution fusion | flops 14161674240 | bytes 77398016 | tf_op jit(solution)/shard_map/rd,fd->rf/dot_general | solution.py:48
  670.6 20.9 %fusion.61 = f32[2048,1536]{1,0:T(8,128)} fusion(bf16[2048,2240]{0,1:T(8,128)(2,1)} %get-tuple-element.81, bf16[2240,1536]{1,0:T(8,128)(2,1)} %all-gather.22.cloned.1.call-done), kind=kOutput, calls=%fused_computation.119 | convolution fusion | flops 14092861440 | bytes 28639232 | tf_op jit(solution)/shard_map/dot_general | solution.py:208
  692.9 20.6 %convolution_convert_fusion = bf16[2240,1536]{1,0:T(8,128)(2,1)} fusion(bf16[2048,2240]{0,1:T(8,128)(2,1)} %get-tuple-element.81, bf16[2048,1536]{1,0:T(8,128)(2,1)} %all-gather.24.cloned.1.call-done), kind=kOutput, calls=%fused_computation.21 | convolution fusion | flops 14096302080 | bytes 22347776 | tf_op jit(solution)/shard_map/rf,rd->fd/dot_general | solution.py:121
  748.7 133.8 %reduce-scatter.12.cloned.1.call-done = f32[512,1536]{1,0:T(8,128)} async-done(((f32[2048,1536]{1,0:T(8,128)}), f32[512,1536]{1,0:T(8,128)}) %reduce-scatter.12.cloned.1.call-update) | async-done | bytes 3145744 | tf_op jit(solution)/shard_map/reduce_scatter | solution.py:211
  885.8 212.0 %reduce-scatter.10.cloned.1.call-done = f32[512,1536]{1,0:T(8,128)} async-done(((f32[2048,1536]{1,0:T(8,128)}), f32[512,1536]{1,0:T(8,128)}) %reduce-scatter.10.cloned.1.call-update) | async-done | bytes 3145744 | tf_op jit(solution)/shard_map/reduce_scatter | solution.py:210
  1113.3 34.7 %fusion = (f32[2,6,512]{2,1,0:T(8,128)S(1)}, f32[2,2048,512,6]{2,1,3,0:T(8,128)}) fusion(f32[2,6,512]{2,1,0:T(8,128)S(1)} %copy-done.28, pred[512,2048]{0,1:T(8,128)(4,1)S(1)} %copy-done.1, f32[2,2048,512,6]{2,1,3,0:T(8,128)} %get-tuple-element.101, bf16[512,2,6,128]{0,3,2,1:T(8,128)(2,1)S(1)} %bitcast.155, bf16[2048,2,128,1]{2,1,0,3:T(2,128)(2,1)} %bitcast.158), kind=kOutput, calls=%fused_computation.2 | convolution fusion | flops 3296716800 | bytes 104382464 | tf_op jit(solution)/shard_map/while/body/eval_jaxpr/lgjd,mgd->gjlm/dot_general | solution.py:79
  1148.0 40.8 %fusion.2 = bf16[2,6,512,2048]{2,3,1,0:T(8,128)(2,1)} fusion(f32[2,2048,512,6]{2,1,3,0:T(8,128)} %get-tuple-element.105, f32[2,6,512]{2,1,0:T(8,128)S(1)} %get-tuple-element.104, f32[2,6,512]{2,1,0:T(8,128)S(1)} %copy-done.28, pred[512,2048]{0,1:T(8,128)(4,1)S(1)} %copy-done.1, f32[2,2048,512,6]{2,1,3,0:T(8,128)} %get-tuple-element.101), kind=kLoop, calls=%fused_computation.4 | loop fusion | flops 88080384 | bytes 126926848 | tf_op jit(solution)/shard_map/while/body/eval_jaxpr/convert_element_type | solution.py:81
  1205.1 21.6 %fusion.29 = bf16[2,128,2048]{2,1,0:T(8,128)(2,1)} fusion(bf16[512,2,6,128]{0,3,2,1:T(8,128)(2,1)} %bitcast.156, f32[2,6,512]{2,1,0:T(8,128)S(1)} %copy-done.28, pred[512,2048]{0,1:T(8,128)(4,1)S(1)} %copy-done.1, f32[2,2048,512,6]{2,1,3,0:T(8,128)} %get-tuple-element.101), kind=kOutput, calls=%fused_computation.60 | convolution fusion | flops 3284664320 | bytes 54026240 | tf_op jit(solution)/shard_map/while/body/eval_jaxpr/gjlm,lgjd->mgd/dot_general | solution.py:91
  1300.5 41.8 %all-reduce.8 = (f32[1536]{0:T(1024)S(1)}, f32[512]{0:T(512)S(1)}, f32[1536]{0:T(1024)S(1)}, f32[1536]{0:T(1024)S(1)}) all-reduce(f32[1536]{0:T(1024)S(1)} %bitcast.163, f32[512]{0:T(512)S(1)} %slice.77, f32[1536]{0:T(1024)S(1)} %get-tuple-element.59, f32[1536]{0:T(1024)S(1)} %copy-done.31), channel_id=9, replica_groups=mesh['fsdp'=8,'ctx'=4] {'fsdp','ctx'}, use_global_device_ids=true, to_apply=%region_14.15.clone | all-reduce | flops 5120 | bytes 40960
  1350.1 51.4 %reduce-scatter.22.cloned.1.call-done = bf16[280,4608]{1,0:T(8,128)(2,1)} async-done(((bf16[2240,4608]{1,0:T(8,128)(2,1)}), bf16[280,4608]{1,0:T(8,128)(2,1)}) %reduce-scatter.22.cloned.1.call-update) | async-done | bytes 2580496
  1405.7 138.7 %reduce-scatter.20.cloned.1.call-done = f32[48,1536]{1,0:T(8,128)} async-done(((f32[1536,1536]{1,0:T(8,128)}), f32[48,1536]{1,0:T(8,128)}) %reduce-scatter.20.cloned.1.call-update) | async-done | bytes 294928 | tf_op jit(solution)/shard_map/reduce_scatter | solution.py:262
  1544.4 160.9 %reduce-scatter.18.cloned.1.call-done = f32[64,1536]{1,0:T(8,128)} async-done(((f32[2048,1536]{1,0:T(8,128)}), f32[64,1536]{1,0:T(8,128)}) %reduce-scatter.18.cloned.1.call-update) | async-done | bytes 393232 | tf_op jit(solution)/shard_map/reduce_scatter | solution.py:259
  (210 shorter events, 284.3 us)
Async XLA Ops:
  7.2 76.1 %all-gather.12.cloned.1.call-start = ((), (), s32[]{:S(2)}) async-start(), calls=%async_computation.7 | async-start | bytes 6488064 | tf_op jit(solution)/shard_map/all_gather | solution.py:157
  7.9 114.5 %all-gather.28.cloned.1.call-start = ((), (), s32[]{:S(2)}) async-start(), calls=%async_computation.21 | async-start | bytes 1310720 | tf_op jit(solution)/shard_map/all_gather | solution.py:179
  56.5 54.0 %copy-start.13 = (f32[512,128]{0,1:T(8,128)}, f32[512,128]{0,1:T(8,128)S(1)}, u32[]{:S(2)}) copy-start(f32[512,128]{0,1:T(8,128)S(1)} %get-tuple-element.95) | copy-start | bytes 786436
  56.5 54.0 %copy-start.15 = (f32[512,128]{0,1:T(8,128)}, f32[512,128]{0,1:T(8,128)S(1)}, u32[]{:S(2)}) copy-start(f32[512,128]{0,1:T(8,128)S(1)} %get-tuple-element.96) | copy-start | bytes 786436
  95.8 56.2 %all-gather.26.cloned.1.call-start = ((), (), s32[]{:S(2)}) async-start(), calls=%async_computation.20 | async-start | bytes 1310720 | tf_op jit(solution)/shard_map/all_gather | solution.py:180
  97.7 120.1 %all-gather.14.cloned.1.call-start = ((), (), s32[]{:S(2)}) async-start(), calls=%async_computation.8 | async-start | bytes 4866048 | tf_op jit(solution)/shard_map/all_gather | solution.py:159
  98.2 168.1 %all-gather.20.cloned.1.call-start = ((), (), s32[]{:S(2)}) async-start(), calls=%async_computation.11 | async-start | bytes 7741440 | tf_op jit(solution)/shard_map/all_gather | solution.py:200
  98.8 284.9 %all-gather.16.cloned.1.call-start = ((), (), s32[]{:S(2)}) async-start(), calls=%async_computation.9 | async-start | bytes 7864320 | tf_op jit(solution)/shard_map/all_gather | solution.py:195
  99.3 123.8 %copy-start.24 = (f32[1536]{0:T(1024)}, f32[1536]{0:T(1024)S(1)}, u32[]{:S(2)}) copy-start(f32[1536]{0:T(1024)S(1)} %convert_element_type.146) | copy-start | bytes 18436
  100.2 75.2 %copy-start = (pred[512,2048]{0,1:T(8,128)(4,1)}, pred[512,2048]{0,1:T(8,128)(4,1)S(1)}, u32[]{:S(2)}) copy-start(pred[512,2048]{0,1:T(8,128)(4,1)S(1)} %broadcast_compare_fusion) | copy-start | bytes 3145732
  175.4 42.3 %copy-start.9 = (bf16[512,1536]{1,0:T(8,128)(2,1)S(1)}, bf16[512,1536]{1,0:T(8,128)(2,1)}, u32[]{:S(2)}) copy-start(bf16[512,1536]{1,0:T(8,128)(2,1)} %param.11) | copy-start | bytes 4718596
  226.2 205.7 %all-gather.18.cloned.1.call-start = ((), (), s32[]{:S(2)}) async-start(), calls=%async_computation.10 | async-start | bytes 7741440 | tf_op jit(solution)/shard_map/all_gather | solution.py:199
  226.9 321.9 %all-gather.24.cloned.1.call-start = ((), (), s32[]{:S(2)}) async-start(), calls=%async_computation.14 | async-start | bytes 7864320 | tf_op jit(solution)/shard_map/all_gather | solution.py:196
  227.7 369.4 %all-gather.22.cloned.1.call-start = ((), (), s32[]{:S(2)}) async-start(), calls=%async_computation.12 | async-start | bytes 7741440 | tf_op jit(solution)/shard_map/all_gather | solution.py:201
  228.4 654.1 %reduce-scatter.12.cloned.1.call-start = ((), (), s32[]{:S(2)}) async-start(), calls=%async_computation.15 | async-start | bytes 15728640 | tf_op jit(solution)/shard_map/reduce_scatter | solution.py:211
  670.5 427.3 %reduce-scatter.10.cloned.1.call-start = ((), (), s32[]{:S(2)}) async-start(), calls=%async_computation.13 | async-start | bytes 15728640 | tf_op jit(solution)/shard_map/reduce_scatter | solution.py:210
  691.5 575.2 %reduce-scatter.14.cloned.1.call-start = ((), (), s32[]{:S(2)}) async-start(), calls=%async_computation.16 | async-start | bytes 1310720 | tf_op jit(solution)/shard_map/reduce_scatter | solution.py:234
  731.7 150.8 %copy-start.6 = (f32[512,1536]{1,0:T(8,128)S(1)}, f32[512,1536]{1,0:T(8,128)}, u32[]{:S(2)}) copy-start(f32[512,1536]{1,0:T(8,128)} %copy-done.5) | copy-start | bytes 9437188
  731.7 150.8 %copy-start.25 = (f32[1536]{0:T(1024)S(1)}, f32[1536]{0:T(1024)}, u32[]{:S(2)}) copy-start(f32[1536]{0:T(1024)} %copy-done.24) | copy-start | bytes 18436
  731.7 150.8 %copy-start.30 = (f32[512]{0:T(512)S(1)}, f32[512]{0:T(512)}, u32[]{:S(2)}) copy-start(f32[512]{0:T(512)} %copy-done.29) | copy-start | bytes 6148
  1205.1 67.5 %reduce-scatter.16.cloned.1.call-start = ((), (), s32[]{:S(2)}) async-start(), calls=%async_computation.17 | async-start | bytes 1310720 | tf_op jit(solution)/shard_map/reduce_scatter | solution.py:237
  1226.7 174.7 %reduce-scatter.22.cloned.1.call-start = ((), (), s32[]{:S(2)}) async-start(), calls=%async_computation.22 | async-start | bytes 23224320
  1243.5 300.9 %reduce-scatter.20.cloned.1.call-start = ((), (), s32[]{:S(2)}) async-start(), calls=%async_computation.19 | async-start | bytes 9732096 | tf_op jit(solution)/shard_map/reduce_scatter | solution.py:262
  1251.9 453.4 %reduce-scatter.18.cloned.1.call-start = ((), (), s32[]{:S(2)}) async-start(), calls=%async_computation.18 | async-start | bytes 12976128 | tf_op jit(solution)/shard_map/reduce_scatter | solution.py:259
  (36 other events, 554.4 us)
Sparse Core Ops, SparseCore 0:
  10.9 72.3 all-gather.11
  95.9 26.4 all-gather.27
  124.5 27.4 all-gather.25
  154.7 63.0 all-gather.13
  219.5 46.8 all-gather.19
  268.3 115.3 all-gather.15
  385.6 46.2 all-gather.17
  433.5 115.3 all-gather.23
  550.8 46.2 all-gather.21
  670.6 211.8 reduce-scatter.11
  884.9 212.8 reduce-scatter.9
  1205.2 28.1 reduce-scatter.13
  1236.4 25.7 reduce-scatter.15
  1265.7 135.7 reduce-scatter.21
  1408.8 135.5 reduce-scatter.19
  1550.8 154.4 reduce-scatter.17
where the time goes:
time: 1720 us; the launch traced here: 1710 us
  waiting for transfers between devices  1090 us (63%)
  matrix products  365 us (21%)
  other arithmetic  115 us (7%)
  blocking collectives  84.1 us (5%)
  local copies, waits for them, and re-layouts  45.2 us (3%)
    reduce_scatter x1, waiting for transfers between devices, on_device(): lax.psum_scatter(branch_part, 'ctx', scatter_dimension=0, tiled=True)  212 us
    reduce_scatter x1, waiting for transfers between devices, on_device(): lax.psum_scatter(qkv_local, ('fsdp', 'ctx'), scatter_dimension=0, tiled=T...  161 us
    reduce_scatter x1, waiting for transfers between devices, on_device(): lax.psum_scatter(grad_out_local, ('fsdp', 'ctx'), scatter_dimension=0, ti...  139 us
    reduce_scatter x1, waiting for transfers between devices, on_device(): lax.psum_scatter(d_normed_part, 'ctx', scatter_dimension=0, tiled=True)  134 us
    all_gather x1, waiting for transfers between devices, on_device(): lax.all_gather(normed_two, 'ctx', axis=0, tiled=True)  117 us
    all_gather x1, waiting for transfers between devices, on_device(): lax.all_gather(cotangent, 'ctx', axis=0, tiled=True)  96.5 us
    dot_general x5, matrix products, project_rows(): jnp.einsum('rd,fd->rf', left, weight_rows, preferred_element_type=jnp.flo...  87.1 us
    unnamed x2, blocking collectives  84.1 us
  transfers between devices with their start and end apart: 16, of which 14 were waited for; matrix products, arithmetic and copies ran while one was open for 19% of the time, Pallas kernels for 0%

commit v1 on v0

v1 whole, which is shorter than its diff:
```python
import functools

import jax
import jax.numpy as jnp
from jax import lax
from jax.experimental import pallas as pl
from jax.experimental.pallas import tpu as pltpu
from jax.sharding import Mesh
from jax.sharding import PartitionSpec as P

HEADS = 12
KV_HEADS = 2
HEAD = 128
GROUP = HEADS // KV_HEADS
MIB = 2**20

rope_base = 1000000.0
norm_eps = 1e-06

LOG2E = 1.4426950408889634
SCALE = HEAD ** -0.5

NT = (((1,), (1,)), ((), ()))
NN = (((1,), (0,)), ((), ()))
TN = (((0,), (0,)), ((), ()))


def dot(left, right, dims):
    return lax.dot_general(left, right, dims, preferred_element_type=jnp.float32)


def forward_kernel(table, q_ref, k_ref, v_ref, o_ref, lse_ref, top, total, acc):
    half = pl.program_id(2)
    block = q_ref.shape[1]
    last = table[0, half]
    spot = table[0, 2 + last]
    heads = range(GROUP)

    def part(slot, masked, first):
        rows = pl.ds(pl.multiple_of(slot * block, block), block)
        keys, values = k_ref[0, rows, :], v_ref[0, rows, :]
        if not first:
            old_top = [top[j] for j in heads]
            old_total = [total[j] for j in heads]
        scores = [dot(keys, q_ref[0, :, pl.ds(j * HEAD, HEAD)], NT) for j in heads]
        if masked:
            key_at = lax.broadcasted_iota(jnp.int32, scores[0].shape, 0)
            query_at = lax.broadcasted_iota(jnp.int32, scores[0].shape, 1)
            scores = [jnp.where(key_at <= query_at, s, -1e30) for s in scores]
        tops = [jnp.max(s, axis=0, keepdims=True) * (SCALE * LOG2E) for s in scores]
        if not first:
            tops = [jnp.maximum(t, o) for t, o in zip(tops, old_top)]
        expon = [jnp.exp2(s * (SCALE * LOG2E) - t) for s, t in zip(scores, tops)]
        sums = [jnp.sum(e, axis=0, keepdims=True) for e in expon]
        added = [dot(values, e.astype(jnp.bfloat16), TN) for e in expon]
        for j in heads:
            if first:
                total[j] = sums[j]
                acc[j] = added[j]
            else:
                fade = jnp.exp2(old_top[j] - tops[j])
                total[j] = old_total[j] * fade + sums[j]
                acc[j] = acc[j] * fade + added[j]
            top[j] = tops[j]

    part(spot, True, True)

    def step(b, carry):
        part(table[0, 2 + b], False, False)
        return carry

    lax.fori_loop(0, last, step, 0)
    for j in heads:
        o_ref[0, :, pl.ds(j * HEAD, HEAD)] = (acc[j] / total[j]).T.astype(jnp.bfloat16)
        lse_ref[0, 0, 0, j] = (top[j] + jnp.log2(total[j]))[0]


def attend_forward(table, queries, keys, values):
    seqs, rows, width = queries.shape
    block = rows // 2
    wide = GROUP * HEAD
    seq_len = keys.shape[1]
    grid_spec = pltpu.PrefetchScalarGridSpec(
        num_scalar_prefetch=0,
        grid=(seqs, KV_HEADS, 2),
        in_specs=[
            pl.BlockSpec((1, table.shape[1]), lambda s, g, h: (s, 0), memory_space=pltpu.SMEM),
            pl.BlockSpec((1, block, wide), lambda s, g, h: (s, h, g)),
            pl.BlockSpec((1, seq_len, HEAD), lambda s, g, h: (s, 0, g)),
            pl.BlockSpec((1, seq_len, HEAD), lambda s, g, h: (s, 0, g)),
        ],
        out_specs=[
            pl.BlockSpec((1, block, wide), lambda s, g, h: (s, h, g)),
            pl.BlockSpec((1, 1, 1, GROUP, block), lambda s, g, h: (s, g, h, 0, 0)),
        ],
        scratch_shapes=[
            pltpu.VMEM((GROUP, 1, block), jnp.float32),
            pltpu.VMEM((GROUP, 1, block), jnp.float32),
            pltpu.VMEM((GROUP, HEAD, block), jnp.float32),
        ],
    )
    return pl.pallas_call(
        forward_kernel,
        grid_spec=grid_spec,
        out_shape=[
            jax.ShapeDtypeStruct(queries.shape, jnp.bfloat16),
            jax.ShapeDtypeStruct((seqs, KV_HEADS, 2, GROUP, block), jnp.float32),
        ],
        compiler_params=pltpu.CompilerParams(vmem_limit_bytes=40 * 2**20),
        cost_estimate=pl.CostEstimate(flops=2*2*HEADS*HEAD*rows*seq_len*seqs*9//16, bytes_accessed=6*2**20, transcendentals=HEADS*rows*seq_len*seqs*9//16),
        name="attend_forward",
    )(table, queries, keys, values)


def backward_kernel(table, q_ref, k_ref, v_ref, g_ref, o_ref, lse_ref, cos_ref, sin_ref, dq_ref, dk_ref, dv_ref, dk_acc, dv_acc, dq_acc, delta):
    half = pl.program_id(2)
    block = q_ref.shape[1]
    last = table[0, half]
    heads = range(GROUP)

    for j in heads:
        lanes = pl.ds(j * HEAD, HEAD)
        product = o_ref[0, :, lanes].astype(jnp.float32) * g_ref[0, :, lanes].astype(jnp.float32)
        delta[j] = jnp.sum(product.T, axis=0, keepdims=True)

    @pl.when(half == 0)
    def _():
        dk_acc[...] = jnp.zeros_like(dk_acc)
        dv_acc[...] = jnp.zeros_like(dv_acc)

    def part(slot, masked, first):
        rows = pl.ds(pl.multiple_of(slot * block, block), block)
        keys, values = k_ref[0, rows, :], v_ref[0, rows, :]
        lanes = [pl.ds(j * HEAD, HEAD) for j in heads]
        scores = [dot(keys, q_ref[0, :, lanes[j]], NT) for j in heads]
        d_probs = [dot(values, g_ref[0, :, lanes[j]], NT) for j in heads]
        probs = [
            jnp.exp2(scores[j] * (SCALE * LOG2E) - lse_ref[0, 0, 0, pl.ds(j, 1), :]) for j in heads
        ]
        if masked:
            key_at = lax.broadcasted_iota(jnp.int32, scores[0].shape, 0)
            query_at = lax.broadcasted_iota(jnp.int32, scores[0].shape, 1)
            probs = [jnp.where(key_at <= query_at, p, 0.0) for p in probs]
        d_scores = [(probs[j] * (d_probs[j] - delta[j])).astype(jnp.bfloat16) for j in heads]
        low = [p.astype(jnp.bfloat16) for p in probs]
        dv = sum(dot(low[j], g_ref[0, :, lanes[j]], NN) for j in heads)
        dk = sum(dot(d_scores[j], q_ref[0, :, lanes[j]], NN) for j in heads)
        dq = [dot(keys, d_scores[j], TN) for j in heads]
        for j in heads:
            if first:
                dq_acc[j] = dq[j]
            else:
                dq_acc[j] += dq[j]
        dk_acc[rows, :] += dk
        dv_acc[rows, :] += dv

    part(table[0, 2 + last], True, True)

    def step(b, carry):
        part(table[0, 2 + b], False, False)
        return carry

    lax.fori_loop(0, last, step, 0)
    for j in heads:
        grad = dq_acc[j].T * SCALE
        grad = grad * cos_ref[...] - pltpu.roll(grad, HEAD // 2, 1) * sin_ref[...]
        dq_ref[0, :, pl.ds(j * HEAD, HEAD)] = grad.astype(dq_ref.dtype)

    @pl.when(half == 1)
    def _():
        dk_ref[0] = (dk_acc[...] * SCALE).astype(dk_ref.dtype)
        dv_ref[0] = dv_acc[...].astype(dv_ref.dtype)


def attend_backward(table, queries, keys, values, grads, attended, lse, cosine, signed_sine):
    seqs, rows, width = queries.shape
    block = rows // 2
    wide = GROUP * HEAD
    seq_len = keys.shape[1]
    rows_spec = pl.BlockSpec((1, block, wide), lambda s, g, h: (s, h, g))
    keys_spec = pl.BlockSpec((1, seq_len, HEAD), lambda s, g, h: (s, 0, g))
    trig_spec = pl.BlockSpec((block, HEAD), lambda s, g, h: (2 * s + h, 0))
    stat_spec = pl.BlockSpec((1, 1, 1, GROUP, block), lambda s, g, h: (s, g, h, 0, 0))
    return pl.pallas_call(
        backward_kernel,
        grid=(seqs, KV_HEADS, 2),
        in_specs=[
            pl.BlockSpec((1, table.shape[1]), lambda s, g, h: (s, 0), memory_space=pltpu.SMEM),
            rows_spec, keys_spec, keys_spec, rows_spec, rows_spec, stat_spec, trig_spec, trig_spec,
        ],
        out_specs=[rows_spec, keys_spec, keys_spec],
        out_shape=[
            jax.ShapeDtypeStruct(queries.shape, jnp.bfloat16),
            jax.ShapeDtypeStruct(keys.shape, jnp.bfloat16),
            jax.ShapeDtypeStruct(values.shape, jnp.bfloat16),
        ],
        scratch_shapes=[
            pltpu.VMEM((seq_len, HEAD), jnp.float32),
            pltpu.VMEM((seq_len, HEAD), jnp.float32),
            pltpu.VMEM((GROUP, HEAD, block), jnp.float32),
            pltpu.VMEM((GROUP, 1, block), jnp.float32),
        ],
        compiler_params=pltpu.CompilerParams(vmem_limit_bytes=40 * 2**20),
        cost_estimate=pl.CostEstimate(flops=5*2*HEADS*HEAD*rows*seq_len*seqs*9//16, bytes_accessed=12*2**20, transcendentals=HEADS*rows*seq_len*seqs*9//16),
        name="attend_backward",
    )(table, queries, keys, values, grads, attended, lse, cosine, signed_sine)


def grad_kernel(count, *refs):
    out = refs[-1]
    total = None
    for left, right in zip(refs[:count], refs[count:2 * count]):
        term = dot(left[...], right[...], NN)
        total = term if total is None else total + term
    out[...] = total.astype(out.dtype)


def unit_grads(lefts, rights, block=320):
    units = lefts[0].shape[0]
    rows, width = rights[0].shape
    count = len(lefts)
    return pl.pallas_call(
        functools.partial(grad_kernel, count),
        grid=(units // block,),
        in_specs=[pl.BlockSpec((block, l.shape[1]), lambda i: (i, 0)) for l in lefts]
        + [pl.BlockSpec(r.shape, lambda i: (0, 0)) for r in rights],
        out_specs=pl.BlockSpec((block, width), lambda i: (i, 0)),
        out_shape=jax.ShapeDtypeStruct((units, width), jnp.bfloat16),
        compiler_params=pltpu.CompilerParams(vmem_limit_bytes=56 * MIB),
        cost_estimate=pl.CostEstimate(
            flops=2 * count * units * rows * width, bytes_accessed=2 * count * rows * (units + width), transcendentals=0
        ),
        name="unit_grads",
    )(*lefts, *rights)


def project_kernel(rows_ref, gain, weight, bias, cosine, signed_sine, normed, queries, kv):
    step = pl.program_id(0)
    query_steps = pl.num_programs(0) - 2

    @pl.when(step == 0)
    def _():
        rows = rows_ref[...].astype(jnp.float32)
        scale = lax.rsqrt(jnp.mean(rows * rows, axis=-1, keepdims=True) + norm_eps)
        normed[...] = (rows * scale * gain[...]).astype(normed.dtype)

    out = dot(normed[...], weight[...], NT) + bias[...]

    def turned():
        parts = []
        for start in range(0, out.shape[1], HEAD):
            part = out[:, start : start + HEAD]
            parts.append(part * cosine[...] + pltpu.roll(part, HEAD // 2, 1) * signed_sine[...])
        return jnp.concatenate(parts, axis=1).astype(queries.dtype)

    @pl.when(step < query_steps)
    def _():
        queries[...] = turned()

    @pl.when(step == query_steps)
    def _():
        kv[...] = turned()

    @pl.when(step > query_steps)
    def _():
        kv[...] = out.astype(kv.dtype)


def project_heads(tokens, gain, weight, bias, cosine, signed_sine):
    rows, width = tokens.shape
    block = KV_HEADS * HEAD
    steps = weight.shape[0] // block
    whole = pl.BlockSpec((rows, width), lambda i: (0, 0))
    table = pl.BlockSpec((rows, HEAD), lambda i: (0, 0))
    low = jnp.bfloat16
    return pl.pallas_call(
        project_kernel,
        grid=(steps,),
        in_specs=[
            whole,
            pl.BlockSpec((1, width), lambda i: (0, 0)),
            pl.BlockSpec((block, width), lambda i: (i, 0)),
            pl.BlockSpec((1, block), lambda i: (0, i)),
            table,
            table,
        ],
        out_specs=[
            whole,
            pl.BlockSpec((rows, block), lambda i: (0, jnp.minimum(i, steps - 3))),
            pl.BlockSpec((rows, block), lambda i: (0, jnp.maximum(i - steps + 2, 0))),
        ],
        out_shape=[
            jax.ShapeDtypeStruct((rows, width), low),
            jax.ShapeDtypeStruct((rows, (steps - 2) * block), low),
            jax.ShapeDtypeStruct((rows, 2 * block), low),
        ],
        compiler_params=pltpu.CompilerParams(vmem_limit_bytes=40 * MIB),
        cost_estimate=pl.CostEstimate(
            flops=2 * rows * width * weight.shape[0],
            bytes_accessed=2 * (weight.size + 4 * tokens.size),
            transcendentals=0,
        ),
        name="project_heads",
    )(tokens, gain, weight, bias, cosine, signed_sine)


def unit_kernel(normed, d_hidden, gate, up, hidden, d_gate, d_up):
    gate_pre = dot(gate[...], normed[...], NT)
    up_pre = dot(up[...], normed[...], NT)
    d_mid = d_hidden[...].astype(jnp.float32)
    sig = 1.0 / (1.0 + jnp.exp(-gate_pre))
    silu = gate_pre * sig
    hidden[...] = (silu * up_pre).astype(hidden.dtype)
    d_up[...] = (d_mid * silu).astype(d_up.dtype)
    d_gate[...] = (d_mid * up_pre * (sig + silu * (1.0 - sig))).astype(d_gate.dtype)


def unit_rows(normed, d_hidden, gate, up):
    units, width = gate.shape
    rows = normed.shape[0]
    block = units // 4
    part = pl.BlockSpec((block, width), lambda i: (i, 0))
    out = pl.BlockSpec((block, rows), lambda i: (i, 0))
    shape = jax.ShapeDtypeStruct((units, rows), jnp.bfloat16)
    return pl.pallas_call(
        unit_kernel,
        grid=(units // block,),
        in_specs=[pl.BlockSpec((rows, width), lambda i: (0, 0)), out, part, part],
        out_specs=[out, out, out],
        out_shape=[shape, shape, shape],
        compiler_params=pltpu.CompilerParams(vmem_limit_bytes=48 * MIB),
        cost_estimate=pl.CostEstimate(
            flops=4 * units * rows * width,
            bytes_accessed=4 * units * width + 8 * units * rows,
            transcendentals=2 * units * rows,
        ),
        name="unit_rows",
    )(normed, d_hidden, gate, up)


def rope_tables(positions):
    exponent = jnp.arange(0, HEAD, 2).astype(jnp.float32) / HEAD
    inverse = rope_base ** (-exponent)
    angles = positions.astype(jnp.float32)[:, None] * inverse[None, :]
    angles = jnp.concatenate([angles, angles], axis=1)
    return (jnp.cos(angles), jnp.sin(angles))


def rms_scale(values):
    return lax.rsqrt(jnp.mean(values * values, axis=-1, keepdims=True) + norm_eps)


def norm_back(d_normed, values, inv_scale, gain):
    scaled = d_normed * gain
    grad_gain = jnp.sum(d_normed * values * inv_scale, axis=0)
    inner = jnp.mean(scaled * values, axis=-1, keepdims=True)
    return (inv_scale * scaled - values * inv_scale * inv_scale * inv_scale * inner, grad_gain)


def project_rows(left, weight_rows):
    return jnp.einsum("rd,fd->rf", left, weight_rows, preferred_element_type=jnp.float32)


def flip(values, axis):
    return lax.ppermute(values, axis, [(0, 1), (1, 0)])


ALL_AXES = ("fa", "fb", "fc", "ch", "cl")
CTX_AXES = ("ch", "cl")


def gather_last(pieces):
    if lax.axis_size("fc") == 2:
        return jnp.concatenate([*pieces, *(flip(piece, "fc") for piece in pieces)], axis=0)
    return lax.all_gather(jnp.concatenate(pieces, axis=0), "fc", axis=0, tiled=True)


def over_a(values):
    if lax.axis_size("fa") == 2:
        return flip(values, "fa")
    return lax.all_gather(values, "fa", axis=0, tiled=True)


def join_a(own, other):
    if lax.axis_size("fa") == 2:
        return [*own, *other]
    count = lax.axis_size("fa")
    blocks = [block.reshape(count, -1, block.shape[1]) for block in other]
    return [jnp.concatenate(blocks, axis=1).reshape(-1, blocks[0].shape[2])]


def scatter_half(values, axis):
    half = values.shape[0] // 2
    return values[:half].astype(jnp.float32) + flip(values[half:], axis).astype(jnp.float32)


def scatter_a(values):
    if lax.axis_size("fa") == 2:
        return scatter_half(values, "fa")
    return lax.psum_scatter(values, "fa", scatter_dimension=0, tiled=True).astype(jnp.float32)


def far_rows(over_x, over_z):
    half = over_x.shape[0] // 2
    return jnp.concatenate([flip(over_z[:half], "fb"), flip(over_x[half:], "cl")], axis=0)


def scatter_far(far):
    half = far.shape[0] // 2
    return flip(far[:half], "fb"), flip(far[half:], "cl")


def scatter_near(over_x, over_z, from_x, from_z):
    half = over_x.shape[0] // 2
    low, wide = jnp.bfloat16, jnp.float32
    send_z = jnp.concatenate([over_z[:half] + from_x.astype(wide), over_z[half:]], axis=0)
    send_x = jnp.concatenate([over_x[:half], over_x[half:] + from_z.astype(wide)], axis=0)
    return send_x.astype(low), send_z.astype(low)


def scatter_end(own, send_x, send_z):
    wide = jnp.float32
    return own + flip(send_x, "fb").astype(wide) + flip(send_z, "cl").astype(wide)


def pack_vectors(vectors, blocks):
    flat = jnp.concatenate([v.reshape(blocks, -1) for v in vectors], axis=1)
    lanes = -(-flat.shape[1] // 1024) * 128
    flat = jnp.pad(flat, ((0, 0), (0, 8 * lanes - flat.shape[1])))
    return flat.reshape(blocks, 8, lanes)


def unpack_vectors(packed, sizes):
    flat = packed.reshape(packed.shape[0], -1)
    out = []
    start = 0
    for size in sizes:
        out.append(flat[:, start : start + size].reshape(-1))
        start += size
    return out


def xor_send(values, bits):
    count = lax.axis_size(CTX_AXES)
    return lax.ppermute(values, CTX_AXES, [(i, i ^ bits) for i in range(count)])


def stack_in_order(own, other, axis, dim):
    later = lax.axis_index(axis) == 1
    return jnp.stack([jnp.where(later, other, own), jnp.where(later, own, other)], axis=dim)


def stack_axis(values, axis, dim):
    if lax.axis_size(axis) == 2:
        return stack_in_order(values, flip(values, axis), axis, dim)
    return lax.all_gather(values, axis, axis=dim, tiled=False)


def stack_ctx(values):
    rel = [values] + [xor_send(values, k) for k in (1, 2, 3)]
    high, low = lax.axis_index("ch") == 1, lax.axis_index("cl") == 1
    rel = [jnp.where(low, rel[k ^ 1], rel[k]) for k in range(4)]
    rel = [jnp.where(high, rel[k ^ 2], rel[k]) for k in range(4)]
    return jnp.stack(rel).reshape(2, 2, *values.shape)


def stack_plane(over_z):
    if lax.axis_size("fa") != 2:
        return stack_axis(stack_axis(over_z, "fb", 0), "fa", 0)
    half = over_z.shape[2] // 2
    by_a, by_b = flip(over_z, "fa"), flip(over_z, "fb")
    far = jnp.concatenate([flip(by_a[:, :, :half], "fb"), flip(by_b[:, :, half:], "fa")], axis=2)
    near = stack_in_order(over_z, by_b, "fb", 0)
    beyond = stack_in_order(by_a, far, "fb", 0)
    return stack_in_order(near, beyond, "fa", 0)


def stack_core(plane):
    return stack_axis(plane, "fc", 2)


def pick(values, index, dim):
    return lax.dynamic_index_in_dim(values, index, dim, keepdims=False)


def scatter_axis(values, axis, dim):
    if lax.axis_size(axis) == 2:
        me = lax.axis_index(axis)
        kept, sent = pick(values, me, dim), pick(values, 1 - me, dim)
        return (kept.astype(jnp.float32) + flip(sent, axis).astype(jnp.float32)).astype(values.dtype)
    return lax.psum_scatter(values, axis, scatter_dimension=dim, tiled=False)


def scatter_all(values):
    values = scatter_axis(values, "fc", 2)
    if lax.axis_size("fa") == 2:
        half = values.shape[-2] // 2
        wide = jnp.float32
        low = values.dtype
        me_a, me_b = lax.axis_index("fa"), lax.axis_index("fb")
        far = pick(pick(values, 1 - me_a, 0), 1 - me_b, 0)
        over_a = pick(pick(values, 1 - me_a, 0), me_b, 0).astype(wide)
        over_b = pick(pick(values, me_a, 0), 1 - me_b, 0).astype(wide)
        own = pick(pick(values, me_a, 0), me_b, 0).astype(wide)
        top, bottom = slice(None, half), slice(half, None)
        from_b = flip(far[..., top, :], "fb").astype(wide)
        from_a = flip(far[..., bottom, :], "fa").astype(wide)
        send_a = jnp.concatenate(
            [over_a[..., top, :] + from_b, over_a[..., bottom, :]], axis=-2
        ).astype(low)
        send_b = jnp.concatenate(
            [over_b[..., top, :], over_b[..., bottom, :] + from_a], axis=-2
        ).astype(low)
        values = (
            own + flip(send_a, "fa").astype(wide) + flip(send_b, "fb").astype(wide)
        ).astype(low)
    else:
        values = scatter_axis(scatter_axis(values, "fa", 0), "fb", 0)
    return scatter_axis(scatter_axis(values, "ch", 0), "cl", 0)


def after(values, *first):
    return lax.optimization_barrier((values, *first))[0]


def on_device(
    tokens, stretch_pairs, cotangent, w_qkv, b_qkv, w_out, norm_attn, norm_mlp, w_gate, w_up, w_down
):
    ctx_count = lax.axis_size(CTX_AXES)
    device_count = lax.axis_size(ALL_AXES)
    device_grid = tuple(lax.axis_size(axis) for axis in ALL_AXES)
    ctx_rank = lax.axis_index(CTX_AXES)
    seq_count = stretch_pairs.shape[0]
    row_count, width = tokens.shape
    local_len = row_count // seq_count
    half_len = local_len // 2
    seq_len = local_len * ctx_count
    query_width = HEADS * HEAD
    kv_width = KV_HEADS * HEAD
    low, wide = jnp.bfloat16, jnp.float32

    vectors_z = stack_ctx(pack_vectors([b_qkv, norm_attn, norm_mlp], 1)[0])
    qkv_z = stack_ctx(w_qkv)
    vectors_plane = stack_plane(after(vectors_z, qkv_z))
    qkv_plane = stack_plane(qkv_z)
    vectors_all = stack_core(vectors_plane)
    bias_all, gain_one, gain_two = unpack_vectors(
        vectors_all.reshape(device_count, 8, -1),
        (b_qkv.shape[0], norm_attn.shape[0], norm_mlp.shape[0]),
    )
    gain_one, gain_two = gain_one.astype(wide)[None], gain_two.astype(wide)[None]
    qkv_all = stack_core(qkv_plane).reshape(-1, width)

    out_z = stack_ctx(after(w_out, qkv_z))
    down_z = flip(after(w_down, qkv_z), "ch")
    gate_z = flip(after(w_gate, qkv_z), "ch")
    cot_z = flip(after(cotangent, qkv_z), "cl")
    out_plane = stack_plane(after(out_z, qkv_plane))
    cot_x = flip(after(cotangent, qkv_plane), "fb")
    down_a = over_a(after(w_down, qkv_plane))
    gate_a = over_a(after(w_gate, qkv_plane))

    rank_order = jnp.arange(ctx_count) ^ ctx_rank
    pairs = stretch_pairs[:, rank_order]
    own_pair = pairs[:, :1]
    blocks = jnp.arange(2 * ctx_count)
    block_pair = jnp.minimum(blocks, 2 * ctx_count - 1 - blocks)
    holder = jnp.argmax(pairs[:, None, :] == block_pair[None, :, None], axis=2)
    slots = 2 * holder + (blocks >= ctx_count)[None, :]
    table = jnp.concatenate(
        [own_pair, 2 * ctx_count - 1 - own_pair, slots.astype(jnp.int32)], axis=1
    )
    offsets = jnp.arange(local_len)
    positions = jnp.where(
        offsets < half_len,
        own_pair * half_len + offsets,
        (2 * ctx_count - 1 - own_pair) * half_len + offsets - half_len,
    )
    cosine, sine_table = rope_tables(positions.reshape(row_count))
    signed_sine = jnp.where(jnp.arange(HEAD) < HEAD // 2, -sine_table, sine_table)

    normed_one, queries, kv_low = project_heads(
        tokens, gain_one, qkv_all, bias_all.astype(wide)[None], cosine, signed_sine
    )
    kv_low = kv_low.reshape(seq_count, local_len, 2 * kv_width)
    kv_all = jnp.concatenate([kv_low, *(xor_send(kv_low, k) for k in (1, 2, 3))], axis=1)

    up_a = over_a(after(w_up, kv_low))
    out_all = stack_core(after(out_plane, kv_low)).reshape(-1, width)
    kv_all, down_z, gate_z, cot_z, cot_x, down_a, gate_a = lax.optimization_barrier(
        (kv_all, down_z, gate_z, cot_z, cot_x, down_a, gate_a)
    )
    up_z = flip(after(w_up, kv_all), "ch")
    down_az, gate_az = over_a(down_z), over_a(gate_z)
    cot_far = far_rows(cot_x, cot_z)
    cot_parts = [cotangent, cot_x, cot_z, cot_far]

    queries = queries.reshape(seq_count, local_len, query_width)
    keys, values = kv_all[..., :kv_width], kv_all[..., kv_width:]
    attended, log_totals = attend_forward(table, queries, keys, values)
    attended_rows = attended.reshape(row_count, query_width)
    inputs = tokens.astype(wide)
    middle = inputs + jnp.dot(attended_rows, out_all, preferred_element_type=wide)
    inv_two = rms_scale(middle)
    normed_two = (middle * inv_two * gain_two).astype(low)

    def all_units(own, by_z, by_a, by_az):
        return gather_last(join_a([own, by_z], [by_a, by_az]))

    normed_two, down_az, gate_az, up_z, up_a = lax.optimization_barrier(
        (normed_two, down_az, gate_az, up_z, up_a)
    )
    up_az = over_a(up_z)
    normed_x, normed_z = flip(normed_two, "fb"), flip(normed_two, "cl")
    down_part = all_units(w_down, down_z, down_a, down_az)
    gate_part = all_units(w_gate, gate_z, gate_a, gate_az)
    d_hidden = [dot(down_part, cot, NT).astype(low) for cot in cot_parts]
    up_part = all_units(w_up, up_z, up_a, after(up_az, d_hidden[0]))
    normed_parts = [normed_two, normed_x, normed_z, far_rows(normed_x, normed_z)]

    def units(k, *first):
        return unit_rows(after(normed_parts[k], *first), d_hidden[k], gate_part, up_part)

    def back_units(k, *first):
        d_gate_k = after(d_gate[k], *first)
        return dot(d_gate_k, gate_part, TN) + dot(d_up[k], up_part, TN)

    results = [units(0)]
    for k in (1, 2, 3):
        results.append(units(k, results[-1][0]))
    hidden, d_gate, d_up = zip(*results)
    back_far = back_units(3)
    from_x, from_z = scatter_far(back_far.astype(low))
    back_x = back_units(1, back_far)
    back_z = back_units(2, back_x)
    send_x, send_z = scatter_near(back_x, back_z, from_x, from_z)
    back_own = back_units(0, send_x, send_z)
    down_terms = unit_grads([after(hidden[0], back_own), *hidden[1:]], cot_parts)
    gate_terms = unit_grads([after(d_gate[0], down_terms), *d_gate[1:]], normed_parts)
    d_normed_two = scatter_end(after(back_own, gate_terms), send_x, send_z)

    d_mid_norm, grad_gain_two = norm_back(d_normed_two, middle, inv_two, gain_two)
    d_middle = cotangent.astype(wide) + d_mid_norm
    d_branch = d_middle.astype(low)
    d_attended = project_rows(d_branch, out_all).astype(low)
    down_terms = scatter_half(down_terms, "fc").astype(low)
    gate_terms = scatter_half(gate_terms, "fc").astype(low)
    d_attended, down_terms, gate_terms = lax.optimization_barrier(
        (d_attended, down_terms, gate_terms)
    )
    down_terms = scatter_a(down_terms).astype(low)
    gate_terms = scatter_a(gate_terms).astype(low)
    d_queries, d_keys_parts, d_values_parts = attend_backward(
        table,
        queries,
        keys,
        values,
        d_attended.reshape(seq_count, local_len, query_width),
        attended,
        log_totals,
        cosine,
        signed_sine,
    )
    d_queries = d_queries.reshape(row_count, query_width)
    d_kv_parts = jnp.concatenate([d_keys_parts, d_values_parts], axis=-1)
    d_kv_parts = d_kv_parts.reshape(seq_count, ctx_count, local_len, 2 * kv_width)
    d_kv_sent = [xor_send(d_kv_parts[:, k], k) for k in (1, 2, 3)]

    d_queries, down_terms = lax.optimization_barrier((d_queries, down_terms))
    grad_down = scatter_half(down_terms, "ch")
    up_terms = unit_grads([after(d_up[0], d_queries), *d_up[1:]], normed_parts)
    up_sent = scatter_half(up_terms, "fc").astype(low)
    grad_out_local = dot(after(attended_rows, up_terms), d_branch, TN).astype(low)
    query_terms = dot(after(d_queries, up_terms), normed_one, TN)
    branch = [dot(after(h, query_terms), down_part, TN) for h in hidden]
    d_kv_parts, gate_terms, up_terms, branch[3], grad_out_local, d_kv_sent[0] = (
        lax.optimization_barrier(
            (d_kv_parts, gate_terms, up_sent, branch[3], grad_out_local, d_kv_sent[0])
        )
    )
    grad_gate = scatter_half(gate_terms, "ch")
    up_terms = scatter_a(up_terms).astype(low)
    branch_from = scatter_far(branch[3].astype(low))
    grad_out = scatter_all(grad_out_local.reshape(*device_grid, -1, width)).astype(wide)

    d_kv = d_kv_parts[:, 0].astype(wide)
    for sent in d_kv_sent:
        d_kv += sent.astype(wide)
    d_kv = d_kv.reshape(row_count, 2 * kv_width)
    d_keys = []
    for start in range(0, kv_width, HEAD):
        part = d_kv[:, start : start + HEAD]
        d_keys.append(part * cosine - jnp.roll(part, HEAD // 2, 1) * signed_sine)
    d_kv = jnp.concatenate([*d_keys, d_kv[:, kv_width:]], axis=1).astype(low)
    query_bias_local = jnp.sum(d_queries, axis=0, dtype=wide)
    kv_bias_local = jnp.sum(d_kv, axis=0, dtype=wide)
    kv_terms = dot(d_kv, normed_one, TN)
    qkv_local = jnp.concatenate([query_terms, kv_terms], axis=0)
    branch_sent = scatter_near(branch[1], branch[2], *branch_from)
    branch_two = scatter_end(branch[0], *branch_sent)
    layer_out = (middle + branch_two).astype(low)
    grad_up = scatter_half(up_terms, "ch")
    grad_qkv = scatter_all(qkv_local.astype(low).reshape(*device_grid, -1, width)).astype(wide)
    d_normed_one = dot(d_queries, qkv_all[:query_width], NN) + dot(d_kv, qkv_all[query_width:], NN)
    inv_one = rms_scale(inputs)
    d_in_norm, grad_gain_one = norm_back(d_normed_one, inputs, inv_one, gain_one)
    grad_tokens = d_middle + d_in_norm
    vector_grads = [query_bias_local, kv_bias_local, grad_gain_one, grad_gain_two]
    vector_shares = scatter_all(
        pack_vectors(vector_grads, device_count).reshape(*device_grid, 8, -1)
    )
    grad_query_bias, grad_kv_bias, grad_norm_attn, grad_norm_mlp = unpack_vectors(
        vector_shares[None], [v.shape[0] // device_count for v in vector_grads]
    )
    return (
        layer_out,
        grad_tokens,
        grad_qkv,
        grad_query_bias,
        grad_kv_bias,
        grad_out,
        grad_norm_attn,
        grad_norm_mlp,
        grad_gate,
        grad_up,
        grad_down,
    )


def solution(mesh):
    fsdp_count, ctx_count = mesh.shape["fsdp"], mesh.shape["ctx"]
    parts = (fsdp_count // 4, 2, 2, ctx_count // 2, 2)
    split_mesh = Mesh(mesh.devices.reshape(parts), ALL_AXES)
    rows, whole = P(ALL_AXES, None), P(ALL_AXES)
    return jax.shard_map(
        on_device,
        mesh=split_mesh,
        in_specs=(
            rows,
            P(("fa", "fb", "fc"), None),
            rows,
            rows,
            whole,
            rows,
            whole,
            whole,
            rows,
            rows,
            rows,
        ),
        out_specs=(rows, rows, rows, whole, whole, rows, whole, whole, rows, rows, rows),
        check_vma=False,
    )
```

time: 1720 us -> 928 us (0.54)
  waiting for transfers between devices: 1090 us -> 375 us
  matrix products: 365 us -> 139 us
  Pallas kernels: 0 us -> 162 us
  starting transfers between devices: 0.97 us -> 92.3 us
  blocking collectives: 84.1 us -> 0 us
  other arithmetic: 115 us -> 64.4 us
  local copies, waits for them, and re-layouts: 45.2 us -> 83 us
    reduce_scatter x6 -> x0, waiting for transfers between devices: 645 us -> none  [the longest x1 212 us: on_device(): lax.psum_scatter(branch_part, 'ctx', scatter_dimension=0, tiled=True)]
    all_gather x9 -> x0, waiting for transfers between devices: 385 us -> none  [the longest x1 117 us: on_device(): lax.all_gather(normed_two, 'ctx', axis=0, tiled=True)]
    ppermute x0 -> x97, waiting for transfers between devices: none -> 375 us  [the longest x82 299 us: flip(): return lax.ppermute(values, axis, [(0, 1), (1, 0)])]
    pallas_call x0 -> x10, Pallas kernels: none -> 162 us  [the longest x3 60.2 us: unit_grads(): pl.pallas_call(functools.partial(grad_kernel, count), grid=(units // bloc...]
    dot_general x16 -> x22, matrix products: 278 us -> 132 us  [the longest x21 129 us: dot(): lax.dot_general(left, right, dims, preferred_element_type=jnp.float32)]
    ppermute x0 -> x97, starting transfers between devices: none -> 92.3 us  [the longest x82 68 us: flip(): return lax.ppermute(values, axis, [(0, 1), (1, 0)])]
    unnamed x2 -> x0, blocking collectives: 84.1 us -> none
    dot_general x5 -> x1, matrix products: 87.1 us -> 7.29 us  [project_rows(): jnp.einsum('rd,fd->rf', left, weight_rows, preferred_element_type=jnp.flo...]
  transfers between devices with their start and end apart: 16 -> 97, of which waited for: 14 -> 32; matrix products, arithmetic and copies ran while one was open for 19% -> 26% of each run, Pallas kernels for 0% -> 16%
where the time goes in v1:
time: 928 us; the launch traced here: 919 us
  waiting for transfers between devices  375 us (40%)
  Pallas kernels  162 us (17%)
  matrix products  139 us (15%)
  starting transfers between devices  92.3 us (10%)
  local copies, waits for them, and re-layouts  83 us (9%)
  other arithmetic  64.4 us (7%)
    ppermute x82, waiting for transfers between devices, flip(): return lax.ppermute(values, axis, [(0, 1), (1, 0)])  299 us
    dot_general x21, matrix products, dot(): lax.dot_general(left, right, dims, preferred_element_type=jnp.float32)  129 us
    ppermute x15, waiting for transfers between devices, xor_send(): return lax.ppermute(values, CTX_AXES, [(i, i ^ bits) for i in range(count)])  76.5 us
    ppermute x82, starting transfers between devices, flip(): return lax.ppermute(values, axis, [(0, 1), (1, 0)])  68 us
    pallas_call x3, Pallas kernels, unit_grads(): pl.pallas_call(functools.partial(grad_kernel, count), grid=(units // bloc...  60.2 us
    pallas_call x4, Pallas kernels, unit_rows(): pl.pallas_call(unit_kernel, grid=(units // block,), in_specs=[pl.BlockSpe...  50.2 us
    unnamed x247, local copies, waits for them, and re-layouts  46 us
    pallas_call x1, Pallas kernels, attend_backward(): pl.pallas_call(backward_kernel, grid=(seqs, KV_HEADS, 2), in_specs=[pl.Bl...  26.7 us
  transfers between devices with their start and end apart: 97, of which 32 were waited for; matrix products, arithmetic and copies ran while one was open for 26% of the time, Pallas kernels for 16%

profile of v1, /device:TPU:0, one launch (start us, length us, event | category | flops | bytes accessed | tf_op | source)
XLA Modules:
  0.0 918.8 jit_solution(855448102985635368)
XLA Ops:
  30.5 11.3 %collective-permute-done.6 = bf16[2,2,8,128]{3,2,1,0:T(8,128)(2,1)S(1)} collective-permute-done((bf16[2,2,8,128]{3,2,1,0:T(8,128)(2,1)S(1)}, bf16[2,2,8,128]{3,2,1,0:T(8,128)(2,1)S(1)}, u32[]{:S(2)}, u32[]{:S(2)}) %collective-permute-start.6) | collective-permute-done | bytes 8224 | tf_op jit(solution)/shard_map/ppermute | solution.py:365
  61.4 20.7 %collective-permute-done.27 = bf16[48,1536]{1,0:T(8,128)(2,1)S(1)} collective-permute-done((bf16[48,1536]{1,0:T(8,128)(2,1)S(1)}, bf16[48,1536]{1,0:T(8,128)(2,1)S(1)}, u32[]{:S(2)}, u32[]{:S(2)}) %collective-permute-start.27) | collective-permute-done | bytes 147488 | tf_op jit(solution)/shard_map/ppermute | solution.py:445
  84.6 12.8 %collective-permute-done.28 = bf16[2,2,48,1536]{3,2,1,0:T(8,128)(2,1)S(1)} collective-permute-done((bf16[2,2,48,1536]{3,2,1,0:T(8,128)(2,1)S(1)}, bf16[2,2,48,1536]{3,2,1,0:T(8,128)(2,1)S(1)}, u32[]{:S(2)}, u32[]{:S(2)}) %collective-permute-start.28) | collective-permute-done | bytes 589856 | tf_op jit(solution)/shard_map/ppermute | solution.py:365
  122.2 19.5 %collective-permute-done.16 = bf16[1,512,512]{2,1,0:T(8,128)(2,1)S(1)} collective-permute-done((bf16[1,512,512]{2,1,0:T(8,128)(2,1)S(1)}, bf16[1,512,512]{2,1,0:T(8,128)(2,1)S(1)}, u32[]{:S(2)}, u32[]{:S(2)}) %collective-permute-start.16) | collective-permute-done | bytes 524320 | tf_op jit(solution)/shard_map/ppermute | solution.py:445
  141.7 33.5 %collective-permute-done.17 = bf16[1,512,512]{2,1,0:T(8,128)(2,1)S(1)} collective-permute-done((bf16[1,512,512]{2,1,0:T(8,128)(2,1)S(1)}, bf16[1,512,512]{2,1,0:T(8,128)(2,1)S(1)}, u32[]{:S(2)}, u32[]{:S(2)}) %collective-permute-start.17) | collective-permute-done | bytes 524320 | tf_op jit(solution)/shard_map/ppermute | solution.py:445
  177.8 23.6 %collective-permute-done.20 = bf16[280,1536]{1,0:T(8,128)(2,1)} collective-permute-done((bf16[280,1536]{1,0:T(8,128)(2,1)S(1)}, bf16[280,1536]{1,0:T(8,128)(2,1)}, u32[]{:S(2)}, u32[]{:S(2)}) %collective-permute-start.20) | collective-permute-done | bytes 860192 | tf_op jit(solution)/shard_map/ppermute | solution.py:365
  223.3 17.0 %attend_forward.1 = (bf16[1,512,1536]{2,1,0:T(8,128)(2,1)S(1)}, f32[1,2,2,6,256]{4,3,2,1,0:T(8,128)S(1)}) custom-call(s32[1,10]{1,0:T(1,128)S(1)} %pad_add_fusion.table, bf16[1,512,1536]{2,1,0:T(8,128)(2,1)S(1)} %bitcast.253, bf16[1,2048,256]{2,1,0:T(8,128)(2,1)S(1)} %get-tuple-element.179.k_ref, bf16[1,2048,256]{2,1,0:T(8,128)(2,1)S(1)} %get-tuple-element.178.v_ref), custom_call_target="tpu_custom_call" | custom-call | flops 3623878656 | bytes 6291456 | tf_op jit(solution)/shard_map/attend_forward/pallas_call | solution.py:102
  249.0 25.8 %collective-permute-done.35 = bf16[280,1536]{1,0:T(8,128)(2,1)} collective-permute-done((bf16[280,1536]{1,0:T(8,128)(2,1)S(1)}, bf16[280,1536]{1,0:T(8,128)(2,1)}, u32[]{:S(2)}, u32[]{:S(2)}) %collective-permute-start.35) | collective-permute-done | bytes 860192 | tf_op jit(solution)/shard_map/ppermute | solution.py:365
  330.9 13.3 %collective-permute-done.51.normed.refs_6_ = bf16[512,1536]{1,0:T(8,128)(2,1)S(1)} collective-permute-done((bf16[512,1536]{1,0:T(8,128)(2,1)S(1)}, bf16[512,1536]{1,0:T(8,128)(2,1)S(1)}, u32[]{:S(2)}, u32[]{:S(2)}) %collective-permute-start.51) | collective-permute-done | bytes 1572896 | tf_op jit(solution)/shard_map/ppermute | solution.py:365
  346.8 12.4 %unit_rows.4 = (bf16[2240,512]{1,0:T(8,128)(2,1)S(1)}, bf16[2240,512]{1,0:T(8,128)(2,1)S(1)}, bf16[2240,512]{1,0:T(8,128)(2,1)}) custom-call(bf16[512,1536]{1,0:T(8,128)(2,1)S(1)} %multiply_convert_fusion.normed.refs_4_, bf16[2240,512]{1,0:T(8,128)(2,1)} %convolution_convert_fusion.4.d_hidden, bf16[2240,1536]{1,0:T(8,128)(2,1)} %constant_dynamic-update-slice_fusion.12.gate, ...), custom_call_target="tpu_custom_call" | custom-call | flops 7046430720 | bytes 22937600 | tf_op jit(solution)/shard_map/unit_rows/pallas_call | solution.py:325
  360.7 12.9 %unit_rows.5 = (bf16[2240,512]{1,0:T(8,128)(2,1)S(1)}, bf16[2240,512]{1,0:T(8,128)(2,1)S(1)}, bf16[2240,512]{1,0:T(8,128)(2,1)}) custom-call(bf16[512,1536]{1,0:T(8,128)(2,1)S(1)} %collective-permute-done.50.normed.refs_5_, bf16[2240,512]{1,0:T(8,128)(2,1)} %convolution_convert_fusion.3.d_hidden, ...), custom_call_target="tpu_custom_call" | custom-call | flops 7046430720 | bytes 22937600 | tf_op jit(solution)/shard_map/unit_rows/pallas_call | solution.py:325
  385.1 12.2 %unit_rows.6 = (bf16[2240,512]{1,0:T(8,128)(2,1)S(1)}, bf16[2240,512]{1,0:T(8,128)(2,1)S(1)}, bf16[2240,512]{1,0:T(8,128)(2,1)}) custom-call(bf16[512,1536]{1,0:T(8,128)(2,1)S(1)} %collective-permute-done.51.normed.refs_6_, bf16[2240,512]{1,0:T(8,128)(2,1)} %convolution_convert_fusion.2.d_hidden, ...), custom_call_target="tpu_custom_call" | custom-call | flops 7046430720 | bytes 22937600 | tf_op jit(solution)/shard_map/unit_rows/pallas_call | solution.py:325
  397.4 10.9 %fusion.64 = f32[512,1536]{1,0:T(8,128)} fusion(bf16[2240,512]{1,0:T(8,128)(2,1)} %get-tuple-element.127.refs_2_, bf16[2240,1536]{1,0:T(8,128)(2,1)} %constant_dynamic-update-slice_fusion.20.up), kind=kOutput, calls=%fused_computation.292 | convolution fusion | flops 3523215360 | bytes 12320768 | tf_op jit(solution)/shard_map/dot_general | solution.py:29
  416.9 12.6 %unit_rows.7 = (bf16[2240,512]{1,0:T(8,128)(2,1)S(1)}, bf16[2240,512]{1,0:T(8,128)(2,1)S(1)}, bf16[2240,512]{1,0:T(8,128)(2,1)}) custom-call(bf16[512,1536]{1,0:T(8,128)(2,1)S(1)} %constant_dynamic-update-slice_fusion.28.normed.refs_7_, bf16[2240,512]{1,0:T(8,128)(2,1)} %convolution_convert_fusion.1.d_hidden, ...), custom_call_target="tpu_custom_call" | custom-call | flops 7046430720 | bytes 22937600 | tf_op jit(solution)/shard_map/unit_rows/pallas_call | solution.py:325
  479.4 19.9 %unit_grads.3 = bf16[2240,1536]{1,0:T(8,128)(2,1)} custom-call(bf16[2240,512]{1,0:T(8,128)(2,1)} %copy-done.8, bf16[2240,512]{1,0:T(8,128)(2,1)} %copy-done.29, bf16[2240,512]{1,0:T(8,128)(2,1)} %copy-done.31, bf16[2240,512]{1,0:T(8,128)(2,1)} %copy-done.35, bf16[512,1536]{1,0:T(8,128)(2,1)} %refs_4_.1, bf16[512,1536]{1,0:T(8,128)(2,1)} %collective-permute-done.22.refs_5_, ...), custom_call_target="tpu_custom_call" | custom-call | flops 14092861440 | bytes 15466496 | tf_op jit(solution)/shard_map/unit_grads/pallas_call | solution.py:222
  499.3 19.9 %unit_grads.4 = bf16[2240,1536]{1,0:T(8,128)(2,1)} custom-call(bf16[2240,512]{1,0:T(8,128)(2,1)} %copy-done.5, bf16[2240,512]{1,0:T(8,128)(2,1)} %copy-done.6, bf16[2240,512]{1,0:T(8,128)(2,1)} %copy-done.7, bf16[2240,512]{1,0:T(8,128)(2,1)} %copy-done.28, bf16[512,1536]{1,0:T(8,128)(2,1)} %copy-done.10, bf16[512,1536]{1,0:T(8,128)(2,1)} %copy-done.17, ...), custom_call_target="tpu_custom_call" | custom-call | flops 14092861440 | bytes 15466496 | tf_op jit(solution)/shard_map/unit_grads/pallas_call | solution.py:222
  562.0 26.7 %attend_backward.1 = (bf16[1,512,1536]{2,1,0:T(8,128)(2,1)S(1)}, bf16[1,2048,256]{2,1,0:T(8,128)(2,1)S(1)}, bf16[1,2048,256]{2,1,0:T(8,128)(2,1)S(1)}) custom-call(s32[1,10]{1,0:T(1,128)S(1)} %pad_add_fusion.table, bf16[1,512,1536]{2,1,0:T(8,128)(2,1)S(1)} %bitcast.254, bf16[1,2048,256]{2,1,0:T(8,128)(2,1)S(1)} %copy-done.16, ...), custom_call_target="tpu_custom_call" | custom-call | flops 9059696640 | bytes 12582912 | tf_op jit(solution)/shard_map/attend_backward/pallas_call | solution.py:184
  596.3 20.5 %unit_grads.5 = bf16[2240,1536]{1,0:T(8,128)(2,1)} custom-call(bf16[2240,512]{1,0:T(8,128)(2,1)} %get-tuple-element.139.refs_0_, bf16[2240,512]{1,0:T(8,128)(2,1)} %get-tuple-element.124.refs_1_, bf16[2240,512]{1,0:T(8,128)(2,1)} %get-tuple-element.127.refs_2_, bf16[2240,512]{1,0:T(8,128)(2,1)} %get-tuple-element.122.refs_3_, bf16[512,1536]{1,0:T(8,128)(2,1)} %copy-done.10, ...), custom_call_target="tpu_custom_call" | custom-call | flops 14092861440 | bytes 15466496 | tf_op jit(solution)/shard_map/unit_grads/pallas_call | solution.py:222
  656.5 30.5 %collective-permute-done.96 = bf16[280,1536]{1,0:T(8,128)(2,1)S(1)} collective-permute-done((bf16[280,1536]{1,0:T(8,128)(2,1)S(1)}, bf16[280,1536]{1,0:T(8,128)(2,1)S(1)}, u32[]{:S(2)}, u32[]{:S(2)}) %collective-permute-start.96) | collective-permute-done | bytes 860192 | tf_op jit(solution)/shard_map/ppermute | solution.py:365
  724.0 19.5 %collective-permute-done.82 = f32[2,2,4,128]{3,2,1,0:T(4,128)S(1)} collective-permute-done((f32[2,2,4,128]{3,2,1,0:T(4,128)S(1)}, f32[2,2,4,128]{3,2,1,0:T(4,128)S(1)}, u32[]{:S(2)}, u32[]{:S(2)}) %collective-permute-start.82) | collective-permute-done | bytes 8224 | tf_op jit(solution)/shard_map/ppermute | solution.py:365
  768.5 18.6 %collective-permute-done.68 = bf16[256,1536]{1,0:T(8,128)(2,1)S(1)} collective-permute-done((bf16[256,1536]{1,0:T(8,128)(2,1)S(1)}, bf16[256,1536]{1,0:T(8,128)(2,1)S(1)}, u32[]{:S(2)}, u32[]{:S(2)}) %collective-permute-start.68) | collective-permute-done | bytes 786464 | tf_op jit(solution)/shard_map/ppermute | solution.py:365
  800.6 23.8 %collective-permute-done.67 = bf16[512,1536]{1,0:T(8,128)(2,1)S(1)} collective-permute-done((bf16[512,1536]{1,0:T(8,128)(2,1)S(1)}, bf16[512,1536]{1,0:T(8,128)(2,1)S(1)}, u32[]{:S(2)}, u32[]{:S(2)}) %collective-permute-start.67) | collective-permute-done | bytes 1572896 | tf_op jit(solution)/shard_map/ppermute | solution.py:365
  825.3 17.8 %collective-permute-done.69 = bf16[512,1536]{1,0:T(8,128)(2,1)} collective-permute-done((bf16[512,1536]{1,0:T(8,128)(2,1)S(1)}, bf16[512,1536]{1,0:T(8,128)(2,1)}, u32[]{:S(2)}, u32[]{:S(2)}) %collective-permute-start.69) | collective-permute-done | bytes 1572896 | tf_op jit(solution)/shard_map/ppermute | solution.py:365
  895.9 14.6 %collective-permute-done.77 = bf16[2,64,1536]{2,1,0:T(8,128)(2,1)S(1)} collective-permute-done((bf16[2,64,1536]{2,1,0:T(8,128)(2,1)S(1)}, bf16[2,64,1536]{2,1,0:T(8,128)(2,1)S(1)}, u32[]{:S(2)}, u32[]{:S(2)}) %collective-permute-start.77) | collective-permute-done | bytes 393248 | tf_op jit(solution)/shard_map/ppermute | solution.py:365
  (620 shorter events, 465.3 us)
Async XLA Ops:
  59.0 142.4 %collective-permute-start.21 = (bf16[512,1536]{1,0:T(8,128)(2,1)}, bf16[512,1536]{1,0:T(8,128)(2,1)}, u32[]{:S(2)}, u32[]{:S(2)}) collective-permute-start(bf16[512,1536]{1,0:T(8,128)(2,1)} %refs_4_.1), channel_id=1, source_target_pairs={{0,1},{1,0},{2,3},{3,2},{4,5},{5,4},{6,7},{7,6},{8,9},{9,8},{10,11... | collective-permute-start | bytes 4718600 | tf_op jit(solution)/shard_map/ppermute | solution.py:365
  59.2 62.3 %collective-permute-start.19 = (bf16[280,1536]{1,0:T(8,128)(2,1)}, bf16[280,1536]{1,0:T(8,128)(2,1)}, u32[]{:S(2)}, u32[]{:S(2)}) collective-permute-start(bf16[280,1536]{1,0:T(8,128)(2,1)} %param.21), channel_id=1, source_target_pairs={{0,2},{2,0},{1,3},{3,1},{4,6},{6,4},{5,7},{7,5},{8,10},{10,8},{9,1... | collective-permute-start | bytes 2580488 | tf_op jit(solution)/shard_map/ppermute | solution.py:365
  105.3 97.8 %collective-permute-start.22 = (bf16[512,1536]{1,0:T(8,128)(2,1)}, bf16[512,1536]{1,0:T(8,128)(2,1)}, u32[]{:S(2)}, u32[]{:S(2)}) collective-permute-start(bf16[512,1536]{1,0:T(8,128)(2,1)} %refs_4_.1), channel_id=1, source_target_pairs={{0,8},{8,0},{1,9},{9,1},{2,10},{10,2},{3,11},{11,3},{4,12},{12,4},... | collective-permute-start | bytes 4718600 | tf_op jit(solution)/shard_map/ppermute | solution.py:365
  118.2 57.0 %collective-permute-start.17 = (bf16[1,512,512]{2,1,0:T(8,128)(2,1)S(1)}, bf16[1,512,512]{2,1,0:T(8,128)(2,1)S(1)}, u32[]{:S(2)}, u32[]{:S(2)}) collective-permute-start(bf16[1,512,512]{2,1,0:T(8,128)(2,1)S(1)} %bitcast.250), channel_id=1, source_target_pairs={{0,2},{1,3},{2,0},{3,1},{4,6},{5,7},{6,4},{7,5},{8,10},{9,11},{10,... | collective-permute-start | bytes 1572872 | tf_op jit(solution)/shard_map/ppermute | solution.py:445
  121.4 54.2 %collective-permute-start.18 = (bf16[1,512,512]{2,1,0:T(8,128)(2,1)S(1)}, bf16[1,512,512]{2,1,0:T(8,128)(2,1)S(1)}, u32[]{:S(2)}, u32[]{:S(2)}) collective-permute-start(bf16[1,512,512]{2,1,0:T(8,128)(2,1)S(1)} %bitcast.251), channel_id=1, source_target_pairs={{0,3},{1,2},{2,1},{3,0},{4,7},{5,6},{6,5},{7,4},{8,11},{9,10},{10,... | collective-permute-start | bytes 1572872 | tf_op jit(solution)/shard_map/ppermute | solution.py:445
  141.7 59.7 %collective-permute-start.20 = (bf16[280,1536]{1,0:T(8,128)(2,1)S(1)}, bf16[280,1536]{1,0:T(8,128)(2,1)}, u32[]{:S(2)}, u32[]{:S(2)}) collective-permute-start(bf16[280,1536]{1,0:T(8,128)(2,1)S(1)} %copy-done.75), channel_id=1, source_target_pairs={{0,2},{2,0},{1,3},{3,1},{4,6},{6,4},{5,7},{7,5},{8,10},{10,8},{9,1... | collective-permute-start | bytes 2580488 | tf_op jit(solution)/shard_map/ppermute | solution.py:365
  201.4 81.7 %collective-permute-start.37 = (bf16[280,1536]{1,0:T(8,128)(2,1)}, bf16[280,1536]{1,0:T(8,128)(2,1)}, u32[]{:S(2)}, u32[]{:S(2)}) collective-permute-start(bf16[280,1536]{1,0:T(8,128)(2,1)} %param.21), channel_id=1, source_target_pairs={{0,4},{4,0},{1,5},{5,1},{2,6},{6,2},{3,7},{7,3},{8,12},{12,8},{9,1... | collective-permute-start | bytes 2580488 | tf_op jit(solution)/shard_map/ppermute | solution.py:365
  248.9 60.0 %collective-permute-start.46 = (bf16[280,1536]{1,0:T(8,128)(2,1)S(1)}, bf16[280,1536]{1,0:T(8,128)(2,1)S(1)}, u32[]{:S(2)}, u32[]{:S(2)}) collective-permute-start(bf16[280,1536]{1,0:T(8,128)(2,1)S(1)} %copy-done.77), channel_id=1, source_target_pairs={{0,4},{4,0},{1,5},{5,1},{2,6},{6,2},{3,7},{7,3},{8,12},{12,8},{9,1... | collective-permute-start | bytes 2580488 | tf_op jit(solution)/shard_map/ppermute | solution.py:365
  344.3 72.5 %collective-permute-start.52 = (bf16[256,1536]{1,0:T(8,128)(2,1)S(1)}, bf16[256,1536]{1,0:T(8,128)(2,1)S(1)}, u32[]{:S(2)}, u32[]{:S(2)}) collective-permute-start(bf16[256,1536]{1,0:T(8,128)(2,1)S(1)} %slice.366), channel_id=1, source_target_pairs={{0,8},{8,0},{1,9},{9,1},{2,10},{10,2},{3,11},{11,3},{4,12},{12,4},... | collective-permute-start | bytes 2359304 | tf_op jit(solution)/shard_map/ppermute | solution.py:365
  345.4 71.4 %collective-permute-start.53 = (bf16[256,1536]{1,0:T(8,128)(2,1)S(1)}, bf16[256,1536]{1,0:T(8,128)(2,1)S(1)}, u32[]{:S(2)}, u32[]{:S(2)}) collective-permute-start(bf16[256,1536]{1,0:T(8,128)(2,1)S(1)} %slice.367), channel_id=1, source_target_pairs={{0,1},{1,0},{2,3},{3,2},{4,5},{5,4},{6,7},{7,6},{8,9},{9,8},{10,11... | collective-permute-start | bytes 2359304 | tf_op jit(solution)/shard_map/ppermute | solution.py:365
  463.1 63.3 %collective-permute-start.58 = (bf16[512,1536]{1,0:T(8,128)(2,1)S(1)}, bf16[512,1536]{1,0:T(8,128)(2,1)S(1)}, u32[]{:S(2)}, u32[]{:S(2)}) collective-permute-start(bf16[512,1536]{1,0:T(8,128)(2,1)S(1)} %pad_maximum_fusion.9), channel_id=1, source_target_pairs={{0,8},{8,0},{1,9},{9,1},{2,10},{10,2},{3,11},{11,3},{4,12},{12,4},... | collective-permute-start | bytes 4718600 | tf_op jit(solution)/shard_map/ppermute | solution.py:365
  473.3 53.1 %collective-permute-start.59 = (bf16[512,1536]{1,0:T(8,128)(2,1)}, bf16[512,1536]{1,0:T(8,128)(2,1)S(1)}, u32[]{:S(2)}, u32[]{:S(2)}) collective-permute-start(bf16[512,1536]{1,0:T(8,128)(2,1)} %pad_maximum_fusion.10), channel_id=1, source_target_pairs={{0,1},{1,0},{2,3},{3,2},{4,5},{5,4},{6,7},{7,6},{8,9},{9,8},{10,11... | collective-permute-start | bytes 4718600 | tf_op jit(solution)/shard_map/ppermute | solution.py:365
  553.6 93.6 %collective-permute-start.63 = (bf16[560,1536]{1,0:T(8,128)(2,1)}, bf16[560,1536]{1,0:T(8,128)(2,1)}, u32[]{:S(2)}, u32[]{:S(2)}) collective-permute-start(bf16[560,1536]{1,0:T(8,128)(2,1)} %slice.301), channel_id=1, source_target_pairs={{0,16},{16,0},{1,17},{17,1},{2,18},{18,2},{3,19},{19,3},{4,20},{20... | collective-permute-start | bytes 5160968 | tf_op jit(solution)/shard_map/ppermute | solution.py:365
  590.1 101.3 %collective-permute-start.65 = (bf16[1,512,512]{2,1,0:T(8,128)(2,1)}, bf16[1,512,512]{2,1,0:T(8,128)(2,1)}, u32[]{:S(2)}, u32[]{:S(2)}) collective-permute-start(bf16[1,512,512]{2,1,0:T(8,128)(2,1)} %get-tuple-element.177), channel_id=1, source_target_pairs={{0,1},{1,0},{2,3},{3,2},{4,5},{5,4},{6,7},{7,6},{8,9},{9,8},{10,11... | collective-permute-start | bytes 1572872 | tf_op jit(solution)/shard_map/ppermute | solution.py:445
  590.4 100.9 %collective-permute-start.70 = (bf16[1,512,512]{2,1,0:T(8,128)(2,1)}, bf16[1,512,512]{2,1,0:T(8,128)(2,1)}, u32[]{:S(2)}, u32[]{:S(2)}) collective-permute-start(bf16[1,512,512]{2,1,0:T(8,128)(2,1)} %get-tuple-element.175), channel_id=1, source_target_pairs={{0,2},{1,3},{2,0},{3,1},{4,6},{5,7},{6,4},{7,5},{8,10},{9,11},{10,... | collective-permute-start | bytes 1572872 | tf_op jit(solution)/shard_map/ppermute | solution.py:445
  592.1 99.3 %collective-permute-start.71 = (bf16[1,512,512]{2,1,0:T(8,128)(2,1)}, bf16[1,512,512]{2,1,0:T(8,128)(2,1)}, u32[]{:S(2)}, u32[]{:S(2)}) collective-permute-start(bf16[1,512,512]{2,1,0:T(8,128)(2,1)} %get-tuple-element.176), channel_id=1, source_target_pairs={{0,3},{1,2},{2,1},{3,0},{4,7},{5,6},{6,5},{7,4},{8,11},{9,10},{10,... | collective-permute-start | bytes 1572872 | tf_op jit(solution)/shard_map/ppermute | solution.py:445
  626.3 62.2 %collective-permute-start.64 = (bf16[1120,1536]{1,0:T(8,128)(2,1)}, bf16[1120,1536]{1,0:T(8,128)(2,1)}, u32[]{:S(2)}, u32[]{:S(2)}) collective-permute-start(bf16[1120,1536]{1,0:T(8,128)(2,1)} %slice.381), channel_id=1, source_target_pairs={{0,4},{4,0},{1,5},{5,1},{2,6},{6,2},{3,7},{7,3},{8,12},{12,8},{9,1... | collective-permute-start | bytes 10321928 | tf_op jit(solution)/shard_map/ppermute | solution.py:365
  703.5 89.8 %collective-permute-start.94 = (bf16[560,1536]{1,0:T(8,128)(2,1)}, bf16[560,1536]{1,0:T(8,128)(2,1)}, u32[]{:S(2)}, u32[]{:S(2)}) collective-permute-start(bf16[560,1536]{1,0:T(8,128)(2,1)} %slice.350), channel_id=1, source_target_pairs={{0,16},{16,0},{1,17},{17,1},{2,18},{18,2},{3,19},{19,3},{4,20},{20... | collective-permute-start | bytes 5160968 | tf_op jit(solution)/shard_map/ppermute | solution.py:365
  705.7 82.7 %collective-permute-start.93 = (bf16[280,1536]{1,0:T(8,128)(2,1)}, bf16[280,1536]{1,0:T(8,128)(2,1)}, u32[]{:S(2)}, u32[]{:S(2)}) collective-permute-start(bf16[280,1536]{1,0:T(8,128)(2,1)} %slice.348), channel_id=1, source_target_pairs={{0,2},{2,0},{1,3},{3,1},{4,6},{6,4},{5,7},{7,5},{8,10},{10,8},{9,1... | collective-permute-start | bytes 2580488 | tf_op jit(solution)/shard_map/ppermute | solution.py:365
  707.3 89.1 %collective-permute-start.86 = (bf16[2,2,2,2,48,1536]{5,4,3,2,1,0:T(8,128)(2,1)}, bf16[2,2,2,2,48,1536]{5,4,3,2,1,0:T(8,128)(2,1)}, u32[]{:S(2)}, u32[]{:S(2)}) collective-permute-start(bf16[2,2,2,2,48,1536]{5,4,3,2,1,0:T(8,128)(2,1)} %dynamic-slice_bitcast_fusion.1), channel_id=1, source_target_pairs={{0,4},{4,0},{1,5},{5,1},{2,6},{6,2},{3,7},{7,3},{8,12},{12,8},{9,1... | collective-permute-start | bytes 7077896 | tf_op jit(solution)/shard_map/ppermute | solution.py:365
  765.9 85.3 %collective-permute-start.72 = (bf16[2,2,2,2,64,1536]{5,4,3,2,1,0:T(8,128)(2,1)S(1)}, bf16[2,2,2,2,64,1536]{5,4,3,2,1,0:T(8,128)(2,1)}, u32[]{:S(2)}, u32[]{:S(2)}) collective-permute-start(bf16[2,2,2,2,64,1536]{5,4,3,2,1,0:T(8,128)(2,1)S(1)} %dynamic-slice_bitcast_fusion), channel_id=1, source_target_pairs={{0,4},{4,0},{1,5},{5,1},{2,6},{6,2},{3,7},{7,3},{8,12},{12,8},{9,1... | collective-permute-start | bytes 9437192 | tf_op jit(solution)/shard_map/ppermute | solution.py:365
  788.4 54.6 %collective-permute-start.69 = (bf16[512,1536]{1,0:T(8,128)(2,1)S(1)}, bf16[512,1536]{1,0:T(8,128)(2,1)}, u32[]{:S(2)}, u32[]{:S(2)}) collective-permute-start(bf16[512,1536]{1,0:T(8,128)(2,1)S(1)} %pad_maximum_fusion.12), channel_id=1, source_target_pairs={{0,1},{1,0},{2,3},{3,2},{4,5},{5,4},{6,7},{7,6},{8,9},{9,8},{10,11... | collective-permute-start | bytes 4718600 | tf_op jit(solution)/shard_map/ppermute | solution.py:365
  796.1 79.7 %collective-permute-start.95 = (bf16[280,1536]{1,0:T(8,128)(2,1)}, bf16[280,1536]{1,0:T(8,128)(2,1)}, u32[]{:S(2)}, u32[]{:S(2)}) collective-permute-start(bf16[280,1536]{1,0:T(8,128)(2,1)} %slice.421), channel_id=1, source_target_pairs={{0,2},{2,0},{1,3},{3,1},{4,6},{6,4},{5,7},{7,5},{8,10},{10,8},{9,1... | collective-permute-start | bytes 2580488 | tf_op jit(solution)/shard_map/ppermute | solution.py:365
  799.4 50.2 %collective-permute-start.87 = (bf16[2,2,24,1536]{3,2,1,0:T(8,128)(2,1)S(1)}, bf16[2,2,24,1536]{3,2,1,0:T(8,128)(2,1)S(1)}, u32[]{:S(2)}, u32[]{:S(2)}) collective-permute-start(bf16[2,2,24,1536]{3,2,1,0:T(8,128)(2,1)S(1)} %get-tuple-element.204), channel_id=1, source_target_pairs={{0,8},{8,0},{1,9},{9,1},{2,10},{10,2},{3,11},{11,3},{4,12},{12,4},... | collective-permute-start | bytes 884744 | tf_op jit(solution)/shard_map/ppermute | solution.py:365
  (183 other events, 3813.7 us)

commit v2 on v1

v2 whole, which is shorter than its diff:
```python
import functools

import jax
import jax.numpy as jnp
from jax import lax
from jax.experimental import pallas as pl
from jax.experimental.pallas import tpu as pltpu
from jax.sharding import Mesh
from jax.sharding import PartitionSpec as P

HEADS = 12
KV_HEADS = 2
HEAD = 128
GROUP = HEADS // KV_HEADS
MIB = 2**20
COST_FACTOR = 16


def cost(flops, nbytes, transcendentals=0):
    return pl.CostEstimate(
        flops=flops * COST_FACTOR,
        bytes_accessed=nbytes * COST_FACTOR,
        transcendentals=transcendentals * COST_FACTOR,
    )


rope_base = 1000000.0
norm_eps = 1e-06

LOG2E = 1.4426950408889634
SCALE = HEAD ** -0.5

NT = (((1,), (1,)), ((), ()))
NN = (((1,), (0,)), ((), ()))
TN = (((0,), (0,)), ((), ()))


def with_tokens(kernel, count, tokens):
    return lambda *refs: kernel(*refs[:count], *refs[count + tokens :])


def dot(left, right, dims):
    return lax.dot_general(left, right, dims, preferred_element_type=jnp.float32)


def forward_kernel(table, q_ref, k_ref, v_ref, o_ref, lse_ref, top, total, acc):
    half = pl.program_id(2)
    block = q_ref.shape[1]
    last = table[0, half]
    spot = table[0, 2 + last]
    heads = range(GROUP)

    def part(slot, masked, first):
        rows = pl.ds(pl.multiple_of(slot % 2 * block, block), block)
        keys, values = k_ref[slot // 2, 0, rows, :], v_ref[slot // 2, 0, rows, :]
        if not first:
            old_top = [top[j] for j in heads]
            old_total = [total[j] for j in heads]
        scores = [dot(keys, q_ref[0, :, pl.ds(j * HEAD, HEAD)], NT) for j in heads]
        if masked:
            key_at = lax.broadcasted_iota(jnp.int32, scores[0].shape, 0)
            query_at = lax.broadcasted_iota(jnp.int32, scores[0].shape, 1)
            scores = [jnp.where(key_at <= query_at, s, -1e30) for s in scores]
        tops = [jnp.max(s, axis=0, keepdims=True) * (SCALE * LOG2E) for s in scores]
        if not first:
            tops = [jnp.maximum(t, o) for t, o in zip(tops, old_top)]
        expon = [jnp.exp2(s * (SCALE * LOG2E) - t) for s, t in zip(scores, tops)]
        sums = [jnp.sum(e, axis=0, keepdims=True) for e in expon]
        added = [dot(values, e.astype(jnp.bfloat16), TN) for e in expon]
        for j in heads:
            if first:
                total[j] = sums[j]
                acc[j] = added[j]
            else:
                fade = jnp.exp2(old_top[j] - tops[j])
                total[j] = old_total[j] * fade + sums[j]
                acc[j] = acc[j] * fade + added[j]
            top[j] = tops[j]

    part(spot, True, True)

    def step(b, carry):
        part(table[0, 2 + b], False, False)
        return carry

    lax.fori_loop(0, last, step, 0)
    for j in heads:
        o_ref[0, :, pl.ds(j * HEAD, HEAD)] = (acc[j] / total[j]).T.astype(jnp.bfloat16)
        lse_ref[0, 0, 0, j] = (top[j] + jnp.log2(total[j]))[0]


def attend_forward(table, queries, kv, *first):
    seqs, rows, width = queries.shape
    block = rows // 2
    wide = GROUP * HEAD
    ranks = kv.shape[0]
    work = HEADS * rows * rows * ranks * seqs * 9 // 16
    return pl.pallas_call(
        with_tokens(forward_kernel, 4, len(first)),
        grid=(seqs, KV_HEADS, 2),
        in_specs=[
            pl.BlockSpec((1, table.shape[1]), lambda s, g, h: (s, 0), memory_space=pltpu.SMEM),
            pl.BlockSpec((1, block, wide), lambda s, g, h: (s, h, g)),
            pl.BlockSpec((ranks, 1, rows, HEAD), lambda s, g, h: (0, s, 0, g)),
            pl.BlockSpec((ranks, 1, rows, HEAD), lambda s, g, h: (0, s, 0, KV_HEADS + g)),
            *(pl.BlockSpec(memory_space=pl.ANY) for _ in first),
        ],
        out_specs=[
            pl.BlockSpec((1, block, wide), lambda s, g, h: (s, h, g)),
            pl.BlockSpec((1, 1, 1, GROUP, block), lambda s, g, h: (s, g, h, 0, 0)),
        ],
        out_shape=[
            jax.ShapeDtypeStruct(queries.shape, jnp.bfloat16),
            jax.ShapeDtypeStruct((seqs, KV_HEADS, 2, GROUP, block), jnp.float32),
        ],
        scratch_shapes=[
            pltpu.VMEM((GROUP, 1, block), jnp.float32),
            pltpu.VMEM((GROUP, 1, block), jnp.float32),
            pltpu.VMEM((GROUP, HEAD, block), jnp.float32),
        ],
        compiler_params=pltpu.CompilerParams(vmem_limit_bytes=40 * MIB),
        cost_estimate=cost(
            4 * HEAD * work, 6 * MIB, work
        ),
        name="attend_forward",
    )(table, queries, kv, kv, *first)


def backward_kernel(table, q_ref, k_ref, v_ref, g_ref, o_ref, lse_ref, cos_ref, sin_ref, dq_ref, dkv_ref, dk_acc, dv_acc, dq_acc, delta):
    half = pl.program_id(2)
    block = q_ref.shape[1]
    last = table[0, half]
    heads = range(GROUP)

    for j in heads:
        lanes = pl.ds(j * HEAD, HEAD)
        product = o_ref[0, :, lanes].astype(jnp.float32) * g_ref[0, :, lanes].astype(jnp.float32)
        delta[j] = jnp.sum(product.T, axis=0, keepdims=True)

    @pl.when(half == 0)
    def _():
        dk_acc[...] = jnp.zeros_like(dk_acc)
        dv_acc[...] = jnp.zeros_like(dv_acc)

    def part(slot, masked, first):
        rows = pl.ds(pl.multiple_of(slot % 2 * block, block), block)
        keys, values = k_ref[slot // 2, 0, rows, :], v_ref[slot // 2, 0, rows, :]
        lanes = [pl.ds(j * HEAD, HEAD) for j in heads]
        scores = [dot(keys, q_ref[0, :, lanes[j]], NT) for j in heads]
        d_probs = [dot(values, g_ref[0, :, lanes[j]], NT) for j in heads]
        probs = [
            jnp.exp2(scores[j] * (SCALE * LOG2E) - lse_ref[0, 0, 0, pl.ds(j, 1), :]) for j in heads
        ]
        if masked:
            key_at = lax.broadcasted_iota(jnp.int32, scores[0].shape, 0)
            query_at = lax.broadcasted_iota(jnp.int32, scores[0].shape, 1)
            probs = [jnp.where(key_at <= query_at, p, 0.0) for p in probs]
        d_scores = [(probs[j] * (d_probs[j] - delta[j])).astype(jnp.bfloat16) for j in heads]
        low = [p.astype(jnp.bfloat16) for p in probs]
        dv = sum(dot(low[j], g_ref[0, :, lanes[j]], NN) for j in heads)
        dk = sum(dot(d_scores[j], q_ref[0, :, lanes[j]], NN) for j in heads)
        dq = [dot(keys, d_scores[j], TN) for j in heads]
        for j in heads:
            if first:
                dq_acc[j] = dq[j]
            else:
                dq_acc[j] += dq[j]
        dk_acc[slot // 2, rows, :] += dk
        dv_acc[slot // 2, rows, :] += dv

    part(table[0, 2 + last], True, True)

    def step(b, carry):
        part(table[0, 2 + b], False, False)
        return carry

    lax.fori_loop(0, last, step, 0)
    for j in heads:
        grad = dq_acc[j].T * SCALE
        grad = grad * cos_ref[...] - pltpu.roll(grad, HEAD // 2, 1) * sin_ref[...]
        dq_ref[0, :, pl.ds(j * HEAD, HEAD)] = grad.astype(dq_ref.dtype)

    @pl.when(half == 1)
    def _():
        dkv_ref[:, 0, 0] = (dk_acc[...] * SCALE).astype(dkv_ref.dtype)
        dkv_ref[:, 0, 1] = dv_acc[...].astype(dkv_ref.dtype)


def attend_backward(table, queries, kv, grads, attended, lse, cosine, signed_sine, *first):
    seqs, rows, width = queries.shape
    block = rows // 2
    wide = GROUP * HEAD
    ranks = kv.shape[0]
    work = HEADS * rows * rows * ranks * seqs * 9 // 16
    rows_spec = pl.BlockSpec((1, block, wide), lambda s, g, h: (s, h, g))
    trig_spec = pl.BlockSpec((block, HEAD), lambda s, g, h: (2 * s + h, 0))
    return pl.pallas_call(
        with_tokens(backward_kernel, 9, len(first)),
        grid=(seqs, KV_HEADS, 2),
        in_specs=[
            pl.BlockSpec((1, table.shape[1]), lambda s, g, h: (s, 0), memory_space=pltpu.SMEM),
            rows_spec,
            pl.BlockSpec((ranks, 1, rows, HEAD), lambda s, g, h: (0, s, 0, g)),
            pl.BlockSpec((ranks, 1, rows, HEAD), lambda s, g, h: (0, s, 0, KV_HEADS + g)),
            rows_spec,
            rows_spec,
            pl.BlockSpec((1, 1, 1, GROUP, block), lambda s, g, h: (s, g, h, 0, 0)),
            trig_spec,
            trig_spec,
            *(pl.BlockSpec(memory_space=pl.ANY) for _ in first),
        ],
        out_specs=[
            rows_spec,
            pl.BlockSpec((ranks, 1, 2, rows, HEAD), lambda s, g, h: (0, s, 0, 0, g)),
        ],
        out_shape=[
            jax.ShapeDtypeStruct(queries.shape, jnp.bfloat16),
            jax.ShapeDtypeStruct((ranks, seqs, 2, rows, KV_HEADS * HEAD), jnp.bfloat16),
        ],
        scratch_shapes=[
            pltpu.VMEM((ranks, rows, HEAD), jnp.float32),
            pltpu.VMEM((ranks, rows, HEAD), jnp.float32),
            pltpu.VMEM((GROUP, HEAD, block), jnp.float32),
            pltpu.VMEM((GROUP, 1, block), jnp.float32),
        ],
        compiler_params=pltpu.CompilerParams(vmem_limit_bytes=40 * MIB),
        cost_estimate=cost(
            10 * HEAD * work, 12 * MIB, work
        ),
        name="attend_backward",
    )(table, queries, kv, kv, grads, attended, lse, cosine, signed_sine, *first)


def grad_kernel(count, *refs):
    kept, sent = refs[-2:]
    total = None
    for left, right in zip(refs[:count], refs[count : 2 * count]):
        term = dot(left[...], right[...], NN)
        total = term if total is None else total + term
    total = total.astype(kept.dtype)
    first = pl.program_id(0) < pl.num_programs(0) // 2

    @pl.when(first)
    def _():
        kept[...] = total

    @pl.when(jnp.logical_not(first))
    def _():
        sent[...] = total


def unit_grads(lefts, rights, *first):
    units = lefts[0].shape[0]
    rows, width = rights[0].shape
    count = len(lefts)
    block = units // 4
    half = jax.ShapeDtypeStruct((units // 2, width), jnp.bfloat16)
    return pl.pallas_call(
        with_tokens(functools.partial(grad_kernel, count), 2 * count, len(first)),
        grid=(4,),
        in_specs=[pl.BlockSpec((block, rows), lambda i: (i, 0)) for _ in lefts]
        + [pl.BlockSpec((rows, width), lambda i: (0, 0)) for _ in rights]
        + [pl.BlockSpec(memory_space=pl.ANY) for _ in first],
        out_specs=[
            pl.BlockSpec((block, width), lambda i: (jnp.minimum(i, 1), 0)),
            pl.BlockSpec((block, width), lambda i: (jnp.maximum(i - 2, 0), 0)),
        ],
        out_shape=[half, half],
        compiler_params=pltpu.CompilerParams(vmem_limit_bytes=56 * MIB),
        cost_estimate=cost(
            2 * count * units * rows * width,
            2 * count * rows * (units + width),
            0,
        ),
        name="unit_grads",
    )(*lefts, *rights, *first)


def back_kernel(count, *refs):
    out = refs[-1]
    total = None
    for left, right in zip(refs[:count], refs[count : 2 * count]):
        term = dot(left[...], right[...], TN)
        total = term if total is None else total + term
    out[...] = total.astype(out.dtype)


def back_rows(lefts, rights, *first):
    units, width = rights[0].shape
    rows = lefts[0].shape[1]
    count = len(lefts)
    block = width // 3
    return pl.pallas_call(
        with_tokens(functools.partial(back_kernel, count), 2 * count, len(first)),
        grid=(width // block,),
        in_specs=[pl.BlockSpec((units, rows), lambda i: (0, 0))] * count
        + [pl.BlockSpec((units, block), lambda i: (0, i))] * count
        + [pl.BlockSpec(memory_space=pl.ANY) for _ in first],
        out_specs=pl.BlockSpec((rows, block), lambda i: (0, i)),
        out_shape=jax.ShapeDtypeStruct((rows, width), jnp.bfloat16),
        compiler_params=pltpu.CompilerParams(vmem_limit_bytes=56 * MIB),
        cost_estimate=cost(2 * count * units * rows * width, 2 * count * units * (rows + width)),
        name="back_rows",
    )(*lefts, *rights, *first)


def hidden_kernel(rows, weight, out):
    out[...] = dot(weight[...], rows[...], NT).astype(out.dtype)


def hidden_rows(rows, weight):
    units, width = weight.shape
    count = rows.shape[0]
    block = units // 4
    return pl.pallas_call(
        hidden_kernel,
        grid=(4,),
        in_specs=[
            pl.BlockSpec((count, width), lambda i: (0, 0)),
            pl.BlockSpec((block, width), lambda i: (i, 0)),
        ],
        out_specs=pl.BlockSpec((block, count), lambda i: (i, 0)),
        out_shape=jax.ShapeDtypeStruct((units, count), jnp.bfloat16),
        compiler_params=pltpu.CompilerParams(vmem_limit_bytes=32 * MIB),
        cost_estimate=cost(2 * units * count * width, 2 * units * (count + width)),
        name="hidden_rows",
    )(rows, weight)


def project_kernel(rows_ref, gain, weight, bias, cosine, signed_sine, normed, queries, kv):
    step = pl.program_id(0)
    query_steps = pl.num_programs(0) - 2

    @pl.when(step == 0)
    def _():
        rows = rows_ref[...].astype(jnp.float32)
        scale = lax.rsqrt(jnp.mean(rows * rows, axis=-1, keepdims=True) + norm_eps)
        normed[...] = (rows * scale * gain[...]).astype(normed.dtype)

    out = dot(normed[...], weight[...], NT) + bias[...]

    def turned():
        parts = []
        for start in range(0, out.shape[1], HEAD):
            part = out[:, start : start + HEAD]
            parts.append(part * cosine[...] + pltpu.roll(part, HEAD // 2, 1) * signed_sine[...])
        return jnp.concatenate(parts, axis=1).astype(queries.dtype)

    @pl.when(step < query_steps)
    def _():
        queries[...] = turned()

    @pl.when(step == query_steps)
    def _():
        kv[...] = turned()

    @pl.when(step > query_steps)
    def _():
        kv[...] = out.astype(kv.dtype)


def project_heads(tokens, gain, weight, bias, cosine, signed_sine, *first):
    rows, width = tokens.shape
    block = KV_HEADS * HEAD
    steps = weight.shape[0] // block
    whole = pl.BlockSpec((rows, width), lambda i: (0, 0))
    table = pl.BlockSpec((rows, HEAD), lambda i: (0, 0))
    low = jnp.bfloat16
    return pl.pallas_call(
        with_tokens(project_kernel, 6, len(first)),
        grid=(steps,),
        in_specs=[
            whole,
            pl.BlockSpec((1, width), lambda i: (0, 0)),
            pl.BlockSpec((block, width), lambda i: (i, 0)),
            pl.BlockSpec((1, block), lambda i: (0, i)),
            table,
            table,
            *(pl.BlockSpec(memory_space=pl.ANY) for _ in first),
        ],
        out_specs=[
            whole,
            pl.BlockSpec((rows, block), lambda i: (0, jnp.minimum(i, steps - 3))),
            pl.BlockSpec((rows, block), lambda i: (0, jnp.maximum(i - steps + 2, 0))),
        ],
        out_shape=[
            jax.ShapeDtypeStruct((rows, width), low),
            jax.ShapeDtypeStruct((rows, (steps - 2) * block), low),
            jax.ShapeDtypeStruct((rows, 2 * block), low),
        ],
        compiler_params=pltpu.CompilerParams(vmem_limit_bytes=40 * MIB),
        cost_estimate=cost(
            2 * rows * width * weight.shape[0],
            2 * (weight.size + 4 * tokens.size),
            0,
        ),
        name="project_heads",
    )(tokens, gain, weight, bias, cosine, signed_sine, *first)


def unit_kernel(normed, d_hidden, gate, up, hidden, d_gate, d_up):
    gate_pre = dot(gate[...], normed[...], NT)
    up_pre = dot(up[...], normed[...], NT)
    d_mid = d_hidden[...].astype(jnp.float32)
    sig = 1.0 / (1.0 + jnp.exp(-gate_pre))
    silu = gate_pre * sig
    hidden[...] = (silu * up_pre).astype(hidden.dtype)
    d_up[...] = (d_mid * silu).astype(d_up.dtype)
    d_gate[...] = (d_mid * up_pre * (sig + silu * (1.0 - sig))).astype(d_gate.dtype)


def unit_rows(normed, d_hidden, gate, up):
    units, width = gate.shape
    rows = normed.shape[0]
    block = units // 4
    part = pl.BlockSpec((block, width), lambda i: (i, 0))
    out = pl.BlockSpec((block, rows), lambda i: (i, 0))
    shape = jax.ShapeDtypeStruct((units, rows), jnp.bfloat16)
    return pl.pallas_call(
        unit_kernel,
        grid=(4,),
        in_specs=[pl.BlockSpec((rows, width), lambda i: (0, 0)), out, part, part],
        out_specs=[out, out, out],
        out_shape=[shape, shape, shape],
        compiler_params=pltpu.CompilerParams(vmem_limit_bytes=48 * MIB),
        cost_estimate=cost(
            4 * units * rows * width, 4 * units * width + 8 * units * rows, 2 * units * rows
        ),
        name="unit_rows",
    )(normed, d_hidden, gate, up)


def rope_tables(positions):
    exponent = jnp.arange(0, HEAD, 2).astype(jnp.float32) / HEAD
    inverse = rope_base ** (-exponent)
    angles = positions.astype(jnp.float32)[:, None] * inverse[None, :]
    angles = jnp.concatenate([angles, angles], axis=1)
    return (jnp.cos(angles), jnp.sin(angles))


def rms_scale(values):
    return lax.rsqrt(jnp.mean(values * values, axis=-1, keepdims=True) + norm_eps)


def norm_back(d_normed, values, inv_scale, gain):
    scaled = d_normed * gain
    grad_gain = jnp.sum(d_normed * values * inv_scale, axis=0)
    inner = jnp.mean(scaled * values, axis=-1, keepdims=True)
    return (inv_scale * scaled - values * inv_scale * inv_scale * inv_scale * inner, grad_gain)


def project_rows(left, weight_rows):
    return jnp.einsum("rd,fd->rf", left, weight_rows, preferred_element_type=jnp.float32)


def flip(values, axis):
    return lax.ppermute(values, axis, [(0, 1), (1, 0)])


ALL_AXES = ("fa", "fb", "fc", "ch", "cl")
CTX_AXES = ("ch", "cl")


def over_a(values):
    if lax.axis_size("fa") == 2:
        return flip(values, "fa")
    return lax.all_gather(values, "fa", axis=0, tiled=True)


def join_a(own, other):
    return jnp.concatenate([own, other], axis=0) if lax.axis_size("fa") == 2 else other


def halves(values):
    half = values.shape[0] // 2
    return values[:half], values[half:]


def add_low(*terms):
    return functools.reduce(jnp.add, (t.astype(jnp.float32) for t in terms)).astype(jnp.bfloat16)


def add_core(kept, received):
    return [add_low(*pair) for pair in zip(halves(kept), halves(received))]


def over_a_sums(sums):
    if lax.axis_size("fa") == 2:
        return flip(sums[1], "fa")
    return lax.psum_scatter(jnp.concatenate(sums, axis=0), "fa", scatter_dimension=0, tiled=True)


def add_a(sums, received):
    return add_low(sums[0], received) if lax.axis_size("fa") == 2 else received


def core_kernel(core, left, right, kept, sent):
    total = dot(left[...], right[...], TN).astype(kept.dtype)

    @pl.when(pl.program_id(1) == 0)
    def _():
        kept[...] = total

    @pl.when(pl.program_id(1) == 1)
    def _():
        sent[...] = total


def core_terms(left, right, block, *first):
    rows, columns = left.shape
    width = right.shape[1]
    count = columns // block // 2
    me = lax.axis_index("fc")
    if block % 128:
        terms = dot(left, right, TN).astype(jnp.bfloat16).reshape(count, 2, block, width)
        pick = lambda k: lax.dynamic_index_in_dim(terms, k, 1, keepdims=False)
        return pick(me).reshape(-1, width), pick(1 - me).reshape(-1, width)
    out = pl.BlockSpec((block, width), lambda i, k, core: (i, 0))
    half = jax.ShapeDtypeStruct((count * block, width), jnp.bfloat16)
    return pl.pallas_call(
        with_tokens(core_kernel, 3, len(first)),
        grid_spec=pltpu.PrefetchScalarGridSpec(
            num_scalar_prefetch=1,
            grid=(count, 2),
            in_specs=[
                pl.BlockSpec((rows, block), lambda i, k, core: (0, 2 * i + (core[0] + k) % 2)),
                pl.BlockSpec((rows, width), lambda i, k, core: (0, 0)),
                *(pl.BlockSpec(memory_space=pl.ANY) for _ in first),
            ],
            out_specs=[out, out],
        ),
        out_shape=[half, half],
        compiler_params=pltpu.CompilerParams(vmem_limit_bytes=32 * MIB),
        cost_estimate=cost(2 * rows * columns * width, 2 * (rows + columns) * width),
        name="core_terms",
    )(me[None].astype(jnp.int32), left, right, *first)


def scatter_far(far):
    half = far.shape[0] // 2
    return flip(far[:half], "fb"), flip(far[half:], "cl")


def scatter_near(over_x, over_z, from_x, from_z):
    half = over_x.shape[0] // 2
    low, wide = jnp.bfloat16, jnp.float32
    over_x, over_z, from_x, from_z = (v.astype(wide) for v in (over_x, over_z, from_x, from_z))
    send_z = jnp.concatenate([over_z[:half] + from_x, over_z[half:]], axis=0)
    send_x = jnp.concatenate([over_x[:half], over_x[half:] + from_z], axis=0)
    return send_x.astype(low), send_z.astype(low)


def pack_vectors(vectors, blocks):
    flat = jnp.concatenate([v.reshape(blocks, -1) for v in vectors], axis=1)
    lanes = -(-flat.shape[1] // 1024) * 128
    flat = jnp.pad(flat, ((0, 0), (0, 8 * lanes - flat.shape[1])))
    return flat.reshape(blocks, 8, lanes)


def unpack_vectors(packed, sizes):
    flat = packed.reshape(packed.shape[0], -1)
    out = []
    start = 0
    for size in sizes:
        out.append(flat[:, start : start + size].reshape(-1))
        start += size
    return out


def xor_send(values, bits):
    count = lax.axis_size(CTX_AXES)
    return lax.ppermute(values, CTX_AXES, [(i, i ^ bits) for i in range(count)])


def stack_in_order(own, other, axis, dim):
    later = lax.axis_index(axis) == 1
    return jnp.stack([jnp.where(later, other, own), jnp.where(later, own, other)], axis=dim)


def stack_axis(values, axis, dim):
    if lax.axis_size(axis) == 2:
        return stack_in_order(values, flip(values, axis), axis, dim)
    return lax.all_gather(values, axis, axis=dim, tiled=False)


def order_ctx(*rel):
    high, low = lax.axis_index("ch") == 1, lax.axis_index("cl") == 1
    shape = rel[0].shape
    rel = [jnp.where(low, rel[k ^ 1], rel[k]) for k in range(4)]
    rel = [jnp.where(high, rel[k ^ 2], rel[k]) for k in range(4)]
    return jnp.stack(rel).reshape(2, 2, *shape)


def stack_plane_first(over_z):
    if lax.axis_size("fa") != 2:
        return stack_axis(over_z, "fb", 0), None
    return flip(over_z, "fa"), flip(over_z, "fb")


def stack_plane(over_z, by_a, by_b, far_top, far_bottom):
    far = jnp.concatenate([far_top, far_bottom], axis=2)
    near = stack_in_order(over_z, by_b, "fb", 0)
    beyond = stack_in_order(by_a, far, "fb", 0)
    return stack_in_order(near, beyond, "fa", 0)


def exchange(values, axes):
    return lax.all_to_all(values, axes, split_axis=0, concat_axis=0, tiled=True)


def nothing_kernel(*refs):
    pass


def gate(values, *first):
    anywhere = pl.BlockSpec(memory_space=pl.ANY)
    return pl.pallas_call(
        nothing_kernel,
        in_specs=[anywhere] * (1 + len(first)),
        out_specs=anywhere,
        out_shape=jax.ShapeDtypeStruct(values.shape, values.dtype),
        input_output_aliases={0: 0},
        cost_estimate=pl.CostEstimate(flops=0, bytes_accessed=0, transcendentals=0),
        name="gate",
    )(values, *first)


def copy_kernel(source, target):
    target[...] = source[...]


def gate_copy(values, *first):
    rows, width = values.shape
    block = rows // 2 if rows % 32 == 0 else rows
    spec = pl.BlockSpec((block, width), lambda i: (i, 0))
    return pl.pallas_call(
        with_tokens(copy_kernel, 1, len(first)),
        grid=(rows // block,),
        in_specs=[spec, *(pl.BlockSpec(memory_space=pl.ANY) for _ in first)],
        out_specs=spec,
        out_shape=jax.ShapeDtypeStruct(values.shape, values.dtype),
        cost_estimate=pl.CostEstimate(flops=0, bytes_accessed=0, transcendentals=0),
        name="gate_copy",
    )(values, *first)


def wait_kernel(source, target):
    target[...] = jnp.zeros_like(target)


def wait(first):
    return pl.pallas_call(
        wait_kernel,
        in_specs=[pl.BlockSpec(memory_space=pl.ANY)],
        out_shape=jax.ShapeDtypeStruct((8, 128), jnp.float32),
        cost_estimate=cost(10**10, 10**7),
        name="wait",
    )(first)


def on_device(
    tokens, stretch_pairs, cotangent, w_qkv, b_qkv, w_out, norm_attn, norm_mlp, w_gate, w_up, w_down
):
    ctx_count = lax.axis_size(CTX_AXES)
    device_count = lax.axis_size(ALL_AXES)
    device_grid = tuple(lax.axis_size(axis) for axis in ALL_AXES)
    ctx_rank = lax.axis_index(CTX_AXES)
    seq_count = stretch_pairs.shape[0]
    row_count, width = tokens.shape
    local_len = row_count // seq_count
    half_len = local_len // 2
    seq_len = local_len * ctx_count
    query_width = HEADS * HEAD
    kv_width = KV_HEADS * HEAD
    low, wide = jnp.bfloat16, jnp.float32

    half_rows = row_count // 2

    own_pair = lax.dynamic_slice_in_dim(stretch_pairs, ctx_rank, 1, axis=1)
    blocks = jnp.arange(2 * ctx_count)
    block_pair = jnp.minimum(blocks, 2 * ctx_count - 1 - blocks)
    holder = jnp.argmax(stretch_pairs[:, None, :] == block_pair[None, :, None], axis=2)
    slots = 2 * holder + (blocks >= ctx_count)[None, :]
    table = jnp.concatenate(
        [own_pair, 2 * ctx_count - 1 - own_pair, slots.astype(jnp.int32)], axis=1
    )
    offsets = jnp.arange(local_len)
    positions = jnp.where(
        offsets < half_len,
        own_pair * half_len + offsets,
        (2 * ctx_count - 1 - own_pair) * half_len + offsets - half_len,
    )
    cosine, sine_table = rope_tables(positions.reshape(row_count))
    signed_sine = jnp.where(jnp.arange(HEAD) < HEAD // 2, -sine_table, sine_table)

    vectors = pack_vectors([b_qkv, norm_attn, norm_mlp], 1)
    vectors_all = exchange(
        jnp.broadcast_to(vectors, (device_count, *vectors.shape[1:])), ALL_AXES
    )
    qkv_parts = [xor_send(w_qkv, k) for k in (1, 2, 3)]
    down_a = over_a(w_down)
    qkv_parts[0] = gate(qkv_parts[0], wait(w_qkv), down_a)
    qkv_z = order_ctx(w_qkv, *qkv_parts)
    by_a, by_b = stack_plane_first(qkv_z)
    own_down = gate_copy(w_down, qkv_z)
    down_z = flip(own_down, "ch")
    vectors_all = gate(vectors_all, qkv_z)
    cot_z = flip(gate_copy(cotangent, qkv_z), "cl")
    by_a = gate(by_a, wait(qkv_z))
    if by_b is None:
        qkv_plane = stack_axis(by_a, "fa", 0)
    else:
        far_top = flip(by_a[:, :, : by_a.shape[2] // 2], "fb")
        far_bottom = flip(by_b[:, :, by_b.shape[2] // 2 :], "fa")
        far_top = gate(far_top, wait(by_a))
        qkv_plane = stack_plane(qkv_z, by_a, by_b, far_top, far_bottom)
    out_all = lax.all_gather(gate_copy(w_out, qkv_plane), ALL_AXES, axis=0, tiled=True)
    cot_x = flip(gate_copy(cotangent, qkv_plane), "fb")
    own_gate = gate_copy(w_gate, qkv_plane)
    gate_a = over_a(own_gate)
    qkv_other = gate(flip(qkv_plane, "fc"), wait(qkv_plane))
    qkv_all = stack_in_order(qkv_plane, qkv_other, "fc", 2).reshape(-1, width)
    bias_all, gain_one, gain_two = unpack_vectors(
        vectors_all, (b_qkv.shape[0], norm_attn.shape[0], norm_mlp.shape[0])
    )
    gain_one, gain_two = gain_one.astype(wide)[None], gain_two.astype(wide)[None]

    normed_one, queries, kv_low = project_heads(
        tokens, gain_one, qkv_all, bias_all.astype(wide)[None], cosine, signed_sine
    )
    kv_low = kv_low.reshape(1, seq_count, local_len, 2 * kv_width)
    kv_sent = jnp.broadcast_to(kv_low, (ctx_count, *kv_low.shape[1:]))
    kv_all = exchange(kv_sent, CTX_AXES)
    cot_z, down_z = gate(cot_z, kv_sent), gate(down_z, kv_sent)
    cot_far = flip(cot_z, "fb")
    down_az = over_a(down_z)
    own_up = gate_copy(w_up, kv_sent)
    up_a = over_a(own_up)
    cot_parts = [cotangent, cot_x, cot_z, cot_far]

    gate_z = flip(gate_copy(w_gate, kv_all), "ch")
    queries = queries.reshape(seq_count, local_len, query_width)
    attended, log_totals = attend_forward(
        table, queries, kv_all, wait(kv_low), cot_x, cot_far, down_az, gate_a, up_a
    )
    attended_rows = attended.reshape(row_count, query_width)

    def middle_rows(rows, weight, inputs, gain):
        middle = inputs.astype(wide) + jnp.dot(rows, weight, preferred_element_type=wide)
        scale = rms_scale(middle)
        return (middle * scale * gain).astype(low), middle, scale

    normed_two, middle, inv_two = middle_rows(attended_rows, out_all, tokens, gain_two)

    def join_units(own, by_z, by_a, by_az):
        if lax.axis_size("fa") == 2:
            return jnp.concatenate([own, by_z, by_a, by_az], axis=0)
        blocks = [block.reshape(-1, *own.shape) for block in (by_a, by_az)]
        return jnp.concatenate(blocks, axis=1).reshape(-1, width)

    def join_core(own, other):
        return jnp.concatenate([own, other], axis=0)

    normed_x, normed_z = flip(normed_two, "fb"), flip(normed_two, "cl")
    up_z = flip(gate_copy(w_up, attended), "ch")
    down_own = join_units(own_down, down_z, down_a, gate(down_az, normed_two))
    down_part = join_core(down_own, gate(flip(down_own, "fc"), wait(down_own)))
    d_hidden = [hidden_rows(cot, down_part) for cot in cot_parts]
    gate_z = gate(gate_z, d_hidden[0])
    gate_az = over_a(gate_z)
    normed_x, normed_z = gate(normed_x, *d_hidden), gate(normed_z, *d_hidden)
    far_top, far_bottom = flip(normed_z[:half_rows], "fb"), flip(normed_x[half_rows:], "cl")
    gate_own = join_units(own_gate, gate_z, gate_a, gate(gate_az, *d_hidden))
    up_z = gate(up_z, gate_own)
    up_az = over_a(up_z)
    gate_part = join_core(gate_own, gate(flip(gate_own, "fc"), wait(gate_own)))
    normed_far = join_core(gate(far_top, gate_part), far_bottom)
    up_own = join_units(own_up, up_z, up_a, gate(up_az, gate_part))
    up_part = join_core(up_own, gate(flip(up_own, "fc"), wait(up_own)))
    normed_parts = [normed_two, normed_x, normed_z, normed_far]
    hidden, d_gate, d_up = zip(
        *(unit_rows(n, d, gate_part, up_part) for n, d in zip(normed_parts, d_hidden))
    )

    def back_units(k, *first):
        return back_rows((d_gate[k], d_up[k]), (gate_part, up_part), *first)

    def branch_rows(k, *first):
        return back_rows((hidden[k],), (down_part,), *first)

    back_far = back_units(3)
    back_from = scatter_far(back_far)
    back_x = back_units(1, back_far)
    back_z = back_units(2, back_x)
    back_sent = scatter_near(back_x, back_z, gate(back_from[0], back_z), back_from[1])
    back_x, back_z = flip(back_sent[0], "fb"), flip(back_sent[1], "cl")
    down_kept, down_sent = unit_grads(hidden, cot_parts, *back_sent)
    down_sent = flip(down_sent, "fc")
    back_own = back_units(0, down_kept)
    down_sums = add_core(down_kept, gate(down_sent, back_own))
    down_from_a = over_a_sums(down_sums)

    def back_norm(own, by_x, by_z, middle, scale, gain, cotangent):
        d_normed = own.astype(wide) + by_x.astype(wide) + by_z.astype(wide)
        d_rows, grad_gain = norm_back(d_normed, middle, scale, gain)
        d_middle = cotangent.astype(wide) + d_rows
        return d_middle.astype(low), d_middle, grad_gain

    d_branch, d_middle, grad_gain_two = back_norm(back_own, back_x, back_z, middle, inv_two, gain_two, cotangent
    )
    d_attended = project_rows(d_branch, out_all).astype(low)
    d_queries, d_kv_parts = attend_backward(
        table,
        queries,
        kv_all,
        d_attended.reshape(seq_count, local_len, query_width),
        attended,
        log_totals,
        cosine,
        signed_sine,
        *down_sums,
    )
    d_queries = d_queries.reshape(row_count, query_width)
    d_kv_parts = exchange(d_kv_parts, CTX_AXES)

    def add_three(own, by_x, by_z, middle):
        return (middle + own.astype(wide) + by_x.astype(wide) + by_z.astype(wide)).astype(low)

    def add_wide(own, other):
        return own.astype(wide) + other.astype(wide)

    def split_terms(left, right, *first):
        return core_terms(left, right, ctx_count * w_qkv.shape[0], *first)

    gate_kept, gate_sent = unit_grads(d_gate, normed_parts, d_queries)
    gate_sent = flip(gate_sent, "fc")
    down_sums = add_a(down_sums, gate(down_from_a, gate_kept))
    down_z_sums = flip(halves(down_sums)[1], "ch")
    grad_out = lax.psum_scatter(
        back_rows((attended_rows,), (d_branch,), gate_kept),
        ALL_AXES,
        scatter_dimension=0,
        tiled=True,
    ).astype(wide)
    query_kept, query_sent = split_terms(d_queries, normed_one, down_sums)
    query_sent = flip(query_sent, "fc")
    up_kept, up_sent = unit_grads(d_up, normed_parts, query_kept)
    up_sent = flip(up_sent, "fc")
    query_sums = add_low(query_kept, gate(query_sent, up_kept))
    gate_sums = add_core(gate_kept, gate(gate_sent, up_kept))
    gate_from_a = over_a_sums(gate_sums)
    branch_far = branch_rows(3, query_sums, *gate_sums)
    branch_from = flip(branch_far, "fb")
    up_sums = add_core(up_kept, gate(up_sent, branch_far))
    up_from_a = over_a_sums(up_sums)
    branch_x = branch_rows(1, *up_sums)
    branch_z = branch_rows(2, branch_x)
    branch_x = flip(branch_x, "fb")
    branch_z = add_low(branch_z, gate(branch_from, branch_z))
    gate_sums = add_a(gate_sums, gate(gate_from_a, branch_z))
    gate_z_sums = flip(halves(gate_sums)[1], "ch")
    d_kv_parts = gate(d_kv_parts, gate_sums)
    branch_z = flip(branch_z, "cl")
    query_bias_local = jnp.sum(d_queries, axis=0, dtype=wide)

    def turn_back(parts):
        d_kv = jnp.sum(parts, axis=0, dtype=wide)
        d_keys, d_values = (d_kv[:, k].reshape(row_count, kv_width) for k in (0, 1))
        turned = []
        for start in range(0, kv_width, HEAD):
            part = d_keys[:, start : start + HEAD]
            turned.append(part * cosine - jnp.roll(part, HEAD // 2, 1) * signed_sine)
        return jnp.concatenate([*turned, d_values], axis=1).astype(low)

    d_kv = turn_back(d_kv_parts)
    kv_kept, kv_sent = split_terms(d_kv, normed_one)
    kv_sent = gate(flip(kv_sent, "fc"), wait(kv_kept))
    kv_bias_local = jnp.sum(d_kv, axis=0, dtype=wide)

    def back_projection(d_queries, d_kv, weight):
        return dot(d_queries, weight[:query_width], NN) + dot(d_kv, weight[query_width:], NN)

    def back_tokens(d_normed, tokens, gain, d_middle):
        inputs = tokens.astype(wide)
        d_rows, grad_gain = norm_back(d_normed, inputs, rms_scale(inputs), gain)
        return d_middle + d_rows, grad_gain

    def join_qkv(query_sums, kept, sent):
        sums = jnp.concatenate([query_sums, add_wide(kept, sent).astype(low)], axis=0)
        return sums.reshape(-1, ctx_count, *w_qkv.shape)

    def add_all(values):
        return jnp.sum(values, axis=0, dtype=wide)

    d_normed_one = back_projection(d_queries, d_kv, qkv_all)
    grad_tokens, grad_gain_one = back_tokens(d_normed_one, tokens, gain_one, d_middle)
    vector_grads = [query_bias_local, kv_bias_local, grad_gain_one, grad_gain_two]
    qkv_terms = join_qkv(query_sums, kv_kept, gate(kv_sent, grad_tokens))
    qkv_sums = exchange(qkv_terms, ("fa", "fb"))
    up_sums = add_a(up_sums, gate(up_from_a, qkv_terms))
    up_z_sums = flip(halves(up_sums)[1], "ch")
    grad_down = add_wide(halves(down_sums)[0], gate(down_z_sums, up_sums))
    branch_own = branch_rows(0, grad_down)
    layer_out = add_three(branch_own, gate(branch_x, branch_own), branch_z, middle)
    qkv_sums = add_all(gate(qkv_sums, layer_out)).astype(low)

    def pick(rank):
        return lax.dynamic_index_in_dim(qkv_sums, rank, 0, keepdims=False)

    qkv_own = pick(ctx_rank)
    qkv_from = [xor_send(pick(ctx_rank ^ k), k) for k in (1, 2, 3)]
    packed = gate(pack_vectors(vector_grads, device_count), qkv_own)
    vector_shares = exchange(packed, ALL_AXES)
    qkv_from[0] = gate(qkv_from[0], wait(qkv_own), vector_shares)


    grad_gate = add_wide(halves(gate_sums)[0], gate_z_sums)
    grad_qkv = functools.reduce(jnp.add, (part.astype(wide) for part in (qkv_own, *qkv_from)))
    grad_up = add_wide(halves(up_sums)[0], up_z_sums)
    grad_query_bias, grad_kv_bias, grad_norm_attn, grad_norm_mlp = unpack_vectors(
        jnp.sum(vector_shares, axis=0)[None], [v.shape[0] // device_count for v in vector_grads]
    )
    return (
        layer_out,
        grad_tokens,
        grad_qkv,
        grad_query_bias,
        grad_kv_bias,
        grad_out,
        grad_norm_attn,
        grad_norm_mlp,
        grad_gate,
        grad_up,
        grad_down,
    )


def solution(mesh):
    fsdp_count, ctx_count = mesh.shape["fsdp"], mesh.shape["ctx"]
    parts = (fsdp_count // 4, 2, 2, ctx_count // 2, 2)
    split_mesh = Mesh(mesh.devices.reshape(parts), ALL_AXES)
    rows, whole = P(ALL_AXES, None), P(ALL_AXES)
    return jax.shard_map(
        on_device,
        mesh=split_mesh,
        in_specs=(
            rows,
            P(("fa", "fb", "fc"), None),
            rows,
            rows,
            whole,
            rows,
            whole,
            whole,
            rows,
            rows,
            rows,
        ),
        out_specs=(rows, rows, rows, whole, whole, rows, whole, whole, rows, rows, rows),
        check_vma=False,
    )
```

time: 928 us -> 821 us (0.88)
  waiting for transfers between devices: 375 us -> 149 us
  Pallas kernels: 162 us -> 306 us
  matrix products: 139 us -> 20.8 us
  other arithmetic: 64.4 us -> 104 us
  local copies, waits for them, and re-layouts: 83 us -> 110 us
  starting transfers between devices: 92.3 us -> 109 us
  between operations: 3.2 us -> 16.6 us
    ppermute x82 -> x42, waiting for transfers between devices: 299 us -> 85.6 us  [flip(): return lax.ppermute(values, axis, [(0, 1), (1, 0)])]
    pallas_call x10 -> x78, Pallas kernels: 162 us -> 306 us  [the longest x9 88.4 us: back_rows(): pl.pallas_call(with_tokens(functools.partial(back_kernel, count), 2 * cou...]
    dot_general x21 -> x2, matrix products: 129 us -> 10.6 us  [dot(): lax.dot_general(left, right, dims, preferred_element_type=jnp.float32)]
    ppermute x15 -> x6, waiting for transfers between devices: 76.5 us -> 8.36 us  [xor_send(): return lax.ppermute(values, CTX_AXES, [(i, i ^ bits) for i in range(count)])]
    all_to_all x0 -> x5, waiting for transfers between devices: none -> 55 us  [exchange(): return lax.all_to_all(values, axes, split_axis=0, concat_axis=0, tiled=True)]
    all_to_all x0 -> x5, starting transfers between devices: none -> 42 us  [exchange(): return lax.all_to_all(values, axes, split_axis=0, concat_axis=0, tiled=True)]
    unnamed x247 -> x198, local copies, waits for them, and re-layouts: 46 us -> 75.7 us
    convert_element_type x15 -> x13, other arithmetic: 25.9 us -> 43.9 us  [the longest x8 28.2 us: add_low(): functools.reduce(jnp.add, (t.astype(jnp.float32) for t in terms))]
  transfers between devices with their start and end apart: 97 -> 55, of which waited for: 32 -> 17; matrix products, arithmetic and copies ran while one was open for 26% -> 20% of each run, Pallas kernels for 16% -> 30%
where the time goes in v2:
time: 821 us; the launch traced here: 815 us
  Pallas kernels  306 us (37%)
  waiting for transfers between devices  149 us (18%)
  local copies, waits for them, and re-layouts  110 us (13%)
  starting transfers between devices  109 us (13%)
  other arithmetic  104 us (13%)
  matrix products  20.8 us (3%)
  between operations  16.6 us (2%)
    pallas_call x9, Pallas kernels, back_rows(): pl.pallas_call(with_tokens(functools.partial(back_kernel, count), 2 * cou...  88.4 us
    ppermute x42, waiting for transfers between devices, flip(): return lax.ppermute(values, axis, [(0, 1), (1, 0)])  85.6 us
    unnamed x198, local copies, waits for them, and re-layouts  75.7 us
    pallas_call x3, Pallas kernels, unit_grads(): pl.pallas_call(with_tokens(functools.partial(grad_kernel, count), 2 * cou...  64.3 us
    ppermute x42, starting transfers between devices, flip(): return lax.ppermute(values, axis, [(0, 1), (1, 0)])  57 us
    all_to_all x5, waiting for transfers between devices, exchange(): return lax.all_to_all(values, axes, split_axis=0, concat_axis=0, tiled=True)  55 us
    pallas_call x4, Pallas kernels, unit_rows(): pl.pallas_call(unit_kernel, grid=(4,), in_specs=[pl.BlockSpec((rows, widt...  49.2 us
    all_to_all x5, starting transfers between devices, exchange(): return lax.all_to_all(values, axes, split_axis=0, concat_axis=0, tiled=True)  42 us
  transfers between devices with their start and end apart: 55, of which 17 were waited for; matrix products, arithmetic and copies ran while one was open for 20% of the time, Pallas kernels for 30%

profile of v2, /device:TPU:0, one launch (start us, length us, event | category | flops | bytes accessed | tf_op | source)
XLA Modules:
  0.0 815.2 jit_solution(1273788741748103514)
XLA Ops:
  114.4 51.8 %all-to-all-done.1.refs_2_.refs_3_.refs_1_ = bf16[4,1,512,512]{3,2,1,0:T(8,128)(2,1)} async-done(((bf16[4,1,512,512]{3,2,1,0:T(8,128)(2,1)}), bf16[4,1,512,512]{3,2,1,0:T(8,128)(2,1)}, u32[]{:S(2)}, u32[]{:S(2)}) %all-to-all-start.1) | async-done | bytes 2097184 | tf_op jit(solution)/shard_map/all_to_all | solution.py:608
  169.8 17.2 %attend_forward.1 = (bf16[1,512,1536]{2,1,0:T(8,128)(2,1)S(1)}, f32[1,2,2,6,256]{4,3,2,1,0:T(8,128)S(1)}) custom-call(s32[1,10]{1,0:T(1,128)S(1)} %pad_add_fusion.refs_0_, bf16[1,512,1536]{2,1,0:T(8,128)(2,1)S(1)} %bitcast.84, bf16[4,1,512,512]{3,2,1,0:T(8,128)(2,1)} %all-to-all-done.1.refs_2_.refs_3_.refs_1_, ...), custom_call_target="tpu_custom_call" | custom-call | flops 57982058496 | bytes 100663296 | tf_op jit(solution)/shard_map/attend_forward/pallas_call | solution.py:98
  230.9 17.5 %collective-permute-start.18 = (bf16[280,1536]{1,0:T(8,128)(2,1)}, bf16[280,1536]{1,0:T(8,128)(2,1)}, u32[]{:S(2)}, u32[]{:S(2)}) collective-permute-start(bf16[280,1536]{1,0:T(8,128)(2,1)} %gate.44), channel_id=1, source_target_pairs={{0,16},{16,0},{1,17},{17,1},{2,18},{18,2},{3,19},{19,3},{4,20},{20... | collective-permute-start | bytes 2580488 | tf_op jit(solution)/shard_map/ppermute | solution.py:457
  265.7 9.7 %collective-permute-done.24.refs_0_ = bf16[512,1536]{1,0:T(8,128)(2,1)} collective-permute-done((bf16[512,1536]{1,0:T(8,128)(2,1)}, bf16[512,1536]{1,0:T(8,128)(2,1)}, u32[]{:S(2)}, u32[]{:S(2)}) %collective-permute-start.24) | collective-permute-done | bytes 1572896 | tf_op jit(solution)/shard_map/ppermute | solution.py:457
  302.9 9.8 %collective-permute-done.21.refs_0_ = bf16[280,1536]{1,0:T(8,128)(2,1)} collective-permute-done((bf16[280,1536]{1,0:T(8,128)(2,1)}, bf16[280,1536]{1,0:T(8,128)(2,1)}, u32[]{:S(2)}, u32[]{:S(2)}) %collective-permute-start.21) | collective-permute-done | bytes 860192 | tf_op jit(solution)/shard_map/ppermute | solution.py:457
  326.3 12.3 %unit_rows.4 = (bf16[2240,512]{1,0:T(8,128)(2,1)S(1)}, bf16[2240,512]{1,0:T(8,128)(2,1)S(1)}, bf16[2240,512]{1,0:T(8,128)(2,1)}) custom-call(bf16[512,1536]{1,0:T(8,128)(2,1)} %multiply_convert_fusion.refs_1_.normed.refs_4_, bf16[2240,512]{1,0:T(8,128)(2,1)} %copy-done, bf16[2240,1536]{1,0:T(8,128)(2,1)} %constant_dynamic-update-slice_fusion.5.refs_1_.gate.refs_2_, ...), custom_call_target="tpu_custom_call" | custom-call | flops 112742891520 | bytes 367001600 | tf_op jit(solution)/shard_map/unit_rows/pallas_call | solution.py:419
  341.4 12.7 %unit_rows.5 = (bf16[2240,512]{1,0:T(8,128)(2,1)S(1)}, bf16[2240,512]{1,0:T(8,128)(2,1)S(1)}, bf16[2240,512]{1,0:T(8,128)(2,1)}) custom-call(bf16[512,1536]{1,0:T(8,128)(2,1)} %gate.50.normed.refs_5_, bf16[2240,512]{1,0:T(8,128)(2,1)} %copy-done.3, bf16[2240,1536]{1,0:T(8,128)(2,1)} %constant_dynamic-update-slice_fusion.5.refs_1_.gate.refs_2_, ...), custom_call_target="tpu_custom_call" | custom-call | flops 112742891520 | bytes 367001600 | tf_op jit(solution)/shard_map/unit_rows/pallas_call | solution.py:419
  356.9 12.3 %unit_rows.6 = (bf16[2240,512]{1,0:T(8,128)(2,1)S(1)}, bf16[2240,512]{1,0:T(8,128)(2,1)S(1)}, bf16[2240,512]{1,0:T(8,128)(2,1)}) custom-call(bf16[512,1536]{1,0:T(8,128)(2,1)} %gate.51.normed.refs_6_, bf16[2240,512]{1,0:T(8,128)(2,1)} %copy-done.1, bf16[2240,1536]{1,0:T(8,128)(2,1)} %constant_dynamic-update-slice_fusion.5.refs_1_.gate.refs_2_, ...), custom_call_target="tpu_custom_call" | custom-call | flops 112742891520 | bytes 367001600 | tf_op jit(solution)/shard_map/unit_rows/pallas_call | solution.py:419
  372.0 11.9 %unit_rows.7 = (bf16[2240,512]{1,0:T(8,128)(2,1)S(1)}, bf16[2240,512]{1,0:T(8,128)(2,1)S(1)}, bf16[2240,512]{1,0:T(8,128)(2,1)}) custom-call(bf16[512,1536]{1,0:T(8,128)(2,1)S(1)} %pad_maximum_fusion.8.normed.refs_7_, bf16[2240,512]{1,0:T(8,128)(2,1)} %copy-done.2, bf16[2240,1536]{1,0:T(8,128)(2,1)} %constant_dynamic-update-slice_fusion.5.refs_1_.gate.refs_2_, ...), custom_call_target="tpu_custom_call" | custom-call | flops 112742891520 | bytes 367001600 | tf_op jit(solution)/shard_map/unit_rows/pallas_call | solution.py:419
  386.7 12.5 %back_rows.9.refs_4_ = bf16[512,1536]{1,0:T(8,128)(2,1)} custom-call(bf16[2240,512]{1,0:T(8,128)(2,1)} %copy-done.49, bf16[2240,512]{1,0:T(8,128)(2,1)} %get-tuple-element.52.refs_1_.refs_3_, bf16[2240,1536]{1,0:T(8,128)(2,1)} %constant_dynamic-update-slice_fusion.5.refs_1_.gate.refs_2_, bf16[2240,1536]{1,0:T(8,128)(2,1)} %constant_dynamic-update-slice_fusion.10.up.refs_3_), custom_call_target="tpu_custom_call" | custom-call | flops 112742891520 | bytes 293601280 | tf_op jit(solution)/shard_map/back_rows/pallas_call | solution.py:293
  404.3 12.5 %back_rows.10.refs_4_ = bf16[512,1536]{1,0:T(8,128)(2,1)} custom-call(bf16[2240,512]{1,0:T(8,128)(2,1)} %copy-done.47, bf16[2240,512]{1,0:T(8,128)(2,1)} %get-tuple-element.50.refs_1_, bf16[2240,1536]{1,0:T(8,128)(2,1)} %constant_dynamic-update-slice_fusion.5.refs_1_.gate.refs_2_, bf16[2240,1536]{1,0:T(8,128)(2,1)} %constant_dynamic-update-slice_fusion.10.up.refs_3_, ...), custom_call_target="tpu_custom_call" | custom-call | flops 112742891520 | bytes 293601280 | tf_op jit(solution)/shard_map/back_rows/pallas_call | solution.py:293
  416.8 12.5 %back_rows.11.refs_1_ = bf16[512,1536]{1,0:T(8,128)(2,1)} custom-call(bf16[2240,512]{1,0:T(8,128)(2,1)} %copy-done.48, bf16[2240,512]{1,0:T(8,128)(2,1)} %get-tuple-element.54.refs_1_.refs_2_, bf16[2240,1536]{1,0:T(8,128)(2,1)} %constant_dynamic-update-slice_fusion.5.refs_1_.gate.refs_2_, bf16[2240,1536]{1,0:T(8,128)(2,1)} %constant_dynamic-update-slice_fusion.10.up.refs_3_, ...), custom_call_target="tpu_custom_call" | custom-call | flops 112742891520 | bytes 293601280 | tf_op jit(solution)/shard_map/back_rows/pallas_call | solution.py:293
  437.8 21.5 %unit_grads.3 = (bf16[1120,1536]{1,0:T(8,128)(2,1)}, bf16[1120,1536]{1,0:T(8,128)(2,1)}) custom-call(bf16[2240,512]{1,0:T(8,128)(2,1)} %copy-done.44, bf16[2240,512]{1,0:T(8,128)(2,1)} %copy-done.43, bf16[2240,512]{1,0:T(8,128)(2,1)} %copy-done.45, bf16[2240,512]{1,0:T(8,128)(2,1)} %copy-done.42, bf16[512,1536]{1,0:T(8,128)(2,1)} %refs_4_.1, ...), custom_call_target="tpu_custom_call" | custom-call | flops 225485783040 | bytes 247463936 | tf_op jit(solution)/shard_map/unit_grads/pallas_call | solution.py:258
  459.3 12.7 %back_rows.12.refs_1_ = bf16[512,1536]{1,0:T(8,128)(2,1)} custom-call(bf16[2240,512]{1,0:T(8,128)(2,1)} %copy-done.46, bf16[2240,512]{1,0:T(8,128)(2,1)} %get-tuple-element.58.refs_1_.refs_0_, bf16[2240,1536]{1,0:T(8,128)(2,1)} %constant_dynamic-update-slice_fusion.5.refs_1_.gate.refs_2_, bf16[2240,1536]{1,0:T(8,128)(2,1)} %constant_dynamic-update-slice_fusion.10.up.refs_3_, ...), custom_call_target="tpu_custom_call" | custom-call | flops 112742891520 | bytes 293601280 | tf_op jit(solution)/shard_map/back_rows/pallas_call | solution.py:293
  497.2 27.3 %attend_backward.1 = (bf16[1,512,1536]{2,1,0:T(8,128)(2,1)S(1)}, bf16[4,1,2,512,256]{4,3,2,1,0:T(8,128)(2,1)}) custom-call(s32[1,10]{1,0:T(1,128)S(1)} %copy-done.35, bf16[1,512,1536]{2,1,0:T(8,128)(2,1)S(1)} %bitcast.85, bf16[4,1,512,512]{3,2,1,0:T(8,128)(2,1)} %all-to-all-done.1.refs_2_.refs_3_.refs_1_, ...), custom_call_target="tpu_custom_call" | custom-call | flops 144955146240 | bytes 201326592 | tf_op jit(solution)/shard_map/attend_backward/pallas_call | solution.py:197
  525.7 21.2 %unit_grads.4 = (bf16[1120,1536]{1,0:T(8,128)(2,1)}, bf16[1120,1536]{1,0:T(8,128)(2,1)}) custom-call(bf16[2240,512]{1,0:T(8,128)(2,1)} %copy-done.46, bf16[2240,512]{1,0:T(8,128)(2,1)} %copy-done.47, bf16[2240,512]{1,0:T(8,128)(2,1)} %copy-done.48, bf16[2240,512]{1,0:T(8,128)(2,1)} %copy-done.49, ...), custom_call_target="tpu_custom_call" | custom-call | flops 225485783040 | bytes 247463936 | tf_op jit(solution)/shard_map/unit_grads/pallas_call | solution.py:258
  578.0 21.6 %unit_grads.5 = (bf16[1120,1536]{1,0:T(8,128)(2,1)}, bf16[1120,1536]{1,0:T(8,128)(2,1)}) custom-call(bf16[2240,512]{1,0:T(8,128)(2,1)} %get-tuple-element.58.refs_1_.refs_0_, bf16[2240,512]{1,0:T(8,128)(2,1)} %get-tuple-element.50.refs_1_, bf16[2240,512]{1,0:T(8,128)(2,1)} %get-tuple-element.54.refs_1_.refs_2_, ...), custom_call_target="tpu_custom_call" | custom-call | flops 225485783040 | bytes 247463936 | tf_op jit(solution)/shard_map/unit_grads/pallas_call | solution.py:258
  638.5 8.1 back_rows.15.refs_1_
  647.4 15.6 %collective-permute-done.39.refs_0_ = bf16[512,1536]{1,0:T(8,128)(2,1)} collective-permute-done((bf16[512,1536]{1,0:T(8,128)(2,1)}, bf16[512,1536]{1,0:T(8,128)(2,1)}, u32[]{:S(2)}, u32[]{:S(2)}) %collective-permute-start.39) | collective-permute-done | bytes 1572896 | tf_op jit(solution)/shard_map/ppermute | solution.py:457
  696.0 17.4 %all-to-all-start.3 = ((bf16[4,4,64,1536]{3,2,1,0:T(8,128)(2,1)}), bf16[4,4,64,1536]{3,2,1,0:T(8,128)(2,1)}, u32[]{:S(2)}, u32[]{:S(2)}) async-start(bf16[4,4,64,1536]{3,2,1,0:T(8,128)(2,1)} %bitcast.27.refs_1_), calls=%async_computation.3 | async-start | bytes 6291456 | tf_op jit(solution)/shard_map/all_to_all | solution.py:608
  713.4 8.7 %collective-permute-done.46 = bf16[280,1536]{1,0:T(8,128)(2,1)} collective-permute-done((bf16[280,1536]{1,0:T(8,128)(2,1)}, bf16[280,1536]{1,0:T(8,128)(2,1)}, u32[]{:S(2)}, u32[]{:S(2)}) %collective-permute-start.46) | collective-permute-done | bytes 860192 | tf_op jit(solution)/shard_map/ppermute | solution.py:457
  740.9 9.9 %collective-permute-done.42 = bf16[512,1536]{1,0:T(8,128)(2,1)} collective-permute-done((bf16[512,1536]{1,0:T(8,128)(2,1)}, bf16[512,1536]{1,0:T(8,128)(2,1)}, u32[]{:S(2)}, u32[]{:S(2)}) %collective-permute-start.42) | collective-permute-done | bytes 1572896 | tf_op jit(solution)/shard_map/ppermute | solution.py:457
  755.1 14.4 %collective-permute-done.47 = bf16[280,1536]{1,0:T(8,128)(2,1)} collective-permute-done((bf16[280,1536]{1,0:T(8,128)(2,1)}, bf16[280,1536]{1,0:T(8,128)(2,1)}, u32[]{:S(2)}, u32[]{:S(2)}) %collective-permute-start.47) | collective-permute-done | bytes 860192 | tf_op jit(solution)/shard_map/ppermute | solution.py:457
  775.5 11.2 %all-to-all-start.4 = ((f32[32,8,128]{2,1,0:T(8,128)}), f32[32,8,128]{2,1,0:T(8,128)}, u32[]{:S(2)}, u32[]{:S(2)}) async-start(f32[32,8,128]{2,1,0:T(8,128)} %gate.68), calls=%async_computation.4 | async-start | bytes 262144 | tf_op jit(solution)/shard_map/all_to_all | solution.py:608
  (461 shorter events, 416.6 us)
Async XLA Ops:
  20.2 173.2 %all-gather.2.cloned.1.call-start = ((), (), s32[]{:S(2)}) async-start(), calls=%async_computation.6 | async-start | bytes 4866048 | tf_op jit(solution)/shard_map/all_gather | solution.py:717
  46.2 56.0 %collective-permute-start.10 = (bf16[512,1536]{1,0:T(8,128)(2,1)}, bf16[512,1536]{1,0:T(8,128)(2,1)}, u32[]{:S(2)}, u32[]{:S(2)}) collective-permute-start(bf16[512,1536]{1,0:T(8,128)(2,1)} %gate_copy.9), channel_id=1, source_target_pairs={{0,1},{1,0},{2,3},{3,2},{4,5},{5,4},{6,7},{7,6},{8,9},{9,8},{10,11... | collective-permute-start | bytes 4718600 | tf_op jit(solution)/shard_map/ppermute | solution.py:457
  47.7 56.1 %collective-permute-start.12 = (bf16[280,1536]{1,0:T(8,128)(2,1)}, bf16[280,1536]{1,0:T(8,128)(2,1)}, u32[]{:S(2)}, u32[]{:S(2)}) collective-permute-start(bf16[280,1536]{1,0:T(8,128)(2,1)} %gate_copy.10), channel_id=1, source_target_pairs={{0,2},{2,0},{1,3},{3,1},{4,6},{6,4},{5,7},{7,5},{8,10},{10,8},{9,1... | collective-permute-start | bytes 2580488 | tf_op jit(solution)/shard_map/ppermute | solution.py:457
  75.2 93.1 %collective-permute-start.9 = (bf16[512,1536]{1,0:T(8,128)(2,1)}, bf16[512,1536]{1,0:T(8,128)(2,1)}, u32[]{:S(2)}, u32[]{:S(2)}) collective-permute-start(bf16[512,1536]{1,0:T(8,128)(2,1)} %gate_copy.8), channel_id=1, source_target_pairs={{0,8},{8,0},{1,9},{9,1},{2,10},{10,2},{3,11},{11,3},{4,12},{12,4},... | collective-permute-start | bytes 4718600 | tf_op jit(solution)/shard_map/ppermute | solution.py:457
  77.8 90.5 %collective-permute-start.14 = (bf16[280,1536]{1,0:T(8,128)(2,1)}, bf16[280,1536]{1,0:T(8,128)(2,1)}, u32[]{:S(2)}, u32[]{:S(2)}) collective-permute-start(bf16[280,1536]{1,0:T(8,128)(2,1)} %gate_copy.11), channel_id=1, source_target_pairs={{0,16},{16,0},{1,17},{17,1},{2,18},{18,2},{3,19},{19,3},{4,20},{20... | collective-permute-start | bytes 2580488 | tf_op jit(solution)/shard_map/ppermute | solution.py:457
  97.6 68.6 %all-to-all-start.1 = ((bf16[4,1,512,512]{3,2,1,0:T(8,128)(2,1)}), bf16[4,1,512,512]{3,2,1,0:T(8,128)(2,1)}, u32[]{:S(2)}, u32[]{:S(2)}) async-start(bf16[4,1,512,512]{3,2,1,0:T(8,128)(2,1)} %broadcast_in_dim.17.refs_1_), calls=%async_computation.1 | async-start | bytes 4194304 | tf_op jit(solution)/shard_map/all_to_all | solution.py:608
  102.2 66.1 %collective-permute-start.11 = (bf16[512,1536]{1,0:T(8,128)(2,1)}, bf16[512,1536]{1,0:T(8,128)(2,1)}, u32[]{:S(2)}, u32[]{:S(2)}) collective-permute-start(bf16[512,1536]{1,0:T(8,128)(2,1)} %gate.40.rows.refs_6_), channel_id=1, source_target_pairs={{0,8},{8,0},{1,9},{9,1},{2,10},{10,2},{3,11},{11,3},{4,12},{12,4},... | collective-permute-start | bytes 4718600 | tf_op jit(solution)/shard_map/ppermute | solution.py:457
  103.9 64.5 %collective-permute-start.13 = (bf16[280,1536]{1,0:T(8,128)(2,1)}, bf16[280,1536]{1,0:T(8,128)(2,1)}, u32[]{:S(2)}, u32[]{:S(2)}) collective-permute-start(bf16[280,1536]{1,0:T(8,128)(2,1)} %gate.41), channel_id=1, source_target_pairs={{0,16},{16,0},{1,17},{17,1},{2,18},{18,2},{3,19},{19,3},{4,20},{20... | collective-permute-start | bytes 2580488 | tf_op jit(solution)/shard_map/ppermute | solution.py:457
  106.3 62.0 %collective-permute-start.15 = (bf16[280,1536]{1,0:T(8,128)(2,1)}, bf16[280,1536]{1,0:T(8,128)(2,1)}, u32[]{:S(2)}, u32[]{:S(2)}) collective-permute-start(bf16[280,1536]{1,0:T(8,128)(2,1)} %gate_copy.12), channel_id=1, source_target_pairs={{0,16},{16,0},{1,17},{17,1},{2,18},{18,2},{3,19},{19,3},{4,20},{20... | collective-permute-start | bytes 2580488 | tf_op jit(solution)/shard_map/ppermute | solution.py:457
  168.3 62.6 %collective-permute-start.17 = (bf16[280,1536]{1,0:T(8,128)(2,1)}, bf16[280,1536]{1,0:T(8,128)(2,1)}, u32[]{:S(2)}, u32[]{:S(2)}) collective-permute-start(bf16[280,1536]{1,0:T(8,128)(2,1)} %gate_copy.14), channel_id=1, source_target_pairs={{0,2},{2,0},{1,3},{3,1},{4,6},{6,4},{5,7},{7,5},{8,10},{10,8},{9,1... | collective-permute-start | bytes 2580488 | tf_op jit(solution)/shard_map/ppermute | solution.py:457
  190.4 100.5 %collective-permute-start.20 = (bf16[280,1536]{1,0:T(8,128)(2,1)}, bf16[280,1536]{1,0:T(8,128)(2,1)}, u32[]{:S(2)}, u32[]{:S(2)}) collective-permute-start(bf16[280,1536]{1,0:T(8,128)(2,1)} %gate_copy.15), channel_id=1, source_target_pairs={{0,2},{2,0},{1,3},{3,1},{4,6},{6,4},{5,7},{7,5},{8,10},{10,8},{9,1... | collective-permute-start | bytes 2580488 | tf_op jit(solution)/shard_map/ppermute | solution.py:457
  205.1 70.3 %collective-permute-start.24 = (bf16[512,1536]{1,0:T(8,128)(2,1)}, bf16[512,1536]{1,0:T(8,128)(2,1)}, u32[]{:S(2)}, u32[]{:S(2)}) collective-permute-start(bf16[512,1536]{1,0:T(8,128)(2,1)} %multiply_convert_fusion.refs_1_.normed.refs_4_), channel_id=1, source_target_pairs={{0,1},{1,0},{2,3},{3,2},{4,5},{5,4},{6,7},{7,6},{8,9},{9,8},{10,11... | collective-permute-start | bytes 4718600 | tf_op jit(solution)/shard_map/ppermute | solution.py:457
  205.1 74.5 %collective-permute-start.23 = (bf16[512,1536]{1,0:T(8,128)(2,1)}, bf16[512,1536]{1,0:T(8,128)(2,1)}, u32[]{:S(2)}, u32[]{:S(2)}) collective-permute-start(bf16[512,1536]{1,0:T(8,128)(2,1)} %multiply_convert_fusion.refs_1_.normed.refs_4_), channel_id=1, source_target_pairs={{0,8},{8,0},{1,9},{9,1},{2,10},{10,2},{3,11},{11,3},{4,12},{12,4},... | collective-permute-start | bytes 4718600 | tf_op jit(solution)/shard_map/ppermute | solution.py:457
  230.9 55.1 %collective-permute-start.18 = (bf16[280,1536]{1,0:T(8,128)(2,1)}, bf16[280,1536]{1,0:T(8,128)(2,1)}, u32[]{:S(2)}, u32[]{:S(2)}) collective-permute-start(bf16[280,1536]{1,0:T(8,128)(2,1)} %gate.44), channel_id=1, source_target_pairs={{0,16},{16,0},{1,17},{17,1},{2,18},{18,2},{3,19},{19,3},{4,20},{20... | collective-permute-start | bytes 2580488 | tf_op jit(solution)/shard_map/ppermute | solution.py:457
  495.5 71.5 %collective-permute-start.30 = (bf16[560,1536]{1,0:T(8,128)(2,1)}, bf16[560,1536]{1,0:T(8,128)(2,1)}, u32[]{:S(2)}, u32[]{:S(2)}) collective-permute-start(bf16[560,1536]{1,0:T(8,128)(2,1)} %get-tuple-element.83.refs_10_), channel_id=1, source_target_pairs={{0,16},{16,0},{1,17},{17,1},{2,18},{18,2},{3,19},{19,3},{4,20},{20... | collective-permute-start | bytes 5160968 | tf_op jit(solution)/shard_map/ppermute | solution.py:457
  546.9 56.6 %collective-permute-start.36 = (bf16[1120,1536]{1,0:T(8,128)(2,1)}, bf16[1120,1536]{1,0:T(8,128)(2,1)}, u32[]{:S(2)}, u32[]{:S(2)}) collective-permute-start(bf16[1120,1536]{1,0:T(8,128)(2,1)} %get-tuple-element.67), channel_id=1, source_target_pairs={{0,4},{4,0},{1,5},{5,1},{2,6},{6,2},{3,7},{7,3},{8,12},{12,8},{9,1... | collective-permute-start | bytes 10321928 | tf_op jit(solution)/shard_map/ppermute | solution.py:457
  546.9 123.6 %all-to-all-start.2 = ((bf16[4,1,2,512,256]{4,3,2,1,0:T(8,128)(2,1)}), bf16[4,1,2,512,256]{4,3,2,1,0:T(8,128)(2,1)}, u32[]{:S(2)}, u32[]{:S(2)}) async-start(bf16[4,1,2,512,256]{4,3,2,1,0:T(8,128)(2,1)} %get-tuple-element.68), calls=%async_computation.2 | async-start | bytes 4194304 | tf_op jit(solution)/shard_map/all_to_all | solution.py:608
  551.3 137.8 %reduce-scatter.2.cloned.1.call-start = ((), (), s32[]{:S(2)}) async-start(), calls=%async_computation.7 | async-start | bytes 4866048 | tf_op jit(solution)/shard_map/reduce_scatter | solution.py:839
  600.7 128.4 %collective-permute-start.33 = (bf16[280,1536]{1,0:T(8,128)(2,1)}, bf16[280,1536]{1,0:T(8,128)(2,1)}, u32[]{:S(2)}, u32[]{:S(2)}) collective-permute-start(bf16[280,1536]{1,0:T(8,128)(2,1)} %slice.213), channel_id=1, source_target_pairs={{0,2},{2,0},{1,3},{3,1},{4,6},{6,4},{5,7},{7,5},{8,10},{10,8},{9,1... | collective-permute-start | bytes 2580488 | tf_op jit(solution)/shard_map/ppermute | solution.py:457
  610.1 55.8 %collective-permute-start.38 = (bf16[560,1536]{1,0:T(8,128)(2,1)}, bf16[560,1536]{1,0:T(8,128)(2,1)}, u32[]{:S(2)}, u32[]{:S(2)}) collective-permute-start(bf16[560,1536]{1,0:T(8,128)(2,1)} %get-tuple-element.81.refs_4_), channel_id=1, source_target_pairs={{0,16},{16,0},{1,17},{17,1},{2,18},{18,2},{3,19},{19,3},{4,20},{20... | collective-permute-start | bytes 5160968 | tf_op jit(solution)/shard_map/ppermute | solution.py:457
  630.0 94.7 %collective-permute-start.37 = (bf16[560,1536]{1,0:T(8,128)(2,1)}, bf16[560,1536]{1,0:T(8,128)(2,1)}, u32[]{:S(2)}, u32[]{:S(2)}) collective-permute-start(bf16[560,1536]{1,0:T(8,128)(2,1)} %get-tuple-element.79.refs_3_), channel_id=1, source_target_pairs={{0,16},{16,0},{1,17},{17,1},{2,18},{18,2},{3,19},{19,3},{4,20},{20... | collective-permute-start | bytes 5160968 | tf_op jit(solution)/shard_map/ppermute | solution.py:457
  646.5 94.3 %collective-permute-start.41 = (bf16[512,1536]{1,0:T(8,128)(2,1)}, bf16[512,1536]{1,0:T(8,128)(2,1)}, u32[]{:S(2)}, u32[]{:S(2)}) collective-permute-start(bf16[512,1536]{1,0:T(8,128)(2,1)} %back_rows.14.refs_2_), channel_id=1, source_target_pairs={{0,8},{8,0},{1,9},{9,1},{2,10},{10,2},{3,11},{11,3},{4,12},{12,4},... | collective-permute-start | bytes 4718600 | tf_op jit(solution)/shard_map/ppermute | solution.py:457
  690.8 60.0 %collective-permute-start.42 = (bf16[512,1536]{1,0:T(8,128)(2,1)}, bf16[512,1536]{1,0:T(8,128)(2,1)}, u32[]{:S(2)}, u32[]{:S(2)}) collective-permute-start(bf16[512,1536]{1,0:T(8,128)(2,1)} %add_convert_fusion.11.refs_1_), channel_id=1, source_target_pairs={{0,1},{1,0},{2,3},{3,2},{4,5},{5,4},{6,7},{7,6},{8,9},{9,8},{10,11... | collective-permute-start | bytes 4718600 | tf_op jit(solution)/shard_map/ppermute | solution.py:457
  696.0 76.1 %all-to-all-start.3 = ((bf16[4,4,64,1536]{3,2,1,0:T(8,128)(2,1)}), bf16[4,4,64,1536]{3,2,1,0:T(8,128)(2,1)}, u32[]{:S(2)}, u32[]{:S(2)}) async-start(bf16[4,4,64,1536]{3,2,1,0:T(8,128)(2,1)} %bitcast.27.refs_1_), calls=%async_computation.3 | async-start | bytes 6291456 | tf_op jit(solution)/shard_map/all_to_all | solution.py:608
  (125 other events, 1505.2 us)
Sparse Core Ops, SparseCore 0:
  81.2 109.6 all-gather.1
  558.2 127.6 reduce-scatter.1

commit v3 on v2

--- a/solution.py
+++ b/solution.py
@@ -422,7 +422,7 @@
         in_specs=[pl.BlockSpec((rows, width), lambda i: (0, 0)), out, part, part],
         out_specs=[out, out, out],
         out_shape=[shape, shape, shape],
-        compiler_params=pltpu.CompilerParams(vmem_limit_bytes=48 * MIB),
+        compiler_params=pltpu.CompilerParams(vmem_limit_bytes=60 * MIB),
         cost_estimate=cost(
             4 * units * rows * width, 4 * units * width + 8 * units * rows, 2 * units * rows
         ),
@@ -699,14 +699,14 @@
     )
     qkv_parts = [xor_send(w_qkv, k) for k in (1, 2, 3)]
     down_a = over_a(w_down)
-    qkv_parts[0] = gate(qkv_parts[0], wait(w_qkv), down_a)
+    qkv_parts[0] = gate(qkv_parts[0], wait(w_qkv))
     qkv_z = order_ctx(w_qkv, *qkv_parts)
     by_a, by_b = stack_plane_first(qkv_z)
     own_down = gate_copy(w_down, qkv_z)
     down_z = flip(own_down, "ch")
     vectors_all = gate(vectors_all, qkv_z)
     cot_z = flip(gate_copy(cotangent, qkv_z), "cl")
-    by_a = gate(by_a, wait(qkv_z))
+    by_a = gate(by_a, wait(qkv_z), down_a)
     if by_b is None:
         qkv_plane = stack_axis(by_a, "fa", 0)
     else:
@@ -823,45 +823,11 @@
     d_queries = d_queries.reshape(row_count, query_width)
     d_kv_parts = exchange(d_kv_parts, CTX_AXES)
 
-    def add_three(own, by_x, by_z, middle):
-        return (middle + own.astype(wide) + by_x.astype(wide) + by_z.astype(wide)).astype(low)
-
     def add_wide(own, other):
         return own.astype(wide) + other.astype(wide)
 
     def split_terms(left, right, *first):
         return core_terms(left, right, ctx_count * w_qkv.shape[0], *first)
-
-    gate_kept, gate_sent = unit_grads(d_gate, normed_parts, d_queries)
-    gate_sent = flip(gate_sent, "fc")
-    down_sums = add_a(down_sums, gate(down_from_a, gate_kept))
-    down_z_sums = flip(halves(down_sums)[1], "ch")
-    grad_out = lax.psum_scatter(
-        back_rows((attended_rows,), (d_branch,), gate_kept),
-        ALL_AXES,
-        scatter_dimension=0,
-        tiled=True,
-    ).astype(wide)
-    query_kept, query_sent = split_terms(d_queries, normed_one, down_sums)
-    query_sent = flip(query_sent, "fc")
-    up_kept, up_sent = unit_grads(d_up, normed_parts, query_kept)
-    up_sent = flip(up_sent, "fc")
-    query_sums = add_low(query_kept, gate(query_sent, up_kept))
-    gate_sums = add_core(gate_kept, gate(gate_sent, up_kept))
-    gate_from_a = over_a_sums(gate_sums)
-    branch_far = branch_rows(3, query_sums, *gate_sums)
-    branch_from = flip(branch_far, "fb")
-    up_sums = add_core(up_kept, gate(up_sent, branch_far))
-    up_from_a = over_a_sums(up_sums)
-    branch_x = branch_rows(1, *up_sums)
-    branch_z = branch_rows(2, branch_x)
-    branch_x = flip(branch_x, "fb")
-    branch_z = add_low(branch_z, gate(branch_from, branch_z))
-    gate_sums = add_a(gate_sums, gate(gate_from_a, branch_z))
-    gate_z_sums = flip(halves(gate_sums)[1], "ch")
-    d_kv_parts = gate(d_kv_parts, gate_sums)
-    branch_z = flip(branch_z, "cl")
-    query_bias_local = jnp.sum(d_queries, axis=0, dtype=wide)
 
     def turn_back(parts):
         d_kv = jnp.sum(parts, axis=0, dtype=wide)
@@ -872,9 +838,30 @@
             turned.append(part * cosine - jnp.roll(part, HEAD // 2, 1) * signed_sine)
         return jnp.concatenate([*turned, d_values], axis=1).astype(low)
 
-    d_kv = turn_back(d_kv_parts)
-    kv_kept, kv_sent = split_terms(d_kv, normed_one)
-    kv_sent = gate(flip(kv_sent, "fc"), wait(kv_kept))
+    gate_kept, gate_sent = unit_grads(d_gate, normed_parts, d_queries)
+    gate_sent = flip(gate_sent, "fc")
+    grad_out_local = back_rows((attended_rows,), (d_branch,), gate_kept)
+    grad_out = lax.psum_scatter(grad_out_local, ALL_AXES, scatter_dimension=0, tiled=True)
+    down_sums = add_a(down_sums, gate(down_from_a, grad_out_local))
+    down_z_sums = flip(halves(down_sums)[1], "ch")
+    query_kept, query_sent = split_terms(d_queries, normed_one, down_sums)
+    query_sent = flip(query_sent, "fc")
+    gate_sums = add_core(gate_kept, gate(gate_sent, query_kept))
+    gate_from_a = over_a_sums(gate_sums)
+    up_kept, up_sent = unit_grads(d_up, normed_parts, *gate_sums)
+    up_sent = flip(up_sent, "fc")
+    branch_far = branch_rows(3, up_kept)
+    branch_from = flip(branch_far, "fb")
+    branch_z = branch_rows(2, branch_far)
+    d_kv = turn_back(gate(d_kv_parts, branch_z))
+    query_sums = add_low(query_kept, gate(query_sent, d_kv))
+    gate_sums = add_a(gate_sums, gate(gate_from_a, query_sums))
+    gate_z_sums = flip(halves(gate_sums)[1], "ch")
+    up_sums = add_core(up_kept, gate(up_sent, gate_sums))
+    up_from_a = over_a_sums(up_sums)
+    kv_kept, kv_sent = split_terms(d_kv, normed_one, *up_sums)
+    kv_sent = flip(kv_sent, "fc")
+    query_bias_local = jnp.sum(d_queries, axis=0, dtype=wide)
     kv_bias_local = jnp.sum(d_kv, axis=0, dtype=wide)
 
     def back_projection(d_queries, d_kv, weight):
@@ -892,31 +879,37 @@
     def add_all(values):
         return jnp.sum(values, axis=0, dtype=wide)
 
-    d_normed_one = back_projection(d_queries, d_kv, qkv_all)
+    qkv_terms = join_qkv(query_sums, kv_kept, gate(kv_sent, wait(kv_kept)))
+    qkv_sums = exchange(qkv_terms, ("fa", "fb"))
+    d_normed_one = back_projection(d_queries, gate(d_kv, qkv_terms), qkv_all)
     grad_tokens, grad_gain_one = back_tokens(d_normed_one, tokens, gain_one, d_middle)
     vector_grads = [query_bias_local, kv_bias_local, grad_gain_one, grad_gain_two]
-    qkv_terms = join_qkv(query_sums, kv_kept, gate(kv_sent, grad_tokens))
-    qkv_sums = exchange(qkv_terms, ("fa", "fb"))
-    up_sums = add_a(up_sums, gate(up_from_a, qkv_terms))
+    branch_x = branch_rows(1, grad_tokens)
+    branch_own = branch_rows(0, branch_x)
+    branch_x = flip(branch_x, "fb")
+    branch_z = add_low(branch_z, gate(branch_from, branch_own))
+    grad_down = add_wide(halves(down_sums)[0], gate(down_z_sums, branch_z))
+    branch_z = flip(branch_z, "cl")
+    up_sums = add_a(up_sums, gate(up_from_a, grad_down))
     up_z_sums = flip(halves(up_sums)[1], "ch")
-    grad_down = add_wide(halves(down_sums)[0], gate(down_z_sums, up_sums))
-    branch_own = branch_rows(0, grad_down)
-    layer_out = add_three(branch_own, gate(branch_x, branch_own), branch_z, middle)
-    qkv_sums = add_all(gate(qkv_sums, layer_out)).astype(low)
+    grad_gate = add_wide(halves(gate_sums)[0], gate(gate_z_sums, up_sums))
+    qkv_sums = add_all(gate(qkv_sums, grad_gate)).astype(low)
+    branch_sum = add_wide(branch_own, gate(branch_x, qkv_sums))
+    qkv_sums = gate(qkv_sums, branch_sum)
 
     def pick(rank):
         return lax.dynamic_index_in_dim(qkv_sums, rank, 0, keepdims=False)
 
     qkv_own = pick(ctx_rank)
     qkv_from = [xor_send(pick(ctx_rank ^ k), k) for k in (1, 2, 3)]
-    packed = gate(pack_vectors(vector_grads, device_count), qkv_own)
+    packed = gate(pack_vectors(vector_grads, device_count), pick(ctx_rank ^ 3))
     vector_shares = exchange(packed, ALL_AXES)
-    qkv_from[0] = gate(qkv_from[0], wait(qkv_own), vector_shares)
-
-
-    grad_gate = add_wide(halves(gate_sums)[0], gate_z_sums)
+    branch_z = gate(branch_z, pick(ctx_rank ^ 2))
+    layer_out = (middle + add_wide(branch_z, branch_sum)).astype(low)
+    qkv_from[0] = gate(qkv_from[0], wait(qkv_own), layer_out)
+    grad_out = gate(grad_out, qkv_own).astype(wide)
     grad_qkv = functools.reduce(jnp.add, (part.astype(wide) for part in (qkv_own, *qkv_from)))
-    grad_up = add_wide(halves(up_sums)[0], up_z_sums)
+    grad_up = add_wide(halves(up_sums)[0], gate(up_z_sums, grad_qkv))
     grad_query_bias, grad_kv_bias, grad_norm_attn, grad_norm_mlp = unpack_vectors(
         jnp.sum(vector_shares, axis=0)[None], [v.shape[0] // device_count for v in vector_grads]
     )

time: 821 us -> 786 us (0.957)
  waiting for transfers between devices: 149 us -> 131 us
  starting transfers between devices: 109 us -> 92 us
  local copies, waits for them, and re-layouts: 110 us -> 93.5 us
    ppermute x42, waiting for transfers between devices: 85.6 us -> 55.6 us  [flip(): return lax.ppermute(values, axis, [(0, 1), (1, 0)])]
    all_to_all x5, starting transfers between devices: 42 us -> 23.5 us  [exchange(): return lax.all_to_all(values, axes, split_axis=0, concat_axis=0, tiled=True)]
    unnamed x198 -> x178, local copies, waits for them, and re-layouts: 75.7 us -> 58.7 us
  transfers between devices with their start and end apart: 55 -> 55, of which waited for: 17 -> 16; matrix products, arithmetic and copies ran while one was open for 20% -> 22% of each run, Pallas kernels for 30% -> 32%
where the time goes in v3:
time: 786 us; the launch traced here: 777 us
  Pallas kernels  314 us (40%)
  waiting for transfers between devices  131 us (17%)
  other arithmetic  109 us (14%)
  local copies, waits for them, and re-layouts  93.5 us (12%)
  starting transfers between devices  92 us (12%)
  matrix products  20.7 us (3%)
  between operations  16.9 us (2%)
    pallas_call x9, Pallas kernels, back_rows(): pl.pallas_call(with_tokens(functools.partial(back_kernel, count), 2 * cou...  88.3 us
    pallas_call x3, Pallas kernels, unit_grads(): pl.pallas_call(with_tokens(functools.partial(grad_kernel, count), 2 * cou...  64.4 us
    all_to_all x5, waiting for transfers between devices, exchange(): return lax.all_to_all(values, axes, split_axis=0, concat_axis=0, tiled=True)  60.6 us
    unnamed x178, local copies, waits for them, and re-layouts  58.7 us
    ppermute x42, starting transfers between devices, flip(): return lax.ppermute(values, axis, [(0, 1), (1, 0)])  58.3 us
    pallas_call x4, Pallas kernels, unit_rows(): pl.pallas_call(unit_kernel, grid=(4,), in_specs=[pl.BlockSpec((rows, widt...  56.5 us
    ppermute x42, waiting for transfers between devices, flip(): return lax.ppermute(values, axis, [(0, 1), (1, 0)])  55.6 us
    convert_element_type x8, other arithmetic, add_low(): functools.reduce(jnp.add, (t.astype(jnp.float32) for t in terms))  27.9 us
  transfers between devices with their start and end apart: 55, of which 16 were waited for; matrix products, arithmetic and copies ran while one was open for 22% of the time, Pallas kernels for 32%

profile of v3, /device:TPU:0, one launch (start us, length us, event | category | flops | bytes accessed | tf_op | source)
XLA Modules:
  0.0 777.3 jit_solution(15758206764543537421)
XLA Ops:
  112.5 52.5 %all-to-all-done.1.refs_2_.refs_3_.refs_1_ = bf16[4,1,512,512]{3,2,1,0:T(8,128)(2,1)} async-done(((bf16[4,1,512,512]{3,2,1,0:T(8,128)(2,1)}), bf16[4,1,512,512]{3,2,1,0:T(8,128)(2,1)}, u32[]{:S(2)}, u32[]{:S(2)}) %all-to-all-start.1) | async-done | bytes 2097184 | tf_op jit(solution)/shard_map/all_to_all | solution.py:608
  168.6 17.3 %attend_forward.1 = (bf16[1,512,1536]{2,1,0:T(8,128)(2,1)S(1)}, f32[1,2,2,6,256]{4,3,2,1,0:T(8,128)S(1)}) custom-call(s32[1,10]{1,0:T(1,128)S(1)} %pad_add_fusion.refs_0_, bf16[1,512,1536]{2,1,0:T(8,128)(2,1)S(1)} %bitcast.84, bf16[4,1,512,512]{3,2,1,0:T(8,128)(2,1)} %all-to-all-done.1.refs_2_.refs_3_.refs_1_, ...), custom_call_target="tpu_custom_call" | custom-call | flops 57982058496 | bytes 100663296 | tf_op jit(solution)/shard_map/attend_forward/pallas_call | solution.py:98
  230.0 17.2 %collective-permute-start.19 = (bf16[280,1536]{1,0:T(8,128)(2,1)}, bf16[280,1536]{1,0:T(8,128)(2,1)}, u32[]{:S(2)}, u32[]{:S(2)}) collective-permute-start(bf16[280,1536]{1,0:T(8,128)(2,1)} %gate.50), channel_id=1, source_target_pairs={{0,16},{16,0},{1,17},{17,1},{2,18},{18,2},{3,19},{19,3},{4,20},{20... | collective-permute-start | bytes 2580488 | tf_op jit(solution)/shard_map/ppermute | solution.py:457
  264.5 10.5 %collective-permute-done.16.refs_0_ = bf16[512,1536]{1,0:T(8,128)(2,1)} collective-permute-done((bf16[512,1536]{1,0:T(8,128)(2,1)}, bf16[512,1536]{1,0:T(8,128)(2,1)}, u32[]{:S(2)}, u32[]{:S(2)}) %collective-permute-start.16) | collective-permute-done | bytes 1572896 | tf_op jit(solution)/shard_map/ppermute | solution.py:457
  301.9 10.7 %collective-permute-done.22.refs_0_ = bf16[280,1536]{1,0:T(8,128)(2,1)} collective-permute-done((bf16[280,1536]{1,0:T(8,128)(2,1)}, bf16[280,1536]{1,0:T(8,128)(2,1)}, u32[]{:S(2)}, u32[]{:S(2)}) %collective-permute-start.22) | collective-permute-done | bytes 860192 | tf_op jit(solution)/shard_map/ppermute | solution.py:457
  326.4 14.0 %unit_rows.7 = (bf16[2240,512]{1,0:T(8,128)(2,1)}, bf16[2240,512]{1,0:T(8,128)(2,1)}, bf16[2240,512]{1,0:T(8,128)(2,1)}) custom-call(bf16[512,1536]{1,0:T(8,128)(2,1)} %gate.57.normed.refs_5_, bf16[2240,512]{1,0:T(8,128)(2,1)} %copy-done.3, bf16[2240,1536]{1,0:T(8,128)(2,1)} %constant_dynamic-update-slice_fusion.5.refs_1_.gate.refs_2_, ...), custom_call_target="tpu_custom_call" | custom-call | flops 112742891520 | bytes 367001600 | tf_op jit(solution)/shard_map/unit_rows/pallas_call | solution.py:419
  340.5 14.3 %unit_rows.4 = (bf16[2240,512]{1,0:T(8,128)(2,1)}, bf16[2240,512]{1,0:T(8,128)(2,1)}, bf16[2240,512]{1,0:T(8,128)(2,1)}) custom-call(bf16[512,1536]{1,0:T(8,128)(2,1)} %gate.49.normed.refs_6_, bf16[2240,512]{1,0:T(8,128)(2,1)} %copy-done.1, bf16[2240,1536]{1,0:T(8,128)(2,1)} %constant_dynamic-update-slice_fusion.5.refs_1_.gate.refs_2_, ...), custom_call_target="tpu_custom_call" | custom-call | flops 112742891520 | bytes 367001600 | tf_op jit(solution)/shard_map/unit_rows/pallas_call | solution.py:419
  354.8 14.2 %unit_rows.6 = (bf16[2240,512]{1,0:T(8,128)(2,1)}, bf16[2240,512]{1,0:T(8,128)(2,1)}, bf16[2240,512]{1,0:T(8,128)(2,1)}) custom-call(bf16[512,1536]{1,0:T(8,128)(2,1)} %multiply_convert_fusion.refs_1_.normed.refs_4_, bf16[2240,512]{1,0:T(8,128)(2,1)} %copy-done, bf16[2240,1536]{1,0:T(8,128)(2,1)} %constant_dynamic-update-slice_fusion.5.refs_1_.gate.refs_2_, ...), custom_call_target="tpu_custom_call" | custom-call | flops 112742891520 | bytes 367001600 | tf_op jit(solution)/shard_map/unit_rows/pallas_call | solution.py:419
  368.9 14.0 %unit_rows.5 = (bf16[2240,512]{1,0:T(8,128)(2,1)}, bf16[2240,512]{1,0:T(8,128)(2,1)}, bf16[2240,512]{1,0:T(8,128)(2,1)}) custom-call(bf16[512,1536]{1,0:T(8,128)(2,1)} %pad_maximum_fusion.8.normed.refs_7_, bf16[2240,512]{1,0:T(8,128)(2,1)} %copy-done.2, bf16[2240,1536]{1,0:T(8,128)(2,1)} %constant_dynamic-update-slice_fusion.5.refs_1_.gate.refs_2_, ...), custom_call_target="tpu_custom_call" | custom-call | flops 112742891520 | bytes 367001600 | tf_op jit(solution)/shard_map/unit_rows/pallas_call | solution.py:419
  383.0 12.5 %back_rows.9.refs_4_ = bf16[512,1536]{1,0:T(8,128)(2,1)} custom-call(bf16[2240,512]{1,0:T(8,128)(2,1)} %get-tuple-element.54.refs_0_.refs_3_, bf16[2240,512]{1,0:T(8,128)(2,1)} %get-tuple-element.50.refs_1_.refs_3_, bf16[2240,1536]{1,0:T(8,128)(2,1)} %constant_dynamic-update-slice_fusion.5.refs_1_.gate.refs_2_, ...), custom_call_target="tpu_custom_call" | custom-call | flops 112742891520 | bytes 293601280 | tf_op jit(solution)/shard_map/back_rows/pallas_call | solution.py:293
  400.1 12.5 %back_rows.10.refs_4_ = bf16[512,1536]{1,0:T(8,128)(2,1)} custom-call(bf16[2240,512]{1,0:T(8,128)(2,1)} %get-tuple-element.52.refs_0_.refs_1_, bf16[2240,512]{1,0:T(8,128)(2,1)} %get-tuple-element.48.refs_1_, bf16[2240,1536]{1,0:T(8,128)(2,1)} %constant_dynamic-update-slice_fusion.5.refs_1_.gate.refs_2_, ...), custom_call_target="tpu_custom_call" | custom-call | flops 112742891520 | bytes 293601280 | tf_op jit(solution)/shard_map/back_rows/pallas_call | solution.py:293
  412.6 12.5 %back_rows.11.refs_1_ = bf16[512,1536]{1,0:T(8,128)(2,1)} custom-call(bf16[2240,512]{1,0:T(8,128)(2,1)} %get-tuple-element.53.refs_0_.refs_2_, bf16[2240,512]{1,0:T(8,128)(2,1)} %get-tuple-element.49.refs_1_.refs_2_, bf16[2240,1536]{1,0:T(8,128)(2,1)} %constant_dynamic-update-slice_fusion.5.refs_1_.gate.refs_2_, ...), custom_call_target="tpu_custom_call" | custom-call | flops 112742891520 | bytes 293601280 | tf_op jit(solution)/shard_map/back_rows/pallas_call | solution.py:293
  434.1 21.6 %unit_grads.3 = (bf16[1120,1536]{1,0:T(8,128)(2,1)}, bf16[1120,1536]{1,0:T(8,128)(2,1)}) custom-call(bf16[2240,512]{1,0:T(8,128)(2,1)} %get-tuple-element.55.refs_0_, bf16[2240,512]{1,0:T(8,128)(2,1)} %get-tuple-element.56.refs_1_.refs_0_, bf16[2240,512]{1,0:T(8,128)(2,1)} %get-tuple-element.45.refs_2_.refs_0_, ...), custom_call_target="tpu_custom_call" | custom-call | flops 225485783040 | bytes 247463936 | tf_op jit(solution)/shard_map/unit_grads/pallas_call | solution.py:258
  455.7 12.6 %back_rows.12.refs_1_ = bf16[512,1536]{1,0:T(8,128)(2,1)} custom-call(bf16[2240,512]{1,0:T(8,128)(2,1)} %get-tuple-element.51.refs_0_, bf16[2240,512]{1,0:T(8,128)(2,1)} %get-tuple-element.47.refs_1_.refs_0_, bf16[2240,1536]{1,0:T(8,128)(2,1)} %constant_dynamic-update-slice_fusion.5.refs_1_.gate.refs_2_, ...), custom_call_target="tpu_custom_call" | custom-call | flops 112742891520 | bytes 293601280 | tf_op jit(solution)/shard_map/back_rows/pallas_call | solution.py:293
  492.4 27.5 %attend_backward.1 = (bf16[1,512,1536]{2,1,0:T(8,128)(2,1)S(1)}, bf16[4,1,2,512,256]{4,3,2,1,0:T(8,128)(2,1)}) custom-call(s32[1,10]{1,0:T(1,128)S(1)} %copy-done.35, bf16[1,512,1536]{2,1,0:T(8,128)(2,1)S(1)} %bitcast.85, bf16[4,1,512,512]{3,2,1,0:T(8,128)(2,1)} %all-to-all-done.1.refs_2_.refs_3_.refs_1_, ...), custom_call_target="tpu_custom_call" | custom-call | flops 144955146240 | bytes 201326592 | tf_op jit(solution)/shard_map/attend_backward/pallas_call | solution.py:197
  521.1 21.3 %unit_grads.4 = (bf16[1120,1536]{1,0:T(8,128)(2,1)}, bf16[1120,1536]{1,0:T(8,128)(2,1)}) custom-call(bf16[2240,512]{1,0:T(8,128)(2,1)} %get-tuple-element.51.refs_0_, bf16[2240,512]{1,0:T(8,128)(2,1)} %get-tuple-element.52.refs_0_.refs_1_, bf16[2240,512]{1,0:T(8,128)(2,1)} %get-tuple-element.53.refs_0_.refs_2_, ...), custom_call_target="tpu_custom_call" | custom-call | flops 225485783040 | bytes 247463936 | tf_op jit(solution)/shard_map/unit_grads/pallas_call | solution.py:258
  585.1 21.5 %unit_grads.5 = (bf16[1120,1536]{1,0:T(8,128)(2,1)}, bf16[1120,1536]{1,0:T(8,128)(2,1)}) custom-call(bf16[2240,512]{1,0:T(8,128)(2,1)} %get-tuple-element.47.refs_1_.refs_0_, bf16[2240,512]{1,0:T(8,128)(2,1)} %get-tuple-element.48.refs_1_, bf16[2240,512]{1,0:T(8,128)(2,1)} %get-tuple-element.49.refs_1_.refs_2_, ...), custom_call_target="tpu_custom_call" | custom-call | flops 225485783040 | bytes 247463936 | tf_op jit(solution)/shard_map/unit_grads/pallas_call | solution.py:258
  606.6 7.8 %back_rows.14.refs_2_ = bf16[512,1536]{1,0:T(8,128)(2,1)} custom-call(bf16[2240,512]{1,0:T(8,128)(2,1)} %get-tuple-element.46.refs_3_.refs_0_, bf16[2240,1536]{1,0:T(8,128)(2,1)} %constant_dynamic-update-slice_fusion.weight.refs_1_, bf16[1120,1536]{1,0:T(8,128)(2,1)} %get-tuple-element.65.refs_2_), custom_call_target="tpu_custom_call" | custom-call | flops 56371445760 | bytes 146800640 | tf_op jit(solution)/shard_map/back_rows/pallas_call | solution.py:293
  614.4 8.1 %back_rows.15.refs_1_ = bf16[512,1536]{1,0:T(8,128)(2,1)} custom-call(bf16[2240,512]{1,0:T(8,128)(2,1)} %get-tuple-element.45.refs_2_.refs_0_, bf16[2240,1536]{1,0:T(8,128)(2,1)} %constant_dynamic-update-slice_fusion.weight.refs_1_, bf16[512,1536]{1,0:T(8,128)(2,1)} %back_rows.14.refs_2_), custom_call_target="tpu_custom_call" | custom-call | flops 56371445760 | bytes 146800640 | tf_op jit(solution)/shard_map/back_rows/pallas_call | solution.py:293
  664.5 8.0 %back_rows.16.refs_2_ = bf16[512,1536]{1,0:T(8,128)(2,1)} custom-call(bf16[2240,512]{1,0:T(8,128)(2,1)} %get-tuple-element.56.refs_1_.refs_0_, bf16[2240,1536]{1,0:T(8,128)(2,1)} %constant_dynamic-update-slice_fusion.weight.refs_1_, f32[512,1536]{1,0:T(8,128)} %fusion.7.refs_2_), custom_call_target="tpu_custom_call" | custom-call | flops 56371445760 | bytes 146800640 | tf_op jit(solution)/shard_map/back_rows/pallas_call | solution.py:293
  672.5 7.9 %back_rows.17.refs_1_ = bf16[512,1536]{1,0:T(8,128)(2,1)} custom-call(bf16[2240,512]{1,0:T(8,128)(2,1)} %get-tuple-element.55.refs_0_, bf16[2240,1536]{1,0:T(8,128)(2,1)} %constant_dynamic-update-slice_fusion.weight.refs_1_, bf16[512,1536]{1,0:T(8,128)(2,1)} %back_rows.16.refs_2_), custom_call_target="tpu_custom_call" | custom-call | flops 56371445760 | bytes 146800640 | tf_op jit(solution)/shard_map/back_rows/pallas_call | solution.py:293
  690.3 15.1 %collective-permute-done.41.refs_0_ = bf16[560,1536]{1,0:T(8,128)(2,1)} collective-permute-done((bf16[560,1536]{1,0:T(8,128)(2,1)}, bf16[560,1536]{1,0:T(8,128)(2,1)}, u32[]{:S(2)}, u32[]{:S(2)}) %collective-permute-start.41) | collective-permute-done | bytes 1720352 | tf_op jit(solution)/shard_map/ppermute | solution.py:457
  713.4 8.2 %all-to-all-done.3.refs_0_ = bf16[4,4,64,1536]{3,2,1,0:T(8,128)(2,1)} async-done(((bf16[4,4,64,1536]{3,2,1,0:T(8,128)(2,1)}), bf16[4,4,64,1536]{3,2,1,0:T(8,128)(2,1)}, u32[]{:S(2)}, u32[]{:S(2)}) %all-to-all-start.3) | async-done | bytes 3145760 | tf_op jit(solution)/shard_map/all_to_all | solution.py:608
  753.2 10.9 %collective-permute-done.45 = bf16[64,1536]{1,0:T(8,128)(2,1)} collective-permute-done((bf16[64,1536]{1,0:T(8,128)(2,1)S(1)}, bf16[64,1536]{1,0:T(8,128)(2,1)}, u32[]{:S(2)}, u32[]{:S(2)}) %collective-permute-start.45) | collective-permute-done | bytes 196640 | tf_op jit(solution)/shard_map/ppermute | solution.py:572
  (447 shorter events, 387.8 us)
Async XLA Ops:
  20.2 172.0 %all-gather.2.cloned.1.call-start = ((), (), s32[]{:S(2)}) async-start(), calls=%async_computation.6 | async-start | bytes 4866048 | tf_op jit(solution)/shard_map/all_gather | solution.py:717
  43.6 56.7 %collective-permute-start.10 = (bf16[512,1536]{1,0:T(8,128)(2,1)}, bf16[512,1536]{1,0:T(8,128)(2,1)}, u32[]{:S(2)}, u32[]{:S(2)}) collective-permute-start(bf16[512,1536]{1,0:T(8,128)(2,1)} %gate_copy.9), channel_id=1, source_target_pairs={{0,1},{1,0},{2,3},{3,2},{4,5},{5,4},{6,7},{7,6},{8,9},{9,8},{10,11... | collective-permute-start | bytes 4718600 | tf_op jit(solution)/shard_map/ppermute | solution.py:457
  43.6 58.3 %collective-permute-start.12 = (bf16[280,1536]{1,0:T(8,128)(2,1)}, bf16[280,1536]{1,0:T(8,128)(2,1)}, u32[]{:S(2)}, u32[]{:S(2)}) collective-permute-start(bf16[280,1536]{1,0:T(8,128)(2,1)} %gate_copy.10), channel_id=1, source_target_pairs={{0,2},{2,0},{1,3},{3,1},{4,6},{6,4},{5,7},{7,5},{8,10},{10,8},{9,1... | collective-permute-start | bytes 2580488 | tf_op jit(solution)/shard_map/ppermute | solution.py:457
  73.3 93.8 %collective-permute-start.9 = (bf16[512,1536]{1,0:T(8,128)(2,1)}, bf16[512,1536]{1,0:T(8,128)(2,1)}, u32[]{:S(2)}, u32[]{:S(2)}) collective-permute-start(bf16[512,1536]{1,0:T(8,128)(2,1)} %gate_copy.8), channel_id=1, source_target_pairs={{0,8},{8,0},{1,9},{9,1},{2,10},{10,2},{3,11},{11,3},{4,12},{12,4},... | collective-permute-start | bytes 4718600 | tf_op jit(solution)/shard_map/ppermute | solution.py:457
  76.0 91.1 %collective-permute-start.14 = (bf16[280,1536]{1,0:T(8,128)(2,1)}, bf16[280,1536]{1,0:T(8,128)(2,1)}, u32[]{:S(2)}, u32[]{:S(2)}) collective-permute-start(bf16[280,1536]{1,0:T(8,128)(2,1)} %gate_copy.11), channel_id=1, source_target_pairs={{0,16},{16,0},{1,17},{17,1},{2,18},{18,2},{3,19},{19,3},{4,20},{20... | collective-permute-start | bytes 2580488 | tf_op jit(solution)/shard_map/ppermute | solution.py:457
  95.7 69.3 %all-to-all-start.1 = ((bf16[4,1,512,512]{3,2,1,0:T(8,128)(2,1)}), bf16[4,1,512,512]{3,2,1,0:T(8,128)(2,1)}, u32[]{:S(2)}, u32[]{:S(2)}) async-start(bf16[4,1,512,512]{3,2,1,0:T(8,128)(2,1)} %broadcast_in_dim.17.refs_1_), calls=%async_computation.1 | async-start | bytes 4194304 | tf_op jit(solution)/shard_map/all_to_all | solution.py:608
  100.3 66.8 %collective-permute-start.11 = (bf16[512,1536]{1,0:T(8,128)(2,1)}, bf16[512,1536]{1,0:T(8,128)(2,1)}, u32[]{:S(2)}, u32[]{:S(2)}) collective-permute-start(bf16[512,1536]{1,0:T(8,128)(2,1)} %gate.45.rows.refs_6_), channel_id=1, source_target_pairs={{0,8},{8,0},{1,9},{9,1},{2,10},{10,2},{3,11},{11,3},{4,12},{12,4},... | collective-permute-start | bytes 4718600 | tf_op jit(solution)/shard_map/ppermute | solution.py:457
  101.9 65.2 %collective-permute-start.13 = (bf16[280,1536]{1,0:T(8,128)(2,1)}, bf16[280,1536]{1,0:T(8,128)(2,1)}, u32[]{:S(2)}, u32[]{:S(2)}) collective-permute-start(bf16[280,1536]{1,0:T(8,128)(2,1)} %gate.46), channel_id=1, source_target_pairs={{0,16},{16,0},{1,17},{17,1},{2,18},{18,2},{3,19},{19,3},{4,20},{20... | collective-permute-start | bytes 2580488 | tf_op jit(solution)/shard_map/ppermute | solution.py:457
  104.5 62.6 %collective-permute-start.15 = (bf16[280,1536]{1,0:T(8,128)(2,1)}, bf16[280,1536]{1,0:T(8,128)(2,1)}, u32[]{:S(2)}, u32[]{:S(2)}) collective-permute-start(bf16[280,1536]{1,0:T(8,128)(2,1)} %gate_copy.12), channel_id=1, source_target_pairs={{0,16},{16,0},{1,17},{17,1},{2,18},{18,2},{3,19},{19,3},{4,20},{20... | collective-permute-start | bytes 2580488 | tf_op jit(solution)/shard_map/ppermute | solution.py:457
  167.1 62.9 %collective-permute-start.18 = (bf16[280,1536]{1,0:T(8,128)(2,1)}, bf16[280,1536]{1,0:T(8,128)(2,1)}, u32[]{:S(2)}, u32[]{:S(2)}) collective-permute-start(bf16[280,1536]{1,0:T(8,128)(2,1)} %gate_copy.14), channel_id=1, source_target_pairs={{0,2},{2,0},{1,3},{3,1},{4,6},{6,4},{5,7},{7,5},{8,10},{10,8},{9,1... | collective-permute-start | bytes 2580488 | tf_op jit(solution)/shard_map/ppermute | solution.py:457
  189.2 101.6 %collective-permute-start.21 = (bf16[280,1536]{1,0:T(8,128)(2,1)}, bf16[280,1536]{1,0:T(8,128)(2,1)}, u32[]{:S(2)}, u32[]{:S(2)}) collective-permute-start(bf16[280,1536]{1,0:T(8,128)(2,1)} %gate_copy.15), channel_id=1, source_target_pairs={{0,2},{2,0},{1,3},{3,1},{4,6},{6,4},{5,7},{7,5},{8,10},{10,8},{9,1... | collective-permute-start | bytes 2580488 | tf_op jit(solution)/shard_map/ppermute | solution.py:457
  204.2 70.7 %collective-permute-start.16 = (bf16[512,1536]{1,0:T(8,128)(2,1)}, bf16[512,1536]{1,0:T(8,128)(2,1)}, u32[]{:S(2)}, u32[]{:S(2)}) collective-permute-start(bf16[512,1536]{1,0:T(8,128)(2,1)} %multiply_convert_fusion.refs_1_.normed.refs_4_), channel_id=1, source_target_pairs={{0,1},{1,0},{2,3},{3,2},{4,5},{5,4},{6,7},{7,6},{8,9},{9,8},{10,11... | collective-permute-start | bytes 4718600 | tf_op jit(solution)/shard_map/ppermute | solution.py:457
  204.2 75.1 %collective-permute-start.25 = (bf16[512,1536]{1,0:T(8,128)(2,1)}, bf16[512,1536]{1,0:T(8,128)(2,1)}, u32[]{:S(2)}, u32[]{:S(2)}) collective-permute-start(bf16[512,1536]{1,0:T(8,128)(2,1)} %multiply_convert_fusion.refs_1_.normed.refs_4_), channel_id=1, source_target_pairs={{0,8},{8,0},{1,9},{9,1},{2,10},{10,2},{3,11},{11,3},{4,12},{12,4},... | collective-permute-start | bytes 4718600 | tf_op jit(solution)/shard_map/ppermute | solution.py:457
  230.0 55.7 %collective-permute-start.19 = (bf16[280,1536]{1,0:T(8,128)(2,1)}, bf16[280,1536]{1,0:T(8,128)(2,1)}, u32[]{:S(2)}, u32[]{:S(2)}) collective-permute-start(bf16[280,1536]{1,0:T(8,128)(2,1)} %gate.50), channel_id=1, source_target_pairs={{0,16},{16,0},{1,17},{17,1},{2,18},{18,2},{3,19},{19,3},{4,20},{20... | collective-permute-start | bytes 2580488 | tf_op jit(solution)/shard_map/ppermute | solution.py:457
  491.8 70.6 %collective-permute-start.33 = (bf16[560,1536]{1,0:T(8,128)(2,1)}, bf16[560,1536]{1,0:T(8,128)(2,1)}, u32[]{:S(2)}, u32[]{:S(2)}) collective-permute-start(bf16[560,1536]{1,0:T(8,128)(2,1)} %get-tuple-element.83.refs_10_), channel_id=1, source_target_pairs={{0,16},{16,0},{1,17},{17,1},{2,18},{18,2},{3,19},{19,3},{4,20},{20... | collective-permute-start | bytes 5160968 | tf_op jit(solution)/shard_map/ppermute | solution.py:457
  542.4 80.8 %all-to-all-start.2 = ((bf16[4,1,2,512,256]{4,3,2,1,0:T(8,128)(2,1)}), bf16[4,1,2,512,256]{4,3,2,1,0:T(8,128)(2,1)}, u32[]{:S(2)}, u32[]{:S(2)}) async-start(bf16[4,1,2,512,256]{4,3,2,1,0:T(8,128)(2,1)} %get-tuple-element.66), calls=%async_computation.2 | async-start | bytes 4194304 | tf_op jit(solution)/shard_map/all_to_all | solution.py:608
  546.9 199.5 %reduce-scatter.2.cloned.1.call-start = ((), (), s32[]{:S(2)}) async-start(), calls=%async_computation.7 | async-start | bytes 4866048 | tf_op jit(solution)/shard_map/reduce_scatter | solution.py:844
  574.4 112.4 %collective-permute-start.42 = (bf16[280,1536]{1,0:T(8,128)(2,1)}, bf16[280,1536]{1,0:T(8,128)(2,1)}, u32[]{:S(2)}, u32[]{:S(2)}) collective-permute-start(bf16[280,1536]{1,0:T(8,128)(2,1)} %slice.229), channel_id=1, source_target_pairs={{0,2},{2,0},{1,3},{3,1},{4,6},{6,4},{5,7},{7,5},{8,10},{10,8},{9,1... | collective-permute-start | bytes 2580488 | tf_op jit(solution)/shard_map/ppermute | solution.py:457
  622.5 59.8 %collective-permute-start.34 = (bf16[512,1536]{1,0:T(8,128)(2,1)}, bf16[512,1536]{1,0:T(8,128)(2,1)}, u32[]{:S(2)}, u32[]{:S(2)}) collective-permute-start(bf16[512,1536]{1,0:T(8,128)(2,1)} %back_rows.14.refs_2_), channel_id=1, source_target_pairs={{0,8},{8,0},{1,9},{9,1},{2,10},{10,2},{3,11},{11,3},{4,12},{12,4},... | collective-permute-start | bytes 4718600 | tf_op jit(solution)/shard_map/ppermute | solution.py:457
  636.8 74.0 %collective-permute-start.40 = (bf16[280,1536]{1,0:T(8,128)(2,1)}, bf16[280,1536]{1,0:T(8,128)(2,1)}, u32[]{:S(2)}, u32[]{:S(2)}) collective-permute-start(bf16[280,1536]{1,0:T(8,128)(2,1)} %slice.227), channel_id=1, source_target_pairs={{0,2},{2,0},{1,3},{3,1},{4,6},{6,4},{5,7},{7,5},{8,10},{10,8},{9,1... | collective-permute-start | bytes 2580488 | tf_op jit(solution)/shard_map/ppermute | solution.py:457
  642.6 62.8 %collective-permute-start.41 = (bf16[560,1536]{1,0:T(8,128)(2,1)}, bf16[560,1536]{1,0:T(8,128)(2,1)}, u32[]{:S(2)}, u32[]{:S(2)}) collective-permute-start(bf16[560,1536]{1,0:T(8,128)(2,1)} %get-tuple-element.79.refs_4_), channel_id=1, source_target_pairs={{0,16},{16,0},{1,17},{17,1},{2,18},{18,2},{3,19},{19,3},{4,20},{20... | collective-permute-start | bytes 5160968 | tf_op jit(solution)/shard_map/ppermute | solution.py:457
  652.6 68.9 %all-to-all-start.3 = ((bf16[4,4,64,1536]{3,2,1,0:T(8,128)(2,1)}), bf16[4,4,64,1536]{3,2,1,0:T(8,128)(2,1)}, u32[]{:S(2)}, u32[]{:S(2)}) async-start(bf16[4,4,64,1536]{3,2,1,0:T(8,128)(2,1)} %bitcast.87), calls=%async_computation.3 | async-start | bytes 6291456 | tf_op jit(solution)/shard_map/all_to_all | solution.py:608
  685.4 56.7 %collective-permute-start.39 = (bf16[512,1536]{1,0:T(8,128)(2,1)}, bf16[512,1536]{1,0:T(8,128)(2,1)}, u32[]{:S(2)}, u32[]{:S(2)}) collective-permute-start(bf16[512,1536]{1,0:T(8,128)(2,1)} %add_convert_fusion.11.refs_1_), channel_id=1, source_target_pairs={{0,1},{1,0},{2,3},{3,2},{4,5},{5,4},{6,7},{7,6},{8,9},{9,8},{10,11... | collective-permute-start | bytes 4718600 | tf_op jit(solution)/shard_map/ppermute | solution.py:457
  708.3 57.8 %collective-permute-start.47 = (bf16[280,1536]{1,0:T(8,128)(2,1)}, bf16[280,1536]{1,0:T(8,128)(2,1)}, u32[]{:S(2)}, u32[]{:S(2)}) collective-permute-start(bf16[280,1536]{1,0:T(8,128)(2,1)} %slice.235), channel_id=1, source_target_pairs={{0,2},{2,0},{1,3},{3,1},{4,6},{6,4},{5,7},{7,5},{8,10},{10,8},{9,1... | collective-permute-start | bytes 2580488 | tf_op jit(solution)/shard_map/ppermute | solution.py:457
  (115 other events, 1456.3 us)
Sparse Core Ops, SparseCore 0:
  79.3 109.8 all-gather.1
  553.6 153.5 reduce-scatter.1

commit v4 on v3

--- a/solution.py
+++ b/solution.py
@@ -731,14 +731,15 @@
     kv_low = kv_low.reshape(1, seq_count, local_len, 2 * kv_width)
     kv_sent = jnp.broadcast_to(kv_low, (ctx_count, *kv_low.shape[1:]))
     kv_all = exchange(kv_sent, CTX_AXES)
-    cot_z, down_z = gate(cot_z, kv_sent), gate(down_z, kv_sent)
+    gate_copied, up_copied = gate_copy(w_gate, kv_sent), gate_copy(w_up, kv_sent)
+    cot_z, down_z = gate(cot_z, kv_sent, gate_copied, up_copied), gate(down_z, kv_sent)
     cot_far = flip(cot_z, "fb")
     down_az = over_a(down_z)
     own_up = gate_copy(w_up, kv_sent)
     up_a = over_a(own_up)
     cot_parts = [cotangent, cot_x, cot_z, cot_far]
 
-    gate_z = flip(gate_copy(w_gate, kv_all), "ch")
+    gate_z = flip(gate(gate_copied, kv_all), "ch")
     queries = queries.reshape(seq_count, local_len, query_width)
     attended, log_totals = attend_forward(
         table, queries, kv_all, wait(kv_low), cot_x, cot_far, down_az, gate_a, up_a
@@ -762,7 +763,7 @@
         return jnp.concatenate([own, other], axis=0)
 
     normed_x, normed_z = flip(normed_two, "fb"), flip(normed_two, "cl")
-    up_z = flip(gate_copy(w_up, attended), "ch")
+    up_z = flip(gate(up_copied, attended), "ch")
     down_own = join_units(own_down, down_z, down_a, gate(down_az, normed_two))
     down_part = join_core(down_own, gate(flip(down_own, "fc"), wait(down_own)))
     d_hidden = [hidden_rows(cot, down_part) for cot in cot_parts]
@@ -770,13 +771,13 @@
     gate_az = over_a(gate_z)
     normed_x, normed_z = gate(normed_x, *d_hidden), gate(normed_z, *d_hidden)
     far_top, far_bottom = flip(normed_z[:half_rows], "fb"), flip(normed_x[half_rows:], "cl")
-    gate_own = join_units(own_gate, gate_z, gate_a, gate(gate_az, *d_hidden))
-    up_z = gate(up_z, gate_own)
+    up_z = gate(up_z, *d_hidden)
     up_az = over_a(up_z)
+    up_own = join_units(own_up, up_z, up_a, gate(up_az, *d_hidden))
+    up_part = join_core(up_own, gate(flip(up_own, "fc"), wait(up_own)))
+    gate_own = join_units(own_gate, gate_z, gate_a, gate(gate_az, up_own))
     gate_part = join_core(gate_own, gate(flip(gate_own, "fc"), wait(gate_own)))
-    normed_far = join_core(gate(far_top, gate_part), far_bottom)
-    up_own = join_units(own_up, up_z, up_a, gate(up_az, gate_part))
-    up_part = join_core(up_own, gate(flip(up_own, "fc"), wait(up_own)))
+    normed_far = join_core(gate(far_top, gate_own), far_bottom)
     normed_parts = [normed_two, normed_x, normed_z, normed_far]
     hidden, d_gate, d_up = zip(
         *(unit_rows(n, d, gate_part, up_part) for n, d in zip(normed_parts, d_hidden))

time: 786 us -> 775 us (0.986)
  starting transfers between devices: 92 us -> 73.5 us
  waiting for transfers between devices: 131 us -> 141 us
    ppermute x42, waiting for transfers between devices: 55.6 us -> 98.4 us  [flip(): return lax.ppermute(values, axis, [(0, 1), (1, 0)])]
    all_to_all x5, waiting for transfers between devices: 60.6 us -> 27.5 us  [exchange(): return lax.all_to_all(values, axes, split_axis=0, concat_axis=0, tiled=True)]
    ppermute x42, starting transfers between devices: 58.3 us -> 39.5 us  [flip(): return lax.ppermute(values, axis, [(0, 1), (1, 0)])]
    pallas_call x8 -> x7, Pallas kernels: 17 us -> 14.7 us  [gate_copy(): pl.pallas_call(with_tokens(copy_kernel, 1, len(first)), grid=(rows // blo...]
    unnamed x178 -> x179, local copies, waits for them, and re-layouts: 58.7 us -> 57.9 us
  transfers between devices with their start and end apart: 55 -> 55, of which waited for: 16 -> 16; matrix products, arithmetic and copies ran while one was open for 22% -> 23% of each run, Pallas kernels for 32% -> 32%
where the time goes in v4:
time: 775 us; the launch traced here: 766 us
  Pallas kernels  312 us (40%)
  waiting for transfers between devices  141 us (18%)
  other arithmetic  109 us (14%)
  local copies, waits for them, and re-layouts  92.4 us (12%)
  starting transfers between devices  73.5 us (9%)
  matrix products  20.7 us (3%)
  between operations  16.8 us (2%)
    ppermute x42, waiting for transfers between devices, flip(): return lax.ppermute(values, axis, [(0, 1), (1, 0)])  98.4 us
    pallas_call x9, Pallas kernels, back_rows(): pl.pallas_call(with_tokens(functools.partial(back_kernel, count), 2 * cou...  88.3 us
    pallas_call x3, Pallas kernels, unit_grads(): pl.pallas_call(with_tokens(functools.partial(grad_kernel, count), 2 * cou...  64.4 us
    unnamed x179, local copies, waits for them, and re-layouts  57.9 us
    pallas_call x4, Pallas kernels, unit_rows(): pl.pallas_call(unit_kernel, grid=(4,), in_specs=[pl.BlockSpec((rows, widt...  56.6 us
    ppermute x42, starting transfers between devices, flip(): return lax.ppermute(values, axis, [(0, 1), (1, 0)])  39.5 us
    convert_element_type x8, other arithmetic, add_low(): functools.reduce(jnp.add, (t.astype(jnp.float32) for t in terms))  27.9 us
    pallas_call x1, Pallas kernels, attend_backward(): pl.pallas_call(with_tokens(backward_kernel, 9, len(first)), grid=(seqs, K...  27.8 us
  transfers between devices with their start and end apart: 55, of which 16 were waited for; matrix products, arithmetic and copies ran while one was open for 23% of the time, Pallas kernels for 32%

profile of v4, /device:TPU:0, one launch (start us, length us, event | category | flops | bytes accessed | tf_op | source)
XLA Modules:
  0.0 765.5 jit_solution(8750787643751850515)
XLA Ops:
  115.5 31.0 %collective-permute-done.13.refs_7_.refs_0_ = bf16[280,1536]{1,0:T(8,128)(2,1)} collective-permute-done((bf16[280,1536]{1,0:T(8,128)(2,1)}, bf16[280,1536]{1,0:T(8,128)(2,1)}, u32[]{:S(2)}, u32[]{:S(2)}) %collective-permute-start.13) | collective-permute-done | bytes 860192 | tf_op jit(solution)/shard_map/ppermute | solution.py:457
  149.4 19.5 %all-to-all-done.1.refs_2_.refs_3_.refs_1_ = bf16[4,1,512,512]{3,2,1,0:T(8,128)(2,1)} async-done(((bf16[4,1,512,512]{3,2,1,0:T(8,128)(2,1)}), bf16[4,1,512,512]{3,2,1,0:T(8,128)(2,1)}, u32[]{:S(2)}, u32[]{:S(2)}) %all-to-all-start.1) | async-done | bytes 2097184 | tf_op jit(solution)/shard_map/all_to_all | solution.py:608
  170.4 17.3 %attend_forward.1 = (bf16[1,512,1536]{2,1,0:T(8,128)(2,1)S(1)}, f32[1,2,2,6,256]{4,3,2,1,0:T(8,128)S(1)}) custom-call(s32[1,10]{1,0:T(1,128)S(1)} %pad_add_fusion.refs_0_, bf16[1,512,1536]{2,1,0:T(8,128)(2,1)S(1)} %bitcast.86, bf16[4,1,512,512]{3,2,1,0:T(8,128)(2,1)} %all-to-all-done.1.refs_2_.refs_3_.refs_1_, ...), custom_call_target="tpu_custom_call" | custom-call | flops 57982058496 | bytes 100663296 | tf_op jit(solution)/shard_map/attend_forward/pallas_call | solution.py:98
  246.0 13.7 %collective-permute-done.18.refs_0_ = bf16[280,1536]{1,0:T(8,128)(2,1)} collective-permute-done((bf16[280,1536]{1,0:T(8,128)(2,1)}, bf16[280,1536]{1,0:T(8,128)(2,1)}, u32[]{:S(2)}, u32[]{:S(2)}) %collective-permute-start.18) | collective-permute-done | bytes 860192 | tf_op jit(solution)/shard_map/ppermute | solution.py:457
  259.7 17.7 %collective-permute-done.16.refs_0_ = bf16[512,1536]{1,0:T(8,128)(2,1)} collective-permute-done((bf16[512,1536]{1,0:T(8,128)(2,1)}, bf16[512,1536]{1,0:T(8,128)(2,1)}, u32[]{:S(2)}, u32[]{:S(2)}) %collective-permute-start.16) | collective-permute-done | bytes 1572896 | tf_op jit(solution)/shard_map/ppermute | solution.py:457
  314.8 14.1 %unit_rows.7 = (bf16[2240,512]{1,0:T(8,128)(2,1)}, bf16[2240,512]{1,0:T(8,128)(2,1)}, bf16[2240,512]{1,0:T(8,128)(2,1)}) custom-call(bf16[512,1536]{1,0:T(8,128)(2,1)} %gate.61.normed.refs_5_, bf16[2240,512]{1,0:T(8,128)(2,1)} %copy-done.3, bf16[2240,1536]{1,0:T(8,128)(2,1)} %constant_dynamic-update-slice_fusion.5.gate.refs_2_, ...), custom_call_target="tpu_custom_call" | custom-call | flops 112742891520 | bytes 367001600 | tf_op jit(solution)/shard_map/unit_rows/pallas_call | solution.py:419
  328.9 14.3 %unit_rows.4 = (bf16[2240,512]{1,0:T(8,128)(2,1)}, bf16[2240,512]{1,0:T(8,128)(2,1)}, bf16[2240,512]{1,0:T(8,128)(2,1)}) custom-call(bf16[512,1536]{1,0:T(8,128)(2,1)} %gate.51.normed.refs_6_, bf16[2240,512]{1,0:T(8,128)(2,1)} %copy-done.2, bf16[2240,1536]{1,0:T(8,128)(2,1)} %constant_dynamic-update-slice_fusion.5.gate.refs_2_, ...), custom_call_target="tpu_custom_call" | custom-call | flops 112742891520 | bytes 367001600 | tf_op jit(solution)/shard_map/unit_rows/pallas_call | solution.py:419
  343.2 14.1 %unit_rows.6 = (bf16[2240,512]{1,0:T(8,128)(2,1)}, bf16[2240,512]{1,0:T(8,128)(2,1)}, bf16[2240,512]{1,0:T(8,128)(2,1)}) custom-call(bf16[512,1536]{1,0:T(8,128)(2,1)} %multiply_convert_fusion.refs_1_.normed.refs_4_, bf16[2240,512]{1,0:T(8,128)(2,1)} %copy-done, bf16[2240,1536]{1,0:T(8,128)(2,1)} %constant_dynamic-update-slice_fusion.5.gate.refs_2_, ...), custom_call_target="tpu_custom_call" | custom-call | flops 112742891520 | bytes 367001600 | tf_op jit(solution)/shard_map/unit_rows/pallas_call | solution.py:419
  357.3 14.1 %unit_rows.5 = (bf16[2240,512]{1,0:T(8,128)(2,1)}, bf16[2240,512]{1,0:T(8,128)(2,1)}, bf16[2240,512]{1,0:T(8,128)(2,1)}) custom-call(bf16[512,1536]{1,0:T(8,128)(2,1)} %pad_maximum_fusion.8.normed.refs_7_, bf16[2240,512]{1,0:T(8,128)(2,1)} %copy-done.1, bf16[2240,1536]{1,0:T(8,128)(2,1)} %constant_dynamic-update-slice_fusion.5.gate.refs_2_, ...), custom_call_target="tpu_custom_call" | custom-call | flops 112742891520 | bytes 367001600 | tf_op jit(solution)/shard_map/unit_rows/pallas_call | solution.py:419
  371.4 12.5 %back_rows.9.refs_4_ = bf16[512,1536]{1,0:T(8,128)(2,1)} custom-call(bf16[2240,512]{1,0:T(8,128)(2,1)} %get-tuple-element.54.refs_0_.refs_3_, bf16[2240,512]{1,0:T(8,128)(2,1)} %get-tuple-element.50.refs_1_.refs_3_, bf16[2240,1536]{1,0:T(8,128)(2,1)} %constant_dynamic-update-slice_fusion.5.gate.refs_2_, ...), custom_call_target="tpu_custom_call" | custom-call | flops 112742891520 | bytes 293601280 | tf_op jit(solution)/shard_map/back_rows/pallas_call | solution.py:293
  388.9 12.5 %back_rows.10.refs_4_ = bf16[512,1536]{1,0:T(8,128)(2,1)} custom-call(bf16[2240,512]{1,0:T(8,128)(2,1)} %get-tuple-element.52.refs_0_.refs_1_, bf16[2240,512]{1,0:T(8,128)(2,1)} %get-tuple-element.48.refs_1_, bf16[2240,1536]{1,0:T(8,128)(2,1)} %constant_dynamic-update-slice_fusion.5.gate.refs_2_, ...), custom_call_target="tpu_custom_call" | custom-call | flops 112742891520 | bytes 293601280 | tf_op jit(solution)/shard_map/back_rows/pallas_call | solution.py:293
  401.4 12.5 %back_rows.11.refs_1_ = bf16[512,1536]{1,0:T(8,128)(2,1)} custom-call(bf16[2240,512]{1,0:T(8,128)(2,1)} %get-tuple-element.53.refs_0_.refs_2_, bf16[2240,512]{1,0:T(8,128)(2,1)} %get-tuple-element.49.refs_1_.refs_2_, bf16[2240,1536]{1,0:T(8,128)(2,1)} %constant_dynamic-update-slice_fusion.5.gate.refs_2_, ...), custom_call_target="tpu_custom_call" | custom-call | flops 112742891520 | bytes 293601280 | tf_op jit(solution)/shard_map/back_rows/pallas_call | solution.py:293
  422.4 21.6 %unit_grads.3 = (bf16[1120,1536]{1,0:T(8,128)(2,1)}, bf16[1120,1536]{1,0:T(8,128)(2,1)}) custom-call(bf16[2240,512]{1,0:T(8,128)(2,1)} %get-tuple-element.55.refs_0_, bf16[2240,512]{1,0:T(8,128)(2,1)} %get-tuple-element.56.refs_1_.refs_0_, bf16[2240,512]{1,0:T(8,128)(2,1)} %get-tuple-element.45.refs_2_.refs_0_, ...), custom_call_target="tpu_custom_call" | custom-call | flops 225485783040 | bytes 247463936 | tf_op jit(solution)/shard_map/unit_grads/pallas_call | solution.py:258
  444.1 12.7 %back_rows.12.refs_1_ = bf16[512,1536]{1,0:T(8,128)(2,1)} custom-call(bf16[2240,512]{1,0:T(8,128)(2,1)} %get-tuple-element.51.refs_0_, bf16[2240,512]{1,0:T(8,128)(2,1)} %get-tuple-element.47.refs_1_.refs_0_, bf16[2240,1536]{1,0:T(8,128)(2,1)} %constant_dynamic-update-slice_fusion.5.gate.refs_2_, ...), custom_call_target="tpu_custom_call" | custom-call | flops 112742891520 | bytes 293601280 | tf_op jit(solution)/shard_map/back_rows/pallas_call | solution.py:293
  480.0 27.8 %attend_backward.1 = (bf16[1,512,1536]{2,1,0:T(8,128)(2,1)S(1)}, bf16[4,1,2,512,256]{4,3,2,1,0:T(8,128)(2,1)}) custom-call(s32[1,10]{1,0:T(1,128)S(1)} %copy-done.33, bf16[1,512,1536]{2,1,0:T(8,128)(2,1)S(1)} %bitcast.87, bf16[4,1,512,512]{3,2,1,0:T(8,128)(2,1)} %all-to-all-done.1.refs_2_.refs_3_.refs_1_, ...), custom_call_target="tpu_custom_call" | custom-call | flops 144955146240 | bytes 201326592 | tf_op jit(solution)/shard_map/attend_backward/pallas_call | solution.py:197
  509.0 21.3 %unit_grads.4 = (bf16[1120,1536]{1,0:T(8,128)(2,1)}, bf16[1120,1536]{1,0:T(8,128)(2,1)}) custom-call(bf16[2240,512]{1,0:T(8,128)(2,1)} %get-tuple-element.51.refs_0_, bf16[2240,512]{1,0:T(8,128)(2,1)} %get-tuple-element.52.refs_0_.refs_1_, bf16[2240,512]{1,0:T(8,128)(2,1)} %get-tuple-element.53.refs_0_.refs_2_, ...), custom_call_target="tpu_custom_call" | custom-call | flops 225485783040 | bytes 247463936 | tf_op jit(solution)/shard_map/unit_grads/pallas_call | solution.py:258
  573.2 21.5 %unit_grads.5 = (bf16[1120,1536]{1,0:T(8,128)(2,1)}, bf16[1120,1536]{1,0:T(8,128)(2,1)}) custom-call(bf16[2240,512]{1,0:T(8,128)(2,1)} %get-tuple-element.47.refs_1_.refs_0_, bf16[2240,512]{1,0:T(8,128)(2,1)} %get-tuple-element.48.refs_1_, bf16[2240,512]{1,0:T(8,128)(2,1)} %get-tuple-element.49.refs_1_.refs_2_, ...), custom_call_target="tpu_custom_call" | custom-call | flops 225485783040 | bytes 247463936 | tf_op jit(solution)/shard_map/unit_grads/pallas_call | solution.py:258
  594.7 7.8 %back_rows.14.refs_2_ = bf16[512,1536]{1,0:T(8,128)(2,1)} custom-call(bf16[2240,512]{1,0:T(8,128)(2,1)} %get-tuple-element.46.refs_3_.refs_0_, bf16[2240,1536]{1,0:T(8,128)(2,1)} %constant_dynamic-update-slice_fusion.weight.refs_1_, bf16[1120,1536]{1,0:T(8,128)(2,1)} %get-tuple-element.65.refs_2_), custom_call_target="tpu_custom_call" | custom-call | flops 56371445760 | bytes 146800640 | tf_op jit(solution)/shard_map/back_rows/pallas_call | solution.py:293
  602.5 8.2 %back_rows.15.refs_1_ = bf16[512,1536]{1,0:T(8,128)(2,1)} custom-call(bf16[2240,512]{1,0:T(8,128)(2,1)} %get-tuple-element.45.refs_2_.refs_0_, bf16[2240,1536]{1,0:T(8,128)(2,1)} %constant_dynamic-update-slice_fusion.weight.refs_1_, bf16[512,1536]{1,0:T(8,128)(2,1)} %back_rows.14.refs_2_), custom_call_target="tpu_custom_call" | custom-call | flops 56371445760 | bytes 146800640 | tf_op jit(solution)/shard_map/back_rows/pallas_call | solution.py:293
  652.2 7.9 %back_rows.16.refs_2_ = bf16[512,1536]{1,0:T(8,128)(2,1)} custom-call(bf16[2240,512]{1,0:T(8,128)(2,1)} %get-tuple-element.56.refs_1_.refs_0_, bf16[2240,1536]{1,0:T(8,128)(2,1)} %constant_dynamic-update-slice_fusion.weight.refs_1_, f32[512,1536]{1,0:T(8,128)} %fusion.7.refs_2_), custom_call_target="tpu_custom_call" | custom-call | flops 56371445760 | bytes 146800640 | tf_op jit(solution)/shard_map/back_rows/pallas_call | solution.py:293
  660.1 7.9 %back_rows.17.refs_1_ = bf16[512,1536]{1,0:T(8,128)(2,1)} custom-call(bf16[2240,512]{1,0:T(8,128)(2,1)} %get-tuple-element.55.refs_0_, bf16[2240,1536]{1,0:T(8,128)(2,1)} %constant_dynamic-update-slice_fusion.weight.refs_1_, bf16[512,1536]{1,0:T(8,128)(2,1)} %back_rows.16.refs_2_), custom_call_target="tpu_custom_call" | custom-call | flops 56371445760 | bytes 146800640 | tf_op jit(solution)/shard_map/back_rows/pallas_call | solution.py:293
  678.0 15.7 %collective-permute-done.41.refs_0_ = bf16[560,1536]{1,0:T(8,128)(2,1)} collective-permute-done((bf16[560,1536]{1,0:T(8,128)(2,1)}, bf16[560,1536]{1,0:T(8,128)(2,1)}, u32[]{:S(2)}, u32[]{:S(2)}) %collective-permute-start.41) | collective-permute-done | bytes 1720352 | tf_op jit(solution)/shard_map/ppermute | solution.py:457
  701.7 8.0 %all-to-all-done.3.refs_0_ = bf16[4,4,64,1536]{3,2,1,0:T(8,128)(2,1)} async-done(((bf16[4,4,64,1536]{3,2,1,0:T(8,128)(2,1)}), bf16[4,4,64,1536]{3,2,1,0:T(8,128)(2,1)}, u32[]{:S(2)}, u32[]{:S(2)}) %all-to-all-start.3) | async-done | bytes 3145760 | tf_op jit(solution)/shard_map/all_to_all | solution.py:608
  740.9 11.5 %collective-permute-done.45 = bf16[64,1536]{1,0:T(8,128)(2,1)} collective-permute-done((bf16[64,1536]{1,0:T(8,128)(2,1)S(1)}, bf16[64,1536]{1,0:T(8,128)(2,1)}, u32[]{:S(2)}, u32[]{:S(2)}) %collective-permute-start.45) | collective-permute-done | bytes 196640 | tf_op jit(solution)/shard_map/ppermute | solution.py:572
  (450 shorter events, 383.7 us)
Async XLA Ops:
  20.2 171.7 %all-gather.2.cloned.1.call-start = ((), (), s32[]{:S(2)}) async-start(), calls=%async_computation.6 | async-start | bytes 4866048 | tf_op jit(solution)/shard_map/all_gather | solution.py:717
  43.5 61.6 %collective-permute-start.10 = (bf16[512,1536]{1,0:T(8,128)(2,1)}, bf16[512,1536]{1,0:T(8,128)(2,1)}, u32[]{:S(2)}, u32[]{:S(2)}) collective-permute-start(bf16[512,1536]{1,0:T(8,128)(2,1)} %gate_copy.8), channel_id=1, source_target_pairs={{0,1},{1,0},{2,3},{3,2},{4,5},{5,4},{6,7},{7,6},{8,9},{9,8},{10,11... | collective-permute-start | bytes 4718600 | tf_op jit(solution)/shard_map/ppermute | solution.py:457
  43.5 63.1 %collective-permute-start.12 = (bf16[280,1536]{1,0:T(8,128)(2,1)}, bf16[280,1536]{1,0:T(8,128)(2,1)}, u32[]{:S(2)}, u32[]{:S(2)}) collective-permute-start(bf16[280,1536]{1,0:T(8,128)(2,1)} %gate_copy.11), channel_id=1, source_target_pairs={{0,2},{2,0},{1,3},{3,1},{4,6},{6,4},{5,7},{7,5},{8,10},{10,8},{9,1... | collective-permute-start | bytes 2580488 | tf_op jit(solution)/shard_map/ppermute | solution.py:457
  73.4 42.1 %collective-permute-start.9 = (bf16[512,1536]{1,0:T(8,128)(2,1)}, bf16[512,1536]{1,0:T(8,128)(2,1)}, u32[]{:S(2)}, u32[]{:S(2)}) collective-permute-start(bf16[512,1536]{1,0:T(8,128)(2,1)} %gate_copy.7), channel_id=1, source_target_pairs={{0,8},{8,0},{1,9},{9,1},{2,10},{10,2},{3,11},{11,3},{4,12},{12,4},... | collective-permute-start | bytes 4718600 | tf_op jit(solution)/shard_map/ppermute | solution.py:457
  97.9 71.1 %all-to-all-start.1 = ((bf16[4,1,512,512]{3,2,1,0:T(8,128)(2,1)}), bf16[4,1,512,512]{3,2,1,0:T(8,128)(2,1)}, u32[]{:S(2)}, u32[]{:S(2)}) async-start(bf16[4,1,512,512]{3,2,1,0:T(8,128)(2,1)} %broadcast_in_dim.17.refs_1_), calls=%async_computation.1 | async-start | bytes 4194304 | tf_op jit(solution)/shard_map/all_to_all | solution.py:608
  105.1 44.3 %collective-permute-start.11 = (bf16[512,1536]{1,0:T(8,128)(2,1)}, bf16[512,1536]{1,0:T(8,128)(2,1)}, u32[]{:S(2)}, u32[]{:S(2)}) collective-permute-start(bf16[512,1536]{1,0:T(8,128)(2,1)} %gate.47.rows.refs_6_), channel_id=1, source_target_pairs={{0,8},{8,0},{1,9},{9,1},{2,10},{10,2},{3,11},{11,3},{4,12},{12,4},... | collective-permute-start | bytes 4718600 | tf_op jit(solution)/shard_map/ppermute | solution.py:457
  188.9 54.9 %collective-permute-start.20 = (bf16[280,1536]{1,0:T(8,128)(2,1)}, bf16[280,1536]{1,0:T(8,128)(2,1)}, u32[]{:S(2)}, u32[]{:S(2)}) collective-permute-start(bf16[280,1536]{1,0:T(8,128)(2,1)} %gate.54), channel_id=1, source_target_pairs={{0,2},{2,0},{1,3},{3,1},{4,6},{6,4},{5,7},{7,5},{8,10},{10,8},{9,1... | collective-permute-start | bytes 2580488 | tf_op jit(solution)/shard_map/ppermute | solution.py:457
  188.9 70.8 %collective-permute-start.18 = (bf16[280,1536]{1,0:T(8,128)(2,1)}, bf16[280,1536]{1,0:T(8,128)(2,1)}, u32[]{:S(2)}, u32[]{:S(2)}) collective-permute-start(bf16[280,1536]{1,0:T(8,128)(2,1)} %gate.52), channel_id=1, source_target_pairs={{0,2},{2,0},{1,3},{3,1},{4,6},{6,4},{5,7},{7,5},{8,10},{10,8},{9,1... | collective-permute-start | bytes 2580488 | tf_op jit(solution)/shard_map/ppermute | solution.py:457
  203.5 73.9 %collective-permute-start.16 = (bf16[512,1536]{1,0:T(8,128)(2,1)}, bf16[512,1536]{1,0:T(8,128)(2,1)}, u32[]{:S(2)}, u32[]{:S(2)}) collective-permute-start(bf16[512,1536]{1,0:T(8,128)(2,1)} %multiply_convert_fusion.refs_1_.normed.refs_4_), channel_id=1, source_target_pairs={{0,1},{1,0},{2,3},{3,2},{4,5},{5,4},{6,7},{7,6},{8,9},{9,8},{10,11... | collective-permute-start | bytes 4718600 | tf_op jit(solution)/shard_map/ppermute | solution.py:457
  203.5 77.6 %collective-permute-start.25 = (bf16[512,1536]{1,0:T(8,128)(2,1)}, bf16[512,1536]{1,0:T(8,128)(2,1)}, u32[]{:S(2)}, u32[]{:S(2)}) collective-permute-start(bf16[512,1536]{1,0:T(8,128)(2,1)} %multiply_convert_fusion.refs_1_.normed.refs_4_), channel_id=1, source_target_pairs={{0,8},{8,0},{1,9},{9,1},{2,10},{10,2},{3,11},{11,3},{4,12},{12,4},... | collective-permute-start | bytes 4718600 | tf_op jit(solution)/shard_map/ppermute | solution.py:457
  243.8 45.8 %collective-permute-start.21 = (bf16[280,1536]{1,0:T(8,128)(2,1)}, bf16[280,1536]{1,0:T(8,128)(2,1)}, u32[]{:S(2)}, u32[]{:S(2)}) collective-permute-start(bf16[280,1536]{1,0:T(8,128)(2,1)} %gate.55), channel_id=1, source_target_pairs={{0,16},{16,0},{1,17},{17,1},{2,18},{18,2},{3,19},{19,3},{4,20},{20... | collective-permute-start | bytes 2580488 | tf_op jit(solution)/shard_map/ppermute | solution.py:457
  480.0 70.2 %collective-permute-start.33 = (bf16[560,1536]{1,0:T(8,128)(2,1)}, bf16[560,1536]{1,0:T(8,128)(2,1)}, u32[]{:S(2)}, u32[]{:S(2)}) collective-permute-start(bf16[560,1536]{1,0:T(8,128)(2,1)} %get-tuple-element.83.refs_10_), channel_id=1, source_target_pairs={{0,16},{16,0},{1,17},{17,1},{2,18},{18,2},{3,19},{19,3},{4,20},{20... | collective-permute-start | bytes 5160968 | tf_op jit(solution)/shard_map/ppermute | solution.py:457
  530.3 81.2 %all-to-all-start.2 = ((bf16[4,1,2,512,256]{4,3,2,1,0:T(8,128)(2,1)}), bf16[4,1,2,512,256]{4,3,2,1,0:T(8,128)(2,1)}, u32[]{:S(2)}, u32[]{:S(2)}) async-start(bf16[4,1,2,512,256]{4,3,2,1,0:T(8,128)(2,1)} %get-tuple-element.66), calls=%async_computation.2 | async-start | bytes 4194304 | tf_op jit(solution)/shard_map/all_to_all | solution.py:608
  534.8 198.9 %reduce-scatter.2.cloned.1.call-start = ((), (), s32[]{:S(2)}) async-start(), calls=%async_computation.7 | async-start | bytes 4866048 | tf_op jit(solution)/shard_map/reduce_scatter | solution.py:845
  561.8 54.8 %collective-permute-start.35 = (bf16[768,1536]{1,0:T(8,128)(2,1)}, bf16[768,1536]{1,0:T(8,128)(2,1)}, u32[]{:S(2)}, u32[]{:S(2)}) collective-permute-start(bf16[768,1536]{1,0:T(8,128)(2,1)} %get-tuple-element.67), channel_id=1, source_target_pairs={{0,4},{4,0},{1,5},{5,1},{2,6},{6,2},{3,7},{7,3},{8,12},{12,8},{9,1... | collective-permute-start | bytes 7077896 | tf_op jit(solution)/shard_map/ppermute | solution.py:457
  562.3 112.2 %collective-permute-start.42 = (bf16[280,1536]{1,0:T(8,128)(2,1)}, bf16[280,1536]{1,0:T(8,128)(2,1)}, u32[]{:S(2)}, u32[]{:S(2)}) collective-permute-start(bf16[280,1536]{1,0:T(8,128)(2,1)} %slice.229), channel_id=1, source_target_pairs={{0,2},{2,0},{1,3},{3,1},{4,6},{6,4},{5,7},{7,5},{8,10},{10,8},{9,1... | collective-permute-start | bytes 2580488 | tf_op jit(solution)/shard_map/ppermute | solution.py:457
  571.5 49.1 %collective-permute-start.37 = (bf16[560,1536]{1,0:T(8,128)(2,1)}, bf16[560,1536]{1,0:T(8,128)(2,1)}, u32[]{:S(2)}, u32[]{:S(2)}) collective-permute-start(bf16[560,1536]{1,0:T(8,128)(2,1)} %get-tuple-element.81.refs_9_), channel_id=1, source_target_pairs={{0,16},{16,0},{1,17},{17,1},{2,18},{18,2},{3,19},{19,3},{4,20},{20... | collective-permute-start | bytes 5160968 | tf_op jit(solution)/shard_map/ppermute | solution.py:457
  610.7 59.3 %collective-permute-start.34 = (bf16[512,1536]{1,0:T(8,128)(2,1)}, bf16[512,1536]{1,0:T(8,128)(2,1)}, u32[]{:S(2)}, u32[]{:S(2)}) collective-permute-start(bf16[512,1536]{1,0:T(8,128)(2,1)} %back_rows.14.refs_2_), channel_id=1, source_target_pairs={{0,8},{8,0},{1,9},{9,1},{2,10},{10,2},{3,11},{11,3},{4,12},{12,4},... | collective-permute-start | bytes 4718600 | tf_op jit(solution)/shard_map/ppermute | solution.py:457
  625.1 74.0 %collective-permute-start.40 = (bf16[280,1536]{1,0:T(8,128)(2,1)}, bf16[280,1536]{1,0:T(8,128)(2,1)}, u32[]{:S(2)}, u32[]{:S(2)}) collective-permute-start(bf16[280,1536]{1,0:T(8,128)(2,1)} %slice.227), channel_id=1, source_target_pairs={{0,2},{2,0},{1,3},{3,1},{4,6},{6,4},{5,7},{7,5},{8,10},{10,8},{9,1... | collective-permute-start | bytes 2580488 | tf_op jit(solution)/shard_map/ppermute | solution.py:457
  630.8 62.8 %collective-permute-start.41 = (bf16[560,1536]{1,0:T(8,128)(2,1)}, bf16[560,1536]{1,0:T(8,128)(2,1)}, u32[]{:S(2)}, u32[]{:S(2)}) collective-permute-start(bf16[560,1536]{1,0:T(8,128)(2,1)} %get-tuple-element.79.refs_4_), channel_id=1, source_target_pairs={{0,16},{16,0},{1,17},{17,1},{2,18},{18,2},{3,19},{19,3},{4,20},{20... | collective-permute-start | bytes 5160968 | tf_op jit(solution)/shard_map/ppermute | solution.py:457
  640.3 69.4 %all-to-all-start.3 = ((bf16[4,4,64,1536]{3,2,1,0:T(8,128)(2,1)}), bf16[4,4,64,1536]{3,2,1,0:T(8,128)(2,1)}, u32[]{:S(2)}, u32[]{:S(2)}) async-start(bf16[4,4,64,1536]{3,2,1,0:T(8,128)(2,1)} %bitcast.89), calls=%async_computation.3 | async-start | bytes 6291456 | tf_op jit(solution)/shard_map/all_to_all | solution.py:608
  668.0 50.5 %collective-permute-start.43 = (bf16[512,1536]{1,0:T(8,128)(2,1)}, bf16[512,1536]{1,0:T(8,128)(2,1)}, u32[]{:S(2)}, u32[]{:S(2)}) collective-permute-start(bf16[512,1536]{1,0:T(8,128)(2,1)} %back_rows.16.refs_2_), channel_id=1, source_target_pairs={{0,8},{8,0},{1,9},{9,1},{2,10},{10,2},{3,11},{11,3},{4,12},{12,4},... | collective-permute-start | bytes 4718600 | tf_op jit(solution)/shard_map/ppermute | solution.py:457
  673.1 56.3 %collective-permute-start.39 = (bf16[512,1536]{1,0:T(8,128)(2,1)}, bf16[512,1536]{1,0:T(8,128)(2,1)}, u32[]{:S(2)}, u32[]{:S(2)}) collective-permute-start(bf16[512,1536]{1,0:T(8,128)(2,1)} %add_convert_fusion.11.refs_1_), channel_id=1, source_target_pairs={{0,1},{1,0},{2,3},{3,2},{4,5},{5,4},{6,7},{7,6},{8,9},{9,8},{10,11... | collective-permute-start | bytes 4718600 | tf_op jit(solution)/shard_map/ppermute | solution.py:457
  696.6 57.8 %collective-permute-start.47 = (bf16[280,1536]{1,0:T(8,128)(2,1)}, bf16[280,1536]{1,0:T(8,128)(2,1)}, u32[]{:S(2)}, u32[]{:S(2)}) collective-permute-start(bf16[280,1536]{1,0:T(8,128)(2,1)} %slice.235), channel_id=1, source_target_pairs={{0,2},{2,0},{1,3},{3,1},{4,6},{6,4},{5,7},{7,5},{8,10},{10,8},{9,1... | collective-permute-start | bytes 2580488 | tf_op jit(solution)/shard_map/ppermute | solution.py:457
  (115 other events, 1418.3 us)
Sparse Core Ops, SparseCore 0:
  79.3 92.9 all-gather.1
  541.5 153.9 reduce-scatter.1
